TPU v7x, 32 devices: a whole 2x2x4 slice. The times are simulated.
32 devices in a mesh: dp: 8 (over z, y), mp: 4 (over x, core).
Axes of the slice: x: 2, y: 2, z: 4, core: 2. Of those that a mesh axis runs over, the one named last changes fastest.
Arguments:
- tokens: bfloat16 [8192, 1536], P(('dp', 'mp')), may hold values from -6 to 6
- gain_attn: float32 [1536], replicated, may hold values from 0.5 to 1.5
- w_query: bfloat16 [1536, 768], P(None, 'mp'), may hold values from -0.01953125 to 0.01953125
- w_key: bfloat16 [1536, 768], P(None, 'mp'), may hold values from -0.15625 to 0.15625
- w_value: bfloat16 [1536, 768], P(None, 'mp'), may hold values from -0.15625 to 0.15625
- w_out: bfloat16 [768, 1536], P('mp'), may hold values from -6 to 6
- bias_table: float32 [32, 12], P(None, 'mp'), may hold values from -4 to 4
- gain_ff: float32 [1536], replicated, may hold values from 0.5 to 1.5
- w_gate: bfloat16 [1536, 3968], P(None, 'mp'), may hold values from -0.15625 to 0.15625
- w_up: bfloat16 [1536, 3968], P(None, 'mp'), may hold values from -0.15625 to 0.15625
- w_down: bfloat16 [3968, 1536], P('mp'), may hold values from -0.09375 to 0.09375
- cotangent: bfloat16 [8192, 1536], P(('dp', 'mp')), may hold values from -6 to 6
- first_length: int32 [8], P('dp'), may hold values from 512 to 1024, as said below
- offset_bucket: int32 [2047], replicated, may hold values from 0 to 31
Outputs:
- output: bfloat16 [8192, 1536], P(('dp', 'mp'))
- grad_input: float32 [8192, 1536], P(('dp', 'mp'))
- grad_gain_attn: float32 [1536], replicated
- grad_query: float32 [1536, 768], P('dp', 'mp')
- grad_key: float32 [1536, 768], P('dp', 'mp')
- grad_value: float32 [1536, 768], P('dp', 'mp')
- grad_out: float32 [768, 1536], P('mp', 'dp')
- grad_table: float32 [32, 12], P(None, 'mp')
- grad_gain_ff: float32 [1536], replicated
- grad_gate: float32 [1536, 3968], P('dp', 'mp')
- grad_up: float32 [1536, 3968], P('dp', 'mp')
- grad_down: float32 [3968, 1536], P('mp', 'dp')
Inputs may be any that keep to these rules, and one draw needn't show every extreme that they name: `first_length`: each group of 1024 tokens holds one row of 1024 tokens (this value 1024) or two rows of 1024 // 2 (this value 1024 // 2); both kinds occur in every draw.
All inputs are finite; a program needn't handle non-finite values.
Results may differ from a plain program's by a relative error of at most 0.013.
Values may be sent and summed in bfloat16 or wider, within the bound.
A program may use at most 192 MiB of HBM per device.

v0:
```python
import jax
import jax.numpy as jnp
from jax import lax
from jax.sharding import PartitionSpec as P

DH = 64


epsilon = 1e-06
masked_score = -1000000000.0
highest = lax.Precision.HIGHEST


def normalize(values, gain):
    return values * lax.rsqrt(jnp.mean(values * values, axis=-1, keepdims=True) + epsilon) * gain


def gated(gate_val, up_val):
    return jax.nn.gelu(gate_val, approximate=True) * up_val


def contract_rows(left, right):
    return lax.dot_general(
        left, right, (((0,), (0,)), ((), ())), preferred_element_type=jnp.float32
    )


def contract_cols(left, right):
    return lax.dot_general(
        left, right, (((1,), (1,)), ((), ())), preferred_element_type=jnp.float32
    )


def skew_bias(bias_rows, start, block, length):
    heads = bias_rows.shape[0]
    span = length + block - 1
    window = lax.dynamic_slice_in_dim(bias_rows, length - block - start, span, 1)
    tiled = jnp.broadcast_to(window[:, None, :], (heads, block, span)).reshape(heads, block * span)
    tiled = jnp.pad(tiled, ((0, 0), (0, block))).reshape(heads, block, length + block)
    return tiled[:, ::-1, :length]


def unskew_sum(grads, block, length):
    heads = grads.shape[0]
    span = length + block - 1
    flipped = grads[:, ::-1, :]
    padded = jnp.pad(flipped, ((0, 0), (0, 0), (0, block))).reshape(heads, block * (length + block))
    return padded[:, : block * span].reshape(heads, block, span).sum(axis=1)


def shards(
    tokens,
    gain_attn,
    w_query,
    w_key,
    w_value,
    w_out,
    bias_table,
    gain_ff,
    w_gate,
    w_up,
    w_down,
    cotangent,
    first_length,
    offset_bucket,
):
    inputs = tokens.astype(jnp.float32)
    normed_part = normalize(inputs, gain_attn).astype(jnp.bfloat16)
    normed = lax.all_gather(normed_part, "mp", axis=0, tiled=True)
    length = normed.shape[0]
    heads = w_query.shape[1] // DH
    query_all = jnp.dot(normed, w_query, preferred_element_type=jnp.float32).astype(jnp.bfloat16)
    key_all = jnp.dot(normed, w_key, preferred_element_type=jnp.float32).astype(jnp.bfloat16)
    value_all = jnp.dot(normed, w_value, preferred_element_type=jnp.float32).astype(jnp.bfloat16)
    key_heads = key_all.reshape(length, heads, DH)
    value_heads = value_all.reshape(length, heads, DH)
    places = jnp.arange(length, dtype=jnp.int32)
    row_side = (places >= first_length[0]).astype(jnp.int32)
    onehot = (
        offset_bucket[:, None] == jnp.arange(bias_table.shape[0], dtype=jnp.int32)[None, :]
    ).astype(jnp.float32)
    bias_rows = lax.dot_general(
        bias_table,
        onehot,
        (((0,), (1,)), ((), ())),
        precision=highest,
        preferred_element_type=jnp.float32,
    )
    block = min(512, length)
    count = length // block
    starts = jnp.arange(count, dtype=jnp.int32) * block
    query_blocks = query_all.reshape(count, block, heads, DH)

    def block_scores(query_block, start):
        bias_block = skew_bias(bias_rows, start, block, length)
        block_side = lax.dynamic_slice_in_dim(row_side, start, block)
        visible = block_side[:, None] == row_side[None, :]
        scores = (
            jnp.einsum("qhd,khd->hqk", query_block, key_heads, preferred_element_type=jnp.float32)
            + bias_block
        )
        return jnp.where(visible[None], scores, masked_score)

    def forward_block(items):
        query_block, start = items
        scores = block_scores(query_block, start)
        row_max = jnp.max(scores, axis=-1, keepdims=True)
        expo = jnp.exp(scores - row_max)
        row_total = jnp.sum(expo, axis=-1, keepdims=True)
        weights = (expo / row_total).astype(jnp.bfloat16)
        block_mixed = jnp.einsum(
            "hqk,khd->qhd", weights, value_heads, preferred_element_type=jnp.float32
        )
        return (block_mixed.astype(jnp.bfloat16), (row_max + jnp.log(row_total))[..., 0])

    mixed_blocks, log_totals = lax.map(forward_block, (query_blocks, starts))
    mixed = mixed_blocks.reshape(length, heads * DH)
    attn_terms = jnp.dot(mixed, w_out, preferred_element_type=jnp.float32)
    attn_part = lax.psum_scatter(attn_terms, "mp", scatter_dimension=0, tiled=True)
    residual = inputs + attn_part
    normed_ff_part = normalize(residual, gain_ff).astype(jnp.bfloat16)
    normed_ff = lax.all_gather(normed_ff_part, "mp", axis=0, tiled=True)
    gate_val = jnp.dot(normed_ff, w_gate, preferred_element_type=jnp.float32)
    up_val = jnp.dot(normed_ff, w_up, preferred_element_type=jnp.float32)
    hidden = gated(gate_val, up_val).astype(jnp.bfloat16)
    ff_terms = jnp.dot(hidden, w_down, preferred_element_type=jnp.float32)
    ff_part = lax.psum_scatter(
        ff_terms.astype(jnp.bfloat16), "mp", scatter_dimension=0, tiled=True
    ).astype(jnp.float32)
    output = (residual + ff_part).astype(jnp.bfloat16)
    cot_full = lax.all_gather(cotangent, "mp", axis=0, tiled=True)
    grad_down_t = contract_rows(cot_full, hidden)
    grad_hidden = contract_cols(cot_full, w_down)
    _, gated_pull = jax.vjp(gated, gate_val, up_val)
    grad_gate_act, grad_up_act = gated_pull(grad_hidden)
    grad_gate_act = grad_gate_act.astype(jnp.bfloat16)
    grad_up_act = grad_up_act.astype(jnp.bfloat16)
    grad_gate = contract_rows(normed_ff, grad_gate_act)
    grad_up = contract_rows(normed_ff, grad_up_act)
    normed_ff_terms = contract_cols(grad_gate_act, w_gate) + contract_cols(grad_up_act, w_up)
    grad_normed_ff = lax.psum_scatter(normed_ff_terms, "mp", scatter_dimension=0, tiled=True)
    _, norm_ff_pull = jax.vjp(normalize, residual, gain_ff)
    residual_grad, gain_ff_grad = norm_ff_pull(grad_normed_ff)
    residual_grad = cotangent.astype(jnp.float32) + residual_grad
    attn_grad = lax.all_gather(residual_grad.astype(jnp.bfloat16), "mp", axis=0, tiled=True)
    grad_out_t = contract_rows(attn_grad, mixed)
    grad_mixed = (
        contract_cols(attn_grad, w_out).astype(jnp.bfloat16).reshape(count, block, heads, DH)
    )
    span = length + block - 1

    def backward_block(carry, items):
        key_acc, value_acc, bias_acc = carry
        query_block, grad_block, lse_block, start = items
        scores = block_scores(query_block, start)
        probs = jnp.exp(scores - lse_block[..., None])
        probs_low = probs.astype(jnp.bfloat16)
        value_acc = value_acc + jnp.einsum(
            "hqk,qhd->khd", probs_low, grad_block, preferred_element_type=jnp.float32
        )
        inner = jnp.einsum(
            "qhd,khd->hqk", grad_block, value_heads, preferred_element_type=jnp.float32
        )
        center = jnp.sum(probs * inner, axis=-1, keepdims=True)
        score_grad = (probs * (inner - center)).astype(jnp.bfloat16)
        query_grad = jnp.einsum(
            "hqk,khd->qhd", score_grad, key_heads, preferred_element_type=jnp.float32
        ).astype(jnp.bfloat16)
        key_acc = key_acc + jnp.einsum(
            "hqk,qhd->khd", score_grad, query_block, preferred_element_type=jnp.float32
        )
        diagonal_sums = unskew_sum(score_grad.astype(jnp.float32), block, length)
        begin = length - block - start
        current = lax.dynamic_slice_in_dim(bias_acc, begin, span, 1)
        bias_acc = lax.dynamic_update_slice_in_dim(bias_acc, current + diagonal_sums, begin, 1)
        return ((key_acc, value_acc, bias_acc), query_grad)

    empty_heads = jnp.zeros((length, heads, DH), jnp.float32)
    empty_bias = jnp.zeros((heads, 2 * length - 1), jnp.float32)
    carried, query_grads = lax.scan(
        backward_block,
        (empty_heads, empty_heads, empty_bias),
        (query_blocks, grad_mixed, log_totals, starts),
    )
    key_grads, value_grads, offset_grads = carried
    grad_q = query_grads.reshape(length, heads * DH)
    grad_k = key_grads.astype(jnp.bfloat16).reshape(length, heads * DH)
    grad_v = value_grads.astype(jnp.bfloat16).reshape(length, heads * DH)
    grad_query = contract_rows(normed, grad_q)
    grad_key = contract_rows(normed, grad_k)
    grad_value = contract_rows(normed, grad_v)
    normed_terms = (
        contract_cols(grad_q, w_query)
        + contract_cols(grad_k, w_key)
        + contract_cols(grad_v, w_value)
    )
    grad_normed = lax.psum_scatter(normed_terms, "mp", scatter_dimension=0, tiled=True)
    _, norm_pull = jax.vjp(normalize, inputs, gain_attn)
    input_grad, gain_attn_grad = norm_pull(grad_normed)
    grad_input = residual_grad + input_grad
    table_grad = lax.dot_general(
        onehot,
        offset_grads,
        (((0,), (1,)), ((), ())),
        precision=highest,
        preferred_element_type=jnp.float32,
    )
    grad_table = lax.psum(table_grad, "dp")
    grad_gain_attn, grad_gain_ff = lax.psum((gain_attn_grad, gain_ff_grad), ("dp", "mp"))
    sum_query, sum_key, sum_value, sum_out, sum_gate, sum_up, sum_down = (
        lax.psum_scatter(grad_query, "dp", scatter_dimension=0, tiled=True),
        lax.psum_scatter(grad_key, "dp", scatter_dimension=0, tiled=True),
        lax.psum_scatter(grad_value, "dp", scatter_dimension=0, tiled=True),
        lax.psum_scatter(grad_out_t, "dp", scatter_dimension=0, tiled=True),
        lax.psum_scatter(grad_gate, "dp", scatter_dimension=0, tiled=True),
        lax.psum_scatter(grad_up, "dp", scatter_dimension=0, tiled=True),
        lax.psum_scatter(grad_down_t, "dp", scatter_dimension=0, tiled=True),
    )
    return (
        output,
        grad_input,
        grad_gain_attn,
        sum_query,
        sum_key,
        sum_value,
        sum_out.T,
        grad_table,
        grad_gain_ff,
        sum_gate,
        sum_up,
        sum_down.T,
    )


def solution(mesh):
    placed = (
        P(("dp", "mp"), None),
        P(),
        P(None, "mp"),
        P(None, "mp"),
        P(None, "mp"),
        P("mp", None),
        P(None, "mp"),
        P(),
        P(None, "mp"),
        P(None, "mp"),
        P("mp", None),
        P(("dp", "mp"), None),
        P("dp"),
        P(),
    )
    return jax.shard_map(
        shards,
        mesh=mesh,
        in_specs=placed,
        out_specs=(
            P(("dp", "mp"), None),
            P(("dp", "mp"), None),
            P(),
            P("dp", "mp"),
            P("dp", "mp"),
            P("dp", "mp"),
            P("mp", "dp"),
            P(None, "mp"),
            P(),
            P("dp", "mp"),
            P("dp", "mp"),
            P("mp", "dp"),
        ),
        check_vma=False,
    )
```

profile of v0, /device:TPU:0, one launch (start us, length us, event | category | flops | bytes accessed | tf_op | source)
XLA Modules:
  0.0 1743.7 jit_solution(15951200550955895964)
XLA Ops:
  13.7 29.9 %all-gather.5.cloned.1.call-done = bf16[1024,1536]{1,0:T(8,128)(2,1)} async-done(((bf16[256,1536]{1,0:T(8,128)(2,1)}), bf16[1024,1536]{1,0:T(8,128)(2,1)}) %all-gather.5.cloned.1.call-update) | async-done | bytes 3145744 | tf_op jit(solution)/shard_map/all_gather | solution.py:69
  56.0 235.1 %while.33 = (s32[]{:T(128)}, bf16[2,512,3,64]{1,3,2,0:T(8,128)(2,1)}, f32[2,3,512]{2,1,0:T(4,128)S(1)}, s32[2]{0:T(128)S(1)}, s32[1024]{0:T(1024)S(1)}, /*index=...) while((s32[]{:T(128)}, ...), condition=%wide.region_4.5_spmd, body=%wide.region_1.4_spmd.sunk | while | flops 415857152 | bytes 142301488 | solution.py:116
  66.1 15.2 reshape.239
  116.7 48.5 %rev.23 = f32[3,512,1024]{2,1,0:T(8,128)} reverse(f32[3,512,1024]{2,1,0:T(8,128)} %slice.26), dimensions={1} | reverse | bytes 12582912 | tf_op jit(solution)/shard_map/while/body/eval_jaxpr/rev | solution.py:40
  183.5 15.2 reshape.239
  234.0 48.5 %rev.23 = f32[3,512,1024]{2,1,0:T(8,128)} reverse(f32[3,512,1024]{2,1,0:T(8,128)} %slice.26), dimensions={1} | reverse | bytes 12582912 | tf_op jit(solution)/shard_map/while/body/eval_jaxpr/rev | solution.py:40
  298.1 58.5 %reduce-scatter.14.cloned.1.call-done = f32[256,1536]{1,0:T(8,128)} async-done(((f32[1024,1536]{1,0:T(8,128)}), f32[256,1536]{1,0:T(8,128)}) %reduce-scatter.14.cloned.1.call-update) | async-done | bytes 1572880 | tf_op jit(solution)/shard_map/reduce_scatter | solution.py:119
  361.3 28.1 %all-gather.7.cloned.1.call-done = bf16[1024,1536]{1,0:T(8,128)(2,1)} async-done(((bf16[256,1536]{1,0:T(8,128)(2,1)}), bf16[1024,1536]{1,0:T(8,128)(2,1)}) %all-gather.7.cloned.1.call-update) | async-done | bytes 3145744 | tf_op jit(solution)/shard_map/all_gather | solution.py:122
  402.9 16.6 all-gather.9.cloned.1.call-done
  439.2 58.5 %reduce-scatter.18.cloned.1.call-done = f32[256,1536]{1,0:T(8,128)} async-done(((f32[1024,1536]{1,0:T(8,128)}), f32[256,1536]{1,0:T(8,128)}) %reduce-scatter.18.cloned.1.call-update) | async-done | bytes 1572880 | tf_op jit(solution)/shard_map/reduce_scatter | solution.py:141
  503.3 28.6 %all-gather.11.cloned.1.call-done = bf16[1024,1536]{1,0:T(8,128)(2,1)} async-done(((bf16[256,1536]{1,0:T(8,128)(2,1)}), bf16[1024,1536]{1,0:T(8,128)(2,1)}) %all-gather.11.cloned.1.call-update) | async-done | bytes 3145744 | tf_op jit(solution)/shard_map/all_gather | solution.py:145
  545.3 512.2 %while.34 = (s32[]{:T(128)}, f32[1024,3,64]{0,2,1:T(8,128)}, f32[1024,3,64]{0,2,1:T(8,128)}, f32[3,2047]{1,0:T(4,128)}, bf16[2,512,3,64]{1,3,2,0:T(8,128)(2,1)},...) while((s32[]{:T(128)}, f32[1024,3,64]{0,2,1:T(8,128)}, ...), condition=%wide.region_13.14_spmd.clone, body=%wide.region_10.13_spmd.clone.sunk | while | flops 1024553984 | bytes 295891232 | solution.py:180
  582.1 15.2 reshape.241
  597.3 13.2 reshape.242
  632.5 48.4 %rev.24 = f32[3,512,1024]{2,1,0:T(8,128)} reverse(f32[3,512,1024]{2,1,0:T(8,128)} %slice.27), dimensions={1} | reverse | bytes 12582912 | tf_op jit(solution)/shard_map/while/body/eval_jaxpr/rev | solution.py:40
  696.5 45.9 %rev.25 = f32[3,512,1024]{2,1,0:T(8,128)} reverse(bf16[3,512,1024]{2,1,0:T(8,128)(2,1)} %copy-done.1), dimensions={1} | reverse | bytes 9437184 | tf_op jit(solution)/shard_map/while/body/eval_jaxpr/rev | solution.py:46
  746.4 19.9 %copy.62 = f32[1,3,512,1536]{3,1,2,0:T(4,128)S(1)} copy(f32[1,3,512,1536]{3,2,1,0:T(8,128)S(1)} %pad_bitcast_fusion.2) | data formatting | bytes 18874368 | tf_op jit(solution)/shard_map/while
  772.1 13.2 reshape.243
  785.3 15.5 reshape.244
  821.9 15.1 reshape.241
  872.2 48.4 %rev.24 = f32[3,512,1024]{2,1,0:T(8,128)} reverse(f32[3,512,1024]{2,1,0:T(8,128)} %slice.27), dimensions={1} | reverse | bytes 12582912 | tf_op jit(solution)/shard_map/while/body/eval_jaxpr/rev | solution.py:40
  938.7 45.9 %rev.25 = f32[3,512,1024]{2,1,0:T(8,128)} reverse(bf16[3,512,1024]{2,1,0:T(8,128)(2,1)} %copy-done.1), dimensions={1} | reverse | bytes 9437184 | tf_op jit(solution)/shard_map/while/body/eval_jaxpr/rev | solution.py:46
  988.6 19.9 %copy.62 = f32[1,3,512,1536]{3,1,2,0:T(4,128)S(1)} copy(f32[1,3,512,1536]{3,2,1,0:T(8,128)S(1)} %pad_bitcast_fusion.2) | data formatting | bytes 18874368 | tf_op jit(solution)/shard_map/while
  1027.5 15.5 reshape.244
  1121.2 21.9 %psum.22 = f32[32,3]{0,1:T(4,128)} all-reduce(f32[32,3]{0,1:T(4,128)S(1)} %fusion.47), channel_id=1, replica_groups=mesh['dp'=8,'mp'=4] {'dp'}, use_global_device_ids=true, to_apply=%region_22.23 | all-reduce | flops 96 | bytes 768 | tf_op jit(solution)/shard_map/psum | solution.py:208
  1147.2 37.4 %all-reduce.3 = (f32[1536]{0:T(1024)}, f32[1536]{0:T(1024)}) all-reduce(f32[1536]{0:T(1024)S(1)} %get-tuple-element.444, f32[1536]{0:T(1024)S(1)} %copy-done.21), channel_id=1, replica_groups=mesh['dp'=8,'mp'=4] {'dp','mp'}, use_global_device_ids=true, to_apply=%region_17.18 | all-reduce | flops 3072 | bytes 24576 | tf_op jit(solution)/shard_map/psum | solution.py:209
  1189.9 99.7 %reduce-scatter.34.cloned.1.call-done = f32[192,992]{1,0:T(8,128)} async-done(((f32[1536,992]{1,0:T(8,128)}), f32[192,992]{1,0:T(8,128)}) %reduce-scatter.34.cloned.1.call-update) | async-done | bytes 761872
  1289.6 121.7 %reduce-scatter.32.cloned.1.call-done = f32[192,992]{1,0:T(8,128)} async-done(((f32[1536,992]{1,0:T(8,128)}), f32[192,992]{1,0:T(8,128)}) %reduce-scatter.32.cloned.1.call-update) | async-done | bytes 761872 | tf_op jit(solution)/shard_map/reduce_scatter | solution.py:216
  1411.2 121.6 %reduce-scatter.30.cloned.1.call-done = f32[192,992]{1,0:T(8,128)} async-done(((f32[1536,992]{1,0:T(8,128)}), f32[192,992]{1,0:T(8,128)}) %reduce-scatter.30.cloned.1.call-update) | async-done | bytes 761872 | tf_op jit(solution)/shard_map/reduce_scatter | solution.py:215
  1532.8 68.5 %reduce-scatter.26.cloned.1.call-done = f32[192,192]{1,0:T(8,128)} async-done(((f32[1536,192]{1,0:T(8,128)}), f32[192,192]{1,0:T(8,128)}) %reduce-scatter.26.cloned.1.call-update) | async-done | bytes 147472 | tf_op jit(solution)/shard_map/reduce_scatter | solution.py:213
  1601.3 67.6 %reduce-scatter.22.cloned.1.call-done = f32[192,192]{1,0:T(8,128)} async-done(((f32[1536,192]{1,0:T(8,128)}), f32[192,192]{1,0:T(8,128)}) %reduce-scatter.22.cloned.1.call-update) | async-done | bytes 147472 | tf_op jit(solution)/shard_map/reduce_scatter | solution.py:211
  1668.9 68.0 %reduce-scatter.24.cloned.1.call-done = f32[192,192]{1,0:T(8,128)} async-done(((f32[1536,192]{1,0:T(8,128)}), f32[192,192]{1,0:T(8,128)}) %reduce-scatter.24.cloned.1.call-update) | async-done | bytes 147472 | tf_op jit(solution)/shard_map/reduce_scatter | solution.py:212
  (248 shorter events, 414.8 us)
Async XLA Ops:
  7.2 412.3 %copy-start = (bf16[992,1536]{1,0:T(8,128)(2,1)S(1)}, bf16[992,1536]{1,0:T(8,128)(2,1)}, u32[]{:S(2)}) copy-start(bf16[992,1536]{1,0:T(8,128)(2,1)} %param.28) | copy-start | bytes 9142276
  7.2 5.8 copy-start.35
  7.2 5.8 copy-start.37
  7.2 36.4 %all-gather.5.cloned.1.call-start = ((), (), s32[]{:S(2)}) async-start(), calls=%async_computation.11 | async-start | bytes 3932160 | tf_op jit(solution)/shard_map/all_gather | solution.py:69
  12.2 344.3 %reduce-scatter.14.cloned.1.call-start = ((), (), s32[]{:S(2)}) async-start(), calls=%async_computation.12 | async-start | bytes 7864320 | tf_op jit(solution)/shard_map/reduce_scatter | solution.py:119
  48.8 5.2 copy-start.16
  298.1 61.6 %copy-start.18 = (f32[1536]{0:T(1024)S(1)}, f32[1536]{0:T(1024)}, u32[]{:S(2)}) copy-start(f32[1536]{0:T(1024)} %param.25) | copy-start | bytes 18436
  298.1 91.3 %all-gather.7.cloned.1.call-start = ((), (), s32[]{:S(2)}) async-start(), calls=%async_computation.13 | async-start | bytes 3932160 | tf_op jit(solution)/shard_map/all_gather | solution.py:122
  358.5 142.2 %copy-start.22 = (f32[256]{0:T(256)}, f32[256]{0:T(256)S(1)}, u32[]{:S(2)}) copy-start(f32[256]{0:T(256)S(1)} %fusion.52) | copy-start | bytes 3076
  360.7 58.8 %all-gather.9.cloned.1.call-start = ((), (), s32[]{:S(2)}) async-start(), calls=%async_computation.15 | async-start | bytes 3932160 | tf_op jit(solution)/shard_map/all_gather | solution.py:131
  361.3 136.4 %reduce-scatter.18.cloned.1.call-start = ((), (), s32[]{:S(2)}) async-start(), calls=%async_computation.16 | async-start | bytes 7864320 | tf_op jit(solution)/shard_map/reduce_scatter | solution.py:141
  389.4 8.2 copy-start.31
  389.4 8.2 copy-start.32
  419.5 10.4 copy-start.33
  439.2 92.8 %all-gather.11.cloned.1.call-start = ((), (), s32[]{:S(2)}) async-start(), calls=%async_computation.17 | async-start | bytes 3932160 | tf_op jit(solution)/shard_map/all_gather | solution.py:145
  500.7 35.2 %copy-start.26 = (f32[256]{0:T(256)}, f32[256]{0:T(256)S(1)}, u32[]{:S(2)}) copy-start(f32[256]{0:T(256)S(1)} %multiply_multiply_fusion.4) | copy-start | bytes 3076
  503.2 640.0 %reduce-scatter.28.cloned.1.call-start = ((), (), s32[]{:S(2)}) async-start(), calls=%async_computation.22 | async-start | bytes 1769472 | tf_op jit(solution)/shard_map/reduce_scatter | solution.py:214
  543.8 601.1 %reduce-scatter.20.cloned.1.call-start = ((), (), s32[]{:S(2)}) async-start(), calls=%async_computation.18 | async-start | bytes 7864320 | tf_op jit(solution)/shard_map/reduce_scatter | solution.py:197
  1067.5 117.1 %reduce-scatter.16.cloned.1.call-start = ((), (), s32[]{:S(2)}) async-start(), calls=%async_computation.14 | async-start | bytes 3932160 | tf_op jit(solution)/shard_map/reduce_scatter | solution.py:127
  1074.1 215.4 %reduce-scatter.34.cloned.1.call-start = ((), (), s32[]{:S(2)}) async-start(), calls=%async_computation.25 | async-start | bytes 7077888
  1090.0 321.2 %reduce-scatter.32.cloned.1.call-start = ((), (), s32[]{:S(2)}) async-start(), calls=%async_computation.24 | async-start | bytes 7077888 | tf_op jit(solution)/shard_map/reduce_scatter | solution.py:216
  1098.7 434.1 %reduce-scatter.30.cloned.1.call-start = ((), (), s32[]{:S(2)}) async-start(), calls=%async_computation.23 | async-start | bytes 7077888 | tf_op jit(solution)/shard_map/reduce_scatter | solution.py:215
  1107.8 493.5 %reduce-scatter.26.cloned.1.call-start = ((), (), s32[]{:S(2)}) async-start(), calls=%async_computation.21 | async-start | bytes 1769472 | tf_op jit(solution)/shard_map/reduce_scatter | solution.py:213
  1112.1 556.8 %reduce-scatter.22.cloned.1.call-start = ((), (), s32[]{:S(2)}) async-start(), calls=%async_computation.19 | async-start | bytes 1769472 | tf_op jit(solution)/shard_map/reduce_scatter | solution.py:211
  1116.3 28.6 %copy-start.20 = (f32[1536]{0:T(1024)S(1)}, f32[1536]{0:T(1024)}, u32[]{:S(2)}) copy-start(f32[1536]{0:T(1024)} %param.19) | copy-start | bytes 18436
  1116.3 28.6 %copy-start.25 = (f32[256]{0:T(256)S(1)}, f32[256]{0:T(256)}, u32[]{:S(2)}) copy-start(f32[256]{0:T(256)} %copy-done.24) | copy-start | bytes 3076
  1116.3 620.6 %reduce-scatter.24.cloned.1.call-start = ((), (), s32[]{:S(2)}) async-start(), calls=%async_computation.20 | async-start | bytes 1769472 | tf_op jit(solution)/shard_map/reduce_scatter | solution.py:212
  1120.6 26.6 %copy-start.21 = (f32[1536]{0:T(1024)S(1)}, f32[1536]{0:T(1024)}, u32[]{:S(2)}) copy-start(f32[1536]{0:T(1024)} %get-tuple-element.442) | copy-start | bytes 18436
  1120.6 64.0 %copy-start.29 = (f32[256]{0:T(256)S(1)}, f32[256]{0:T(256)}, u32[]{:S(2)}) copy-start(f32[256]{0:T(256)} %copy-done.28) | copy-start | bytes 3076
  1120.6 64.0 %copy-start.19 = (f32[1536]{0:T(1024)S(1)}, f32[1536]{0:T(1024)}, u32[]{:S(2)}) copy-start(f32[1536]{0:T(1024)} %param.25) | copy-start | bytes 18436
  1120.6 64.0 %copy-start.23 = (f32[256]{0:T(256)S(1)}, f32[256]{0:T(256)}, u32[]{:S(2)}) copy-start(f32[256]{0:T(256)} %copy-done.22) | copy-start | bytes 3076
  1120.6 64.0 %copy-start.27 = (f32[256]{0:T(256)S(1)}, f32[256]{0:T(256)}, u32[]{:S(2)}) copy-start(f32[256]{0:T(256)} %copy-done.26) | copy-start | bytes 3076
  (29 other events, 72.4 us)
Sparse Core Ops, SparseCore 0:
  12.3 31.2 all-gather.4
  298.2 58.3 reduce-scatter.13
  360.8 28.5 all-gather.6
  390.9 28.5 all-gather.8
  439.3 58.3 reduce-scatter.17
  503.3 28.5 all-gather.10
  543.9 64.8 reduce-scatter.27
  1067.6 58.3 reduce-scatter.19
  1128.5 38.6 reduce-scatter.15
  1171.6 117.8 reduce-scatter.33
  1294.1 117.0 reduce-scatter.31
  1415.7 117.1 reduce-scatter.29
  1537.2 64.0 reduce-scatter.25
  1605.1 63.6 reduce-scatter.21
  1673.1 63.7 reduce-scatter.23
where the time goes:
time: 1770 us; the launch traced here: 1740 us
  waiting for transfers between devices  768 us (43%)
  local copies, waits for them, and re-layouts  653 us (37%)
  matrix products  155 us (9%)
  blocking collectives  59.3 us (3%)
  other arithmetic  47.9 us (3%)
  loops' own time  43.6 us (2%)
    rev x4, local copies, waits for them, and re-layouts, skew_bias(): return tiled[:, ::-1, :length]  194 us
    while x38, local copies, waits for them, and re-layouts  167 us
    reduce_scatter x1, waiting for transfers between devices, shards(): lax.psum_scatter(grad_up, 'dp', scatter_dimension=0, tiled=True)  122 us
    reduce_scatter x1, waiting for transfers between devices, shards(): lax.psum_scatter(grad_gate, 'dp', scatter_dimension=0, tiled=True)  122 us
    unnamed x16, waiting for transfers between devices  100 us
    rev x2, local copies, waits for them, and re-layouts, unskew_sum(): flipped = grads[:, ::-1, :]  91.8 us
    reduce_scatter x1, waiting for transfers between devices, shards(): lax.psum_scatter(grad_value, 'dp', scatter_dimension=0, tiled=True)  68.5 us
    reduce_scatter x1, waiting for transfers between devices, shards(): lax.psum_scatter(grad_key, 'dp', scatter_dimension=0, tiled=True)  68 us
  transfers between devices with their start and end apart: 15, of which 12 were waited for; matrix products, arithmetic and copies ran while one was open for 32% of the time, Pallas kernels for 0%

commit v1 on v0

--- a/solution.py
+++ b/solution.py
@@ -1,14 +1,356 @@
+import functools
+
 import jax
 import jax.numpy as jnp
 from jax import lax
+from jax.experimental import pallas as pl
+from jax.experimental.pallas import tpu as pltpu
 from jax.sharding import PartitionSpec as P
 
+MESH = pl.DeviceIdType.MESH
 DH = 64
-
-
 epsilon = 1e-06
 masked_score = -1000000000.0
 highest = lax.Precision.HIGHEST
+bf16 = jnp.bfloat16
+f32 = jnp.float32
+VMEM_BYTES = 60 * 2**20
+
+
+def mm(left, right):
+    return jnp.dot(left, right, preferred_element_type=f32)
+
+
+def contract_rows(left, right):
+    return lax.dot_general(left, right, (((0,), (0,)), ((), ())), preferred_element_type=f32)
+
+
+def contract_cols(left, right):
+    return lax.dot_general(left, right, (((1,), (1,)), ((), ())), preferred_element_type=f32)
+
+
+def rms(values):
+    return values * lax.rsqrt(jnp.mean(values * values, axis=-1, keepdims=True) + epsilon)
+
+
+class Links:
+    def __init__(self, send, recv):
+        self.send, self.recv, self.used = send, recv, 0
+
+    def copy(self, src, dst, to):
+        at = self.used
+        self.used += 1
+        return pltpu.make_async_remote_copy(
+            src_ref=src,
+            dst_ref=dst,
+            send_sem=self.send.at[at],
+            recv_sem=self.recv.at[at],
+            device_id=to,
+            device_id_type=MESH,
+        )
+
+
+class Group:
+    def __init__(self):
+        self.dp, self.me = lax.axis_index("dp"), lax.axis_index("mp")
+        self.core = self.me + 1 - 2 * lax.rem(self.me, 2)
+        self.far = lax.rem(self.me + 2, 4)
+        self.diag = 3 - self.me
+
+    def at(self, mp):
+        return (self.dp, mp)
+
+
+def greet(peers):
+    barrier = pltpu.get_barrier_semaphore()
+    for peer in peers:
+        pl.semaphore_signal(barrier, inc=1, device_id=peer, device_id_type=MESH)
+    pl.semaphore_wait(barrier, len(peers))
+
+
+def block_rows(dev, rows, start=0, size=None):
+    return pl.ds(pl.multiple_of(dev * rows + start, 16), rows if size is None else size)
+
+
+class Gather:
+    def __init__(self, links, group, full, rows, chunks, source=None):
+        size = rows // chunks
+        own = block_rows(group.me, rows)
+        self.near = links.copy(full.at[own] if source is None else source, full.at[own], group.at(group.core))
+        self.far, self.passed = [], []
+        for i in range(chunks):
+            mine = block_rows(group.me, rows, i * size, size)
+            theirs = block_rows(group.far, rows, i * size, size)
+            src = full.at[mine] if source is None else source.at[pl.ds(i * size, size)]
+            self.far.append(links.copy(src, full.at[mine], group.at(group.far)))
+            self.passed.append(links.copy(full.at[theirs], full.at[theirs], group.at(group.core)))
+
+    def start(self):
+        self.near.start()
+        for copy in self.far:
+            copy.start()
+
+    def forward(self, i):
+        self.far[i].wait_recv()
+        self.passed[i].start()
+
+    def wait_send(self):
+        self.near.wait_send()
+        for copy in self.far + self.passed:
+            copy.wait_send()
+
+
+def build_strips(strip, bucket, table):
+    buckets, heads = table.shape
+    index = bucket[...]
+    width = index.shape[1]
+    for h in range(heads):
+        row = jnp.zeros(index.shape, f32)
+        for b in range(buckets):
+            row = jnp.where(index == b, table[b, h], row)
+        strip[h] = pltpu.roll(
+            jnp.broadcast_to(row, (128, width)), width - 127, 1, stride=1, stride_axis=0
+        )
+
+
+def add_bias(scores, strip, h, dev, length):
+    parts = []
+    count = length // 128
+    for i in range(scores.shape[0] // 128):
+        first = (count - 1 - i) * 128 - dev * scores.shape[0]
+        parts.append(
+            scores[i * 128 : (i + 1) * 128]
+            + strip[h, :, pl.ds(pl.multiple_of(first, 128), length)]
+        )
+    return jnp.concatenate(parts, axis=0)
+
+
+def visible_pairs(dev, rows, length, first):
+    query = lax.broadcasted_iota(jnp.int32, (rows, length), 0) + dev * rows >= first
+    key = lax.broadcasted_iota(jnp.int32, (rows, length), 1) >= first
+    return query == key
+
+
+def head_lanes(shape, h):
+    lane = lax.broadcasted_iota(jnp.int32, shape, len(shape) - 1)
+    return (lane >= h * DH) & (lane < (h + 1) * DH)
+
+
+def attend_kernel(
+    quarters,
+    tokens,
+    gain_attn,
+    gain_ff,
+    w_query,
+    w_key,
+    w_value,
+    bucket,
+    table,
+    first,
+    w_out,
+    cot,
+    qkv,
+    mixed,
+    lse,
+    h1,
+    normed_ff,
+    normed_out,
+    cot_full,
+    normed,
+    out_full,
+    mixed_all,
+    strip,
+    key_heads,
+    value_heads,
+    mixed_sum,
+    send,
+    recv,
+    local,
+):
+    group = Group()
+    me, core, far, diag = group.me, group.core, group.far, group.diag
+    rows, width = tokens.shape
+    length = 4 * rows
+    heads = table.shape[1]
+    links = Links(send, recv)
+    zs = []
+    if quarters > 1:
+        z = group.dp // 2
+        zs = [lax.rem(z + t, 4) for t in (1, 2, 3)]
+        z_peers = [(2 * other + lax.rem(group.dp, 2), me) for other in zs]
+    peers = [group.at(core), group.at(far), group.at(diag)]
+    if quarters > 1:
+        peers += z_peers
+    out_own = pltpu.make_async_copy(w_out, out_full.at[me], local.at[0])
+    out_own.start()
+    cot_own = pltpu.make_async_copy(cot, cot_full.at[block_rows(me, rows)], local.at[1])
+    cot_own.start()
+    greet(peers)
+
+    x = tokens[...].astype(f32)
+    normed[block_rows(me, rows), :] = (rms(x) * gain_attn[...]).astype(bf16)
+    gather = Gather(links, group, normed, rows, 2)
+    gather.start()
+    out_own.wait()
+    depth = w_out.shape[0]
+    part = depth // quarters
+    mine = pl.ds(pl.multiple_of((z if quarters > 1 else 0) * part, 16), part)
+    out_near = links.copy(out_full.at[me], out_full.at[me], group.at(core))
+    out_far = links.copy(out_full.at[me, mine], out_full.at[me, mine], group.at(far))
+    out_near.start()
+    out_z = []
+    if quarters > 1:
+        for peer in z_peers:
+            out_z.append(links.copy(out_full.at[far, mine], out_full.at[far, mine], peer))
+    out_pass = links.copy(out_full.at[far], out_full.at[far], group.at(core))
+    cot_gather = Gather(links, group, cot_full, rows, 4, source=cot)
+    cot_gather.near.start()
+    mixed_near = links.copy(
+        mixed.at[block_rows(core, rows)], mixed_all.at[me], group.at(core)
+    )
+    mixed_far = links.copy(mixed.at[block_rows(far, rows)], mixed_all.at[me], group.at(far))
+    mixed_diag = links.copy(mixed.at[block_rows(diag, rows)], mixed_all.at[me], group.at(diag))
+
+    build_strips(strip, bucket, table)
+
+    def project(dev):
+        block = normed[block_rows(dev, rows), :]
+        at = block_rows(dev, rows)
+        qkv[0, at, :] = mm(block, w_query[...]).astype(bf16)
+        key = mm(block, w_key[...]).astype(bf16)
+        value = mm(block, w_value[...]).astype(bf16)
+        qkv[1, at, :] = key
+        qkv[2, at, :] = value
+        for h in range(heads):
+            lanes = head_lanes(key.shape, h)
+            key_heads[h, at, :] = jnp.where(lanes, key, jnp.zeros_like(key))
+            value_heads[h, at, :] = jnp.where(lanes, value, jnp.zeros_like(value))
+
+    project(me)
+    gather.near.wait_recv()
+    project(core)
+    gather.forward(0)
+    gather.forward(1)
+    out_far.start()
+    project(far)
+    for copy in gather.passed:
+        copy.wait_recv()
+    normed_save = pltpu.make_async_copy(normed, normed_out, local.at[2])
+    normed_save.start()
+    project(diag)
+
+    def attend(dev):
+        at = block_rows(dev, rows)
+        seen = visible_pairs(dev, rows, length, first[0])
+        mixed_sum[...] = jnp.zeros_like(mixed_sum)
+        lse[at, :] = jnp.zeros((rows, 128), f32)
+
+        def one_head(h, carry):
+            scores = contract_cols(qkv[0, at, :], key_heads[h])
+            scores = jnp.where(seen, add_bias(scores, strip, h, dev, length), masked_score)
+            top = jnp.max(scores, axis=-1, keepdims=True)
+            expo = jnp.exp(scores - top)
+            total = jnp.sum(expo, axis=-1, keepdims=True)
+            weights = (expo * (1.0 / total)).astype(bf16)
+            mixed_sum[...] += mm(weights, value_heads[h])
+            lane = lax.broadcasted_iota(jnp.int32, (rows, 128), 1)
+            lse[at, :] = jnp.where(lane == h, top + jnp.log(total), lse[at, :])
+            return carry
+
+        lax.fori_loop(0, heads, one_head, 0)
+        mixed[at, :] = mixed_sum[...].astype(bf16)
+
+    attend(far)
+    mixed_far.start()
+    out_far.wait_recv()
+    for copy in out_z:
+        copy.start()
+    for copy in cot_gather.far:
+        copy.start()
+    attend(diag)
+    mixed_diag.start()
+    attend(core)
+    mixed_near.start()
+    for copy in out_z:
+        copy.wait_recv()
+    out_pass.start()
+    cot_gather.forward(0)
+    attend(me)
+    mixed_all[me] = mixed[block_rows(me, rows), :]
+    cot_gather.forward(1)
+    out_near.wait_recv()
+    attn = mm(mixed_all[me], out_full[me])
+    mixed_near.wait_recv()
+    attn = attn + mm(mixed_all[core], out_full[core])
+    mixed_far.wait_recv()
+    attn = attn + mm(mixed_all[far], out_full[far])
+    mixed_diag.wait_recv()
+    out_pass.wait_recv()
+    attn = attn + mm(mixed_all[diag], out_full[diag])
+    residual = x + attn
+    h1[...] = residual
+    normed_ff[...] = (rms(residual) * gain_ff[...]).astype(bf16)
+    cot_gather.forward(2)
+    cot_gather.forward(3)
+
+    gather.wait_send()
+    for copy in [out_near, out_far, out_pass, mixed_near, mixed_far, mixed_diag] + out_z:
+        copy.wait_send()
+    cot_gather.near.wait_recv()
+    for copy in cot_gather.passed:
+        copy.wait_recv()
+    cot_gather.wait_send()
+    normed_save.wait()
+    cot_own.wait()
+
+
+def in_vmem():
+    return pl.BlockSpec(memory_space=pltpu.VMEM)
+
+
+def anywhere():
+    return pl.BlockSpec(memory_space=pl.ANY)
+
+
+def in_smem():
+    return pl.BlockSpec(memory_space=pltpu.SMEM)
+
+
+def attention_forward(n_dp, tokens, gain_attn, gain_ff, w_query, w_key, w_value, bucket, table, first, w_out, cot):
+    rows, width = tokens.shape
+    length = 4 * rows
+    cols = w_query.shape[1]
+    heads = table.shape[1]
+    shape = jax.ShapeDtypeStruct
+    return pl.pallas_call(
+        functools.partial(attend_kernel, 4 if n_dp == 8 else 1),
+        out_shape=(
+            shape((3, length, cols), bf16),
+            shape((length, cols), bf16),
+            shape((length, 128), f32),
+            shape((rows, width), f32),
+            shape((rows, width), bf16),
+            shape((length, width), bf16),
+            shape((length, width), bf16),
+        ),
+        in_specs=[in_vmem()] * 7 + [in_smem()] * 2 + [anywhere()] * 2,
+        out_specs=[in_vmem()] * 5 + [anywhere()] * 2,
+        scratch_shapes=[
+            pltpu.VMEM((length, width), bf16),
+            pltpu.VMEM((4, cols, width), bf16),
+            pltpu.VMEM((4, rows, cols), bf16),
+            pltpu.VMEM((heads, 128, 2 * length), f32),
+            pltpu.VMEM((heads, length, cols), bf16),
+            pltpu.VMEM((heads, length, cols), bf16),
+            pltpu.VMEM((rows, cols), f32),
+            pltpu.SemaphoreType.DMA((32,)),
+            pltpu.SemaphoreType.DMA((32,)),
+            pltpu.SemaphoreType.DMA((4,)),
+        ],
+        compiler_params=pltpu.CompilerParams(
+            collective_id=0, has_side_effects=True, vmem_limit_bytes=VMEM_BYTES
+        ),
+    )(tokens, gain_attn, gain_ff, w_query, w_key, w_value, bucket, table, first, w_out, cot)
 
 
 def normalize(values, gain):
@@ -17,18 +359,6 @@
 
 def gated(gate_val, up_val):
     return jax.nn.gelu(gate_val, approximate=True) * up_val
-
-
-def contract_rows(left, right):
-    return lax.dot_general(
-        left, right, (((0,), (0,)), ((), ())), preferred_element_type=jnp.float32
-    )
-
-
-def contract_cols(left, right):
-    return lax.dot_general(
-        left, right, (((1,), (1,)), ((), ())), preferred_element_type=jnp.float32
-    )
 
 
 def skew_bias(bias_rows, start, block, length):
@@ -65,13 +395,15 @@
     offset_bucket,
 ):
     inputs = tokens.astype(jnp.float32)
-    normed_part = normalize(inputs, gain_attn).astype(jnp.bfloat16)
-    normed = lax.all_gather(normed_part, "mp", axis=0, tiled=True)
+    n_dp = lax.axis_size("dp")
+    bucket = jnp.pad(offset_bucket, (0, 1), constant_values=-1)[None, :]
+    qkv, mixed, lse, residual, normed_ff_part, normed, cot_full = attention_forward(
+        n_dp, tokens, gain_attn[None], gain_ff[None], w_query, w_key, w_value, bucket, bias_table,
+        first_length, w_out, cotangent)
+    normed_ff = lax.all_gather(normed_ff_part, "mp", axis=0, tiled=True)
     length = normed.shape[0]
     heads = w_query.shape[1] // DH
-    query_all = jnp.dot(normed, w_query, preferred_element_type=jnp.float32).astype(jnp.bfloat16)
-    key_all = jnp.dot(normed, w_key, preferred_element_type=jnp.float32).astype(jnp.bfloat16)
-    value_all = jnp.dot(normed, w_value, preferred_element_type=jnp.float32).astype(jnp.bfloat16)
+    query_all, key_all, value_all = qkv[0], qkv[1], qkv[2]
     key_heads = key_all.reshape(length, heads, DH)
     value_heads = value_all.reshape(length, heads, DH)
     places = jnp.arange(length, dtype=jnp.int32)
@@ -101,25 +433,7 @@
         )
         return jnp.where(visible[None], scores, masked_score)
 
-    def forward_block(items):
-        query_block, start = items
-        scores = block_scores(query_block, start)
-        row_max = jnp.max(scores, axis=-1, keepdims=True)
-        expo = jnp.exp(scores - row_max)
-        row_total = jnp.sum(expo, axis=-1, keepdims=True)
-        weights = (expo / row_total).astype(jnp.bfloat16)
-        block_mixed = jnp.einsum(
-            "hqk,khd->qhd", weights, value_heads, preferred_element_type=jnp.float32
-        )
-        return (block_mixed.astype(jnp.bfloat16), (row_max + jnp.log(row_total))[..., 0])
-
-    mixed_blocks, log_totals = lax.map(forward_block, (query_blocks, starts))
-    mixed = mixed_blocks.reshape(length, heads * DH)
-    attn_terms = jnp.dot(mixed, w_out, preferred_element_type=jnp.float32)
-    attn_part = lax.psum_scatter(attn_terms, "mp", scatter_dimension=0, tiled=True)
-    residual = inputs + attn_part
-    normed_ff_part = normalize(residual, gain_ff).astype(jnp.bfloat16)
-    normed_ff = lax.all_gather(normed_ff_part, "mp", axis=0, tiled=True)
+    log_totals = lse[:, :heads].reshape(count, block, heads).transpose(0, 2, 1)
     gate_val = jnp.dot(normed_ff, w_gate, preferred_element_type=jnp.float32)
     up_val = jnp.dot(normed_ff, w_up, preferred_element_type=jnp.float32)
     hidden = gated(gate_val, up_val).astype(jnp.bfloat16)
@@ -128,7 +442,6 @@
         ff_terms.astype(jnp.bfloat16), "mp", scatter_dimension=0, tiled=True
     ).astype(jnp.float32)
     output = (residual + ff_part).astype(jnp.bfloat16)
-    cot_full = lax.all_gather(cotangent, "mp", axis=0, tiled=True)
     grad_down_t = contract_rows(cot_full, hidden)
     grad_hidden = contract_cols(cot_full, w_down)
     _, gated_pull = jax.vjp(gated, gate_val, up_val)

time: 1770 us -> 1460 us (0.82)
  local copies, waits for them, and re-layouts: 653 us -> 459 us
  waiting for transfers between devices: 768 us -> 648 us
  Pallas kernels: 0 us -> 61.3 us
  matrix products: 155 us -> 117 us
    unnamed x16 -> x12, waiting for transfers between devices: 100 us -> 0.2 us
    rev x4 -> x2, local copies, waits for them, and re-layouts: 194 us -> 97 us  [skew_bias(): return tiled[:, ::-1, :length]]
    pallas_call x0 -> x1, Pallas kernels: none -> 61.3 us  [attention_forward(): pl.pallas_call(functools.partial(attend_kernel, 4 if n_dp == 8 else 1), o...]
    reduce_scatter x1, waiting for transfers between devices: 58.5 us -> 105 us  [shards(): lax.psum_scatter(grad_down_t, 'dp', scatter_dimension=0, tiled=True)]
    all_gather x2 -> x0, waiting for transfers between devices: 46.5 us -> none  [the longest x1 29.9 us: shards(): normed = lax.all_gather(normed_part, 'mp', axis=0, tiled=True)]
    while x40 -> x38, local copies, waits for them, and re-layouts: 169 us -> 123 us
    reshape x4 -> x2, local copies, waits for them, and re-layouts: 52.7 us -> 26.4 us  [skew_bias(): jnp.broadcast_to(window[:, None, :], (heads, block, span))]
    pad x4 -> x2, local copies, waits for them, and re-layouts: 44.1 us -> 21.9 us  [skew_bias(): jnp.pad(tiled, ((0, 0), (0, block))).reshape(heads, block, length + block)]
  transfers between devices with their start and end apart: 15 -> 12, of which waited for: 12 -> 9; matrix products, arithmetic and copies ran while one was open for 32% -> 39% of each run, Pallas kernels for 0% -> 0%
where the time goes in v1:
time: 1460 us; the launch traced here: 1440 us
  waiting for transfers between devices  648 us (44%)
  local copies, waits for them, and re-layouts  459 us (31%)
  matrix products  117 us (8%)
  Pallas kernels  61.3 us (4%)
  blocking collectives  58.8 us (4%)
  other arithmetic  38.3 us (3%)
  loops' own time  36.1 us (2%)
  between operations  15.6 us (1%)
    while x38, local copies, waits for them, and re-layouts  123 us
    reduce_scatter x1, waiting for transfers between devices, shards(): lax.psum_scatter(grad_gate, 'dp', scatter_dimension=0, tiled=True)  121 us
    reduce_scatter x1, waiting for transfers between devices, shards(): lax.psum_scatter(grad_up, 'dp', scatter_dimension=0, tiled=True)  121 us
    reduce_scatter x1, waiting for transfers between devices, shards(): lax.psum_scatter(grad_down_t, 'dp', scatter_dimension=0, tiled=True)  105 us
    rev x2, local copies, waits for them, and re-layouts, skew_bias(): return tiled[:, ::-1, :length]  97 us
    rev x2, local copies, waits for them, and re-layouts, unskew_sum(): flipped = grads[:, ::-1, :]  91.9 us
    reduce_scatter x1, waiting for transfers between devices, shards(): lax.psum_scatter(grad_query, 'dp', scatter_dimension=0, tiled=True)  68.1 us
    reduce_scatter x1, waiting for transfers between devices, shards(): lax.psum_scatter(grad_value, 'dp', scatter_dimension=0, tiled=True)  67.8 us
  transfers between devices with their start and end apart: 12, of which 9 were waited for; matrix products, arithmetic and copies ran while one was open for 39% of the time, Pallas kernels for 0%

profile of v1, /device:TPU:0, one launch (start us, length us, event | category | flops | bytes accessed | tf_op | source)
XLA Modules:
  0.0 1436.0 jit_solution(4472687245736267071)
XLA Ops:
  19.3 61.3 %shard_map.229 = (bf16[3,1024,192]{2,1,0:T(8,128)(2,1)}, bf16[1024,192]{1,0:T(8,128)(2,1)}, f32[1024,128]{1,0:T(8,128)}, f32[256,1536]{1,0:T(8,128)}, bf16[256,1...) custom-call(bf16[256,1536]{1,0:T(8,128)(2,1)} %tokens.1, ...), custom_call_target="tpu_custom_call" | custom-call | tf_op jit(solution)/shard_map/pallas_call | solution.py:325
  80.9 27.3 %all-gather.3.cloned.1.call-done = bf16[1024,1536]{1,0:T(8,128)(2,1)} async-done(((bf16[256,1536]{1,0:T(8,128)(2,1)}), bf16[1024,1536]{1,0:T(8,128)(2,1)}) %all-gather.3.cloned.1.call-update) | async-done | bytes 3145744 | tf_op jit(solution)/shard_map/all_gather | solution.py:403
  136.1 56.9 %reduce-scatter.13.cloned.1.call-done = f32[256,1536]{1,0:T(8,128)} async-done(((f32[1024,1536]{1,0:T(8,128)}), f32[256,1536]{1,0:T(8,128)}) %reduce-scatter.13.cloned.1.call-update) | async-done | bytes 1572880 | tf_op jit(solution)/shard_map/reduce_scatter | solution.py:454
  214.9 12.8 all-gather.5.cloned.1.call-done
  239.7 512.8 %while.19 = (s32[]{:T(128)}, f32[1024,3,64]{0,2,1:T(8,128)}, f32[1024,3,64]{0,2,1:T(8,128)}, f32[3,2047]{1,0:T(4,128)S(1)}, bf16[2,512,3,64]{1,3,2,0:T(8,128)(2,...) while((s32[]{:T(128)}, f32[1024,3,64]{0,2,1:T(8,128)}, ...), condition=%wide.region_7.8_spmd.clone, body=%wide.region_4.7_spmd.clone.sunk | while | flops 1024553984 | bytes 305328544 | solution.py:493
  279.8 15.1 %reshape.152 = f32[2357760]{0:T(1024)} reshape(f32[3,512,1535]{2,1,0:T(8,128)} %broadcast_in_dim.91) | data formatting | bytes 18862080 | tf_op jit(solution)/shard_map/while
  294.9 13.2 reshape.153
  308.2 11.0 pad.25
  330.2 48.5 %rev.16 = f32[3,512,1024]{2,1,0:T(8,128)} reverse(f32[3,512,1024]{2,1,0:T(8,128)} %slice.37), dimensions={1} | reverse | bytes 12582912 | tf_op jit(solution)/shard_map/while/body/eval_jaxpr/rev | solution.py:370
  394.5 45.9 %rev.17 = f32[3,512,1024]{2,1,0:T(8,128)} reverse(bf16[3,512,1024]{2,1,0:T(8,128)(2,1)} %copy-done.1), dimensions={1} | reverse | bytes 9437184 | tf_op jit(solution)/shard_map/while/body/eval_jaxpr/rev | solution.py:376
  444.5 19.9 %copy.56 = f32[1,3,512,1536]{3,1,2,0:T(4,128)S(1)} copy(f32[1,3,512,1536]{3,2,1,0:T(8,128)S(1)} %pad_bitcast_fusion.2) | data formatting | bytes 18874368 | tf_op jit(solution)/shard_map/while
  470.2 13.2 reshape.154
  483.3 15.6 %reshape.155 = f32[3,512,1535]{2,1,0:T(8,128)} reshape(f32[2357760]{0:T(1024)} %reshape.154) | data formatting | bytes 18862080 | tf_op jit(solution)/shard_map/while/body/eval_jaxpr/reshape | solution.py:378
  521.0 15.1 %reshape.152 = f32[2357760]{0:T(1024)} reshape(f32[3,512,1535]{2,1,0:T(8,128)} %broadcast_in_dim.91) | data formatting | bytes 18862080 | tf_op jit(solution)/shard_map/while
  536.1 13.2 reshape.153
  549.3 11.0 pad.25
  571.4 48.5 %rev.16 = f32[3,512,1024]{2,1,0:T(8,128)} reverse(f32[3,512,1024]{2,1,0:T(8,128)} %slice.37), dimensions={1} | reverse | bytes 12582912 | tf_op jit(solution)/shard_map/while/body/eval_jaxpr/rev | solution.py:370
  636.7 45.9 %rev.17 = f32[3,512,1024]{2,1,0:T(8,128)} reverse(bf16[3,512,1024]{2,1,0:T(8,128)(2,1)} %copy-done.1), dimensions={1} | reverse | bytes 9437184 | tf_op jit(solution)/shard_map/while/body/eval_jaxpr/rev | solution.py:376
  686.7 19.9 %copy.56 = f32[1,3,512,1536]{3,1,2,0:T(4,128)S(1)} copy(f32[1,3,512,1536]{3,2,1,0:T(8,128)S(1)} %pad_bitcast_fusion.2) | data formatting | bytes 18874368 | tf_op jit(solution)/shard_map/while
  712.4 13.2 reshape.154
  725.5 15.6 %reshape.155 = f32[3,512,1535]{2,1,0:T(8,128)} reshape(f32[2357760]{0:T(1024)} %reshape.154) | data formatting | bytes 18862080 | tf_op jit(solution)/shard_map/while/body/eval_jaxpr/reshape | solution.py:378
  768.1 9.5 fusion.56
  777.9 8.6 fusion.55
  786.6 8.6 fusion.54
  809.8 21.6 %psum.22 = f32[32,3]{0,1:T(4,128)} all-reduce(f32[32,3]{0,1:T(4,128)S(1)} %fusion.37), channel_id=1, replica_groups=mesh['dp'=8,'mp'=4] {'dp'}, use_global_device_ids=true, to_apply=%region_17.18 | all-reduce | flops 96 | bytes 768 | tf_op jit(solution)/shard_map/psum | solution.py:521
  835.3 37.2 %all-reduce.3 = (f32[1536]{0:T(1024)}, f32[1536]{0:T(1024)}) all-reduce(f32[1536]{0:T(1024)S(1)} %get-tuple-element.289, f32[1536]{0:T(1024)S(1)} %copy-done.19), channel_id=1, replica_groups=mesh['dp'=8,'mp'=4] {'dp','mp'}, use_global_device_ids=true, to_apply=%region_12.13 | all-reduce | flops 3072 | bytes 24576 | tf_op jit(solution)/shard_map/psum | solution.py:522
  877.7 105.0 %reduce-scatter.29.cloned.1.call-done = f32[192,992]{1,0:T(8,128)} async-done(((f32[1536,992]{1,0:T(8,128)}), f32[192,992]{1,0:T(8,128)}) %reduce-scatter.29.cloned.1.call-update) | async-done | bytes 761872 | tf_op jit(solution)/shard_map/reduce_scatter | solution.py:530
  982.8 121.3 %reduce-scatter.27.cloned.1.call-done = f32[192,992]{1,0:T(8,128)} async-done(((f32[1536,992]{1,0:T(8,128)}), f32[192,992]{1,0:T(8,128)}) %reduce-scatter.27.cloned.1.call-update) | async-done | bytes 761872 | tf_op jit(solution)/shard_map/reduce_scatter | solution.py:529
  1104.0 121.3 %reduce-scatter.25.cloned.1.call-done = f32[192,992]{1,0:T(8,128)} async-done(((f32[1536,992]{1,0:T(8,128)}), f32[192,992]{1,0:T(8,128)}) %reduce-scatter.25.cloned.1.call-update) | async-done | bytes 761872 | tf_op jit(solution)/shard_map/reduce_scatter | solution.py:528
  1225.3 67.8 %reduce-scatter.21.cloned.1.call-done = f32[192,192]{1,0:T(8,128)} async-done(((f32[1536,192]{1,0:T(8,128)}), f32[192,192]{1,0:T(8,128)}) %reduce-scatter.21.cloned.1.call-update) | async-done | bytes 147472 | tf_op jit(solution)/shard_map/reduce_scatter | solution.py:526
  1293.1 68.1 %reduce-scatter.17.cloned.1.call-done = f32[192,192]{1,0:T(8,128)} async-done(((f32[1536,192]{1,0:T(8,128)}), f32[192,192]{1,0:T(8,128)}) %reduce-scatter.17.cloned.1.call-update) | async-done | bytes 147472 | tf_op jit(solution)/shard_map/reduce_scatter | solution.py:524
  1361.3 67.6 %reduce-scatter.19.cloned.1.call-done = f32[192,192]{1,0:T(8,128)} async-done(((f32[1536,192]{1,0:T(8,128)}), f32[192,192]{1,0:T(8,128)}) %reduce-scatter.19.cloned.1.call-update) | async-done | bytes 147472 | tf_op jit(solution)/shard_map/reduce_scatter | solution.py:525
  (198 shorter events, 224.6 us)
Async XLA Ops:
  7.2 110.7 %copy-start = (bf16[992,1536]{1,0:T(8,128)(2,1)S(1)}, bf16[992,1536]{1,0:T(8,128)(2,1)}, u32[]{:S(2)}) copy-start(bf16[992,1536]{1,0:T(8,128)(2,1)} %param.26) | copy-start | bytes 9142276
  7.2 11.5 copy-start.24
  7.2 101.0 %all-gather.3.cloned.1.call-start = ((), (), s32[]{:S(2)}) async-start(), calls=%async_computation.10 | async-start | bytes 3932160 | tf_op jit(solution)/shard_map/all_gather | solution.py:403
  80.7 112.2 %reduce-scatter.13.cloned.1.call-start = ((), (), s32[]{:S(2)}) async-start(), calls=%async_computation.12 | async-start | bytes 7864320 | tf_op jit(solution)/shard_map/reduce_scatter | solution.py:454
  108.2 6.3 copy-start.27
  108.2 6.3 copy-start.29
  125.2 3.5 copy-start.30
  134.4 58.5 %copy-start.16 = (f32[1536]{0:T(1024)S(1)}, f32[1536]{0:T(1024)}, u32[]{:S(2)}) copy-start(f32[1536]{0:T(1024)} %param.23) | copy-start | bytes 18436
  134.4 93.3 %all-gather.5.cloned.1.call-start = ((), (), s32[]{:S(2)}) async-start(), calls=%async_computation.13 | async-start | bytes 3932160 | tf_op jit(solution)/shard_map/all_gather | solution.py:458
  136.1 62.9 %copy-start.20 = (f32[256]{0:T(256)}, f32[256]{0:T(256)S(1)}, u32[]{:S(2)}) copy-start(f32[256]{0:T(256)S(1)} %fusion.41) | copy-start | bytes 3076
  192.9 3.6 copy-start.5
  192.9 3.6 copy-start.8
  199.0 632.4 %reduce-scatter.23.cloned.1.call-start = ((), (), s32[]{:S(2)}) async-start(), calls=%async_computation.18 | async-start | bytes 1769472 | tf_op jit(solution)/shard_map/reduce_scatter | solution.py:527
  201.3 12.9 copy-start.26
  239.6 593.5 %reduce-scatter.15.cloned.1.call-start = ((), (), s32[]{:S(2)}) async-start(), calls=%async_computation.14 | async-start | bytes 7864320 | tf_op jit(solution)/shard_map/reduce_scatter | solution.py:510
  385.1 4.0 copy-start.2
  385.2 4.0 copy-start.7
  626.2 4.0 copy-start.2
  626.3 4.0 copy-start.7
  761.4 111.1 %reduce-scatter.11.cloned.1.call-start = ((), (), s32[]{:S(2)}) async-start(), calls=%async_computation.11 | async-start | bytes 3932160 | tf_op jit(solution)/shard_map/reduce_scatter | solution.py:441
  768.0 214.8 %reduce-scatter.29.cloned.1.call-start = ((), (), s32[]{:S(2)}) async-start(), calls=%async_computation.21 | async-start | bytes 7077888 | tf_op jit(solution)/shard_map/reduce_scatter | solution.py:530
  777.6 326.4 %reduce-scatter.27.cloned.1.call-start = ((), (), s32[]{:S(2)}) async-start(), calls=%async_computation.20 | async-start | bytes 7077888 | tf_op jit(solution)/shard_map/reduce_scatter | solution.py:529
  786.5 438.8 %reduce-scatter.25.cloned.1.call-start = ((), (), s32[]{:S(2)}) async-start(), calls=%async_computation.19 | async-start | bytes 7077888 | tf_op jit(solution)/shard_map/reduce_scatter | solution.py:528
  795.2 498.0 %reduce-scatter.21.cloned.1.call-start = ((), (), s32[]{:S(2)}) async-start(), calls=%async_computation.17 | async-start | bytes 1769472 | tf_op jit(solution)/shard_map/reduce_scatter | solution.py:526
  799.4 561.9 %reduce-scatter.17.cloned.1.call-start = ((), (), s32[]{:S(2)}) async-start(), calls=%async_computation.15 | async-start | bytes 1769472 | tf_op jit(solution)/shard_map/reduce_scatter | solution.py:524
  803.6 5.6 copy-start.25
  803.6 29.5 %copy-start.18 = (f32[1536]{0:T(1024)S(1)}, f32[1536]{0:T(1024)}, u32[]{:S(2)}) copy-start(f32[1536]{0:T(1024)} %param.17) | copy-start | bytes 18436
  803.6 625.3 %reduce-scatter.19.cloned.1.call-start = ((), (), s32[]{:S(2)}) async-start(), calls=%async_computation.16 | async-start | bytes 1769472 | tf_op jit(solution)/shard_map/reduce_scatter | solution.py:525
  807.8 27.5 %copy-start.19 = (f32[1536]{0:T(1024)S(1)}, f32[1536]{0:T(1024)}, u32[]{:S(2)}) copy-start(f32[1536]{0:T(1024)} %get-tuple-element.287) | copy-start | bytes 18436
  807.8 64.7 %copy-start.17 = (f32[1536]{0:T(1024)S(1)}, f32[1536]{0:T(1024)}, u32[]{:S(2)}) copy-start(f32[1536]{0:T(1024)} %param.23) | copy-start | bytes 18436
  807.8 64.7 %copy-start.21 = (f32[256]{0:T(256)S(1)}, f32[256]{0:T(256)}, u32[]{:S(2)}) copy-start(f32[256]{0:T(256)} %copy-done.20) | copy-start | bytes 3076
  807.8 64.7 %copy-start.23 = (f32[256]{0:T(256)S(1)}, f32[256]{0:T(256)}, u32[]{:S(2)}) copy-start(f32[256]{0:T(256)} %copy-done.22) | copy-start | bytes 3076
  (20 other events, 39.7 us)
Sparse Core Ops, SparseCore 0:
  80.8 27.3 all-gather.2
  134.5 58.3 reduce-scatter.12
  199.1 28.5 all-gather.4
  239.8 64.8 reduce-scatter.22
  761.5 58.3 reduce-scatter.14
  822.4 38.1 reduce-scatter.10
  864.7 117.9 reduce-scatter.28
  986.9 117.0 reduce-scatter.26
  1108.2 117.0 reduce-scatter.24
  1229.1 63.9 reduce-scatter.20
  1297.5 63.7 reduce-scatter.16
  1365.1 63.7 reduce-scatter.18

commit v2 on v1

--- a/solution.py
+++ b/solution.py
@@ -216,9 +216,9 @@
     def project(dev):
         block = normed[block_rows(dev, rows), :]
         at = block_rows(dev, rows)
-        qkv[0, at, :] = mm(block, w_query[...]).astype(bf16)
-        key = mm(block, w_key[...]).astype(bf16)
-        value = mm(block, w_value[...]).astype(bf16)
+        qkv[0, at, :] = contract_cols(block, w_query[...]).astype(bf16)
+        key = contract_cols(block, w_key[...]).astype(bf16)
+        value = contract_cols(block, w_value[...]).astype(bf16)
         qkv[1, at, :] = key
         qkv[2, at, :] = value
         for h in range(heads):
@@ -319,7 +319,7 @@
 def attention_forward(n_dp, tokens, gain_attn, gain_ff, w_query, w_key, w_value, bucket, table, first, w_out, cot):
     rows, width = tokens.shape
     length = 4 * rows
-    cols = w_query.shape[1]
+    cols = w_query.shape[0]
     heads = table.shape[1]
     shape = jax.ShapeDtypeStruct
     return pl.pallas_call(
@@ -353,29 +353,768 @@
     )(tokens, gain_attn, gain_ff, w_query, w_key, w_value, bucket, table, first, w_out, cot)
 
 
-def normalize(values, gain):
-    return values * lax.rsqrt(jnp.mean(values * values, axis=-1, keepdims=True) + epsilon) * gain
-
-
-def gated(gate_val, up_val):
-    return jax.nn.gelu(gate_val, approximate=True) * up_val
-
-
-def skew_bias(bias_rows, start, block, length):
-    heads = bias_rows.shape[0]
-    span = length + block - 1
-    window = lax.dynamic_slice_in_dim(bias_rows, length - block - start, span, 1)
-    tiled = jnp.broadcast_to(window[:, None, :], (heads, block, span)).reshape(heads, block * span)
-    tiled = jnp.pad(tiled, ((0, 0), (0, block))).reshape(heads, block, length + block)
-    return tiled[:, ::-1, :length]
-
-
-def unskew_sum(grads, block, length):
-    heads = grads.shape[0]
-    span = length + block - 1
-    flipped = grads[:, ::-1, :]
-    padded = jnp.pad(flipped, ((0, 0), (0, 0), (0, block))).reshape(heads, block * (length + block))
-    return padded[:, : block * span].reshape(heads, block, span).sum(axis=1)
+def norm_pull(values, gain, grad):
+    inverse = lax.rsqrt(jnp.mean(values * values, axis=-1, keepdims=True) + epsilon)
+    scaled = grad * gain
+    along = jnp.mean(values * scaled, axis=-1, keepdims=True)
+    gain_grad = jnp.sum(grad * values * inverse, axis=0, keepdims=True)
+    return inverse * scaled - values * (along * inverse * inverse * inverse), gain_grad
+
+
+class Scatter:
+    def __init__(self, links, group, tx, rx, rows, parts):
+        self.tx, self.rx, self.size = tx, rx, rows // parts
+        core, far = group.at(group.core), group.at(group.far)
+        self.near = links.copy(tx.at[2], rx.at[2], core)
+        self.diag, self.far = [], []
+        for i in range(parts):
+            at = pl.ds(i * self.size, self.size)
+            self.diag.append(links.copy(tx.at[0, at], rx.at[0, at], core))
+            self.far.append(links.copy(tx.at[1, at], rx.at[1, at], far))
+
+    def send_diag(self, i, terms):
+        self.tx[0, pl.ds(i * self.size, self.size), :] = terms.astype(bf16)
+        self.diag[i].start()
+
+    def send_near(self, terms):
+        self.tx[2] = terms.astype(bf16)
+        self.near.start()
+
+    def send_far(self, i, terms):
+        at = pl.ds(i * self.size, self.size)
+        self.diag[i].wait_recv()
+        self.tx[1, at, :] = (terms + self.rx[0, at, :].astype(f32)).astype(bf16)
+        self.far[i].start()
+
+    def total(self, own):
+        self.near.wait_recv()
+        for copy in self.far:
+            copy.wait_recv()
+        return own + self.rx[2].astype(f32) + self.rx[1].astype(f32)
+
+    def wait_send(self):
+        for copy in [self.near] + self.diag + self.far:
+            copy.wait_send()
+
+
+GELU_SLOPE = 0.7978845608028654
+GELU_CUBE = 0.044715
+
+
+def feed_kernel(
+    exchange,
+    normed_own,
+    h1,
+    gain,
+    gate_w,
+    up_w,
+    down_w,
+    cot_full,
+    output,
+    grad_h1,
+    grad_attn,
+    gain_grad,
+    down_out,
+    gate_out,
+    up_out,
+    normed,
+    cot,
+    wg,
+    wu,
+    wd,
+    gate,
+    up,
+    back,
+    hidden,
+    gate_act,
+    up_act,
+    far_terms,
+    own_terms,
+    tx,
+    rx,
+    tx_ff,
+    rx_ff,
+    down_grad,
+    weight_grad,
+    y_recv,
+    send,
+    recv,
+    local,
+):
+    group = Group()
+    me, core, far, diag = group.me, group.core, group.far, group.diag
+    rows, width = h1.shape
+    half = rows // 2
+    part = width // 4
+    links = Links(send, recv)
+    peers = [group.at(core), group.at(far)]
+    if exchange:
+        z, y = group.dp // 2, lax.rem(group.dp, 2)
+        order = z_order(z)
+        y_peer = (2 * z + 1 - y, me)
+        peers.append(y_peer)
+    else:
+        order, y = [0, 1, 2, 3], 0
+
+    def block_at(t):
+        found = jnp.int32(order[3])
+        for i in range(3):
+            found = jnp.where(t == i, order[i], found)
+        return found
+
+    loads = [
+        pltpu.make_async_copy(src, dst, local.at[i])
+        for i, (src, dst) in enumerate(
+            [(gate_w, wg), (up_w, wu), (cot_full, cot), (down_w, wd)]
+        )
+    ]
+    for load in loads:
+        load.start()
+    normed[block_rows(me, rows), :] = normed_own[...]
+    greet(peers)
+    gather = Gather(links, group, normed, rows, 2)
+    gather.start()
+    scatter = Scatter(links, group, tx, rx, rows, 2)
+    scatter_ff = Scatter(links, group, tx_ff, rx_ff, rows, 1)
+
+    def pair(ref, first, second):
+        return jnp.concatenate(
+            [
+                ref[pl.ds(pl.multiple_of(first, 128), half), :],
+                ref[pl.ds(pl.multiple_of(second, 128), half), :],
+            ],
+            axis=0,
+        )
+
+    def unit(first, second):
+        block = pair(normed, first, second)
+        gate[...] = contract_cols(block, wg[...])
+        up[...] = contract_cols(block, wu[...])
+        back[...] = contract_cols(pair(cot, first, second), wd[...])
+
+        def act(i, carry):
+            at = pl.ds(pl.multiple_of(i * 16, 16), 16)
+            start = jnp.where(i < half // 16, first, second - half)
+            to = pl.ds(pl.multiple_of(start + i * 16, 16), 16)
+            v, u, g = gate[at, :], up[at, :], back[at, :]
+            square = v * v
+            t = jnp.tanh(GELU_SLOPE * v * (1.0 + GELU_CUBE * square))
+            lift = 0.5 * (1.0 + t)
+            value = v * lift
+            slope = lift + 0.5 * v * (1.0 - t * t) * (
+                GELU_SLOPE * (1.0 + 3.0 * GELU_CUBE * square)
+            )
+            hidden[to, :] = (value * u).astype(bf16)
+            gate_act[to, :] = (g * u * slope).astype(bf16)
+            up_act[to, :] = (g * value).astype(bf16)
+            return carry
+
+        lax.fori_loop(0, rows // 16, act, 0)
+
+    def terms(first, second):
+        return mm(pair(gate_act, first, second), wg[...]) + mm(
+            pair(up_act, first, second), wu[...]
+        )
+
+    def weight_blocks(left, right, store):
+        def one(t, carry):
+            block = block_at(t)
+            store(
+                t,
+                block,
+                contract_rows(
+                    left[:, pl.ds(pl.multiple_of(block * part, 128), part)], right[...]
+                ).astype(bf16),
+            )
+            return carry
+
+        lax.fori_loop(0, 4, one, 0)
+
+    loads[0].wait()
+    loads[1].wait()
+    loads[2].wait()
+    loads[3].wait()
+    unit(me * rows, me * rows + half)
+    gather.near.wait_recv()
+    unit(core * rows, core * rows + half)
+    gather.forward(0)
+    gather.passed[0].wait_recv()
+    unit(far * rows, diag * rows)
+    both = terms(far * rows, diag * rows)
+    scatter.send_diag(0, both[half:])
+    far_terms[pl.ds(0, half), :] = both[:half]
+    gather.forward(1)
+    own_terms[...] = terms(me * rows, me * rows + half)
+    scatter.send_far(0, far_terms[pl.ds(0, half), :])
+    gather.passed[1].wait_recv()
+    unit(far * rows + half, diag * rows + half)
+
+    def y_copy(t, block):
+        return pltpu.make_async_remote_copy(
+            src_ref=down_grad.at[block, 1 - y],
+            dst_ref=y_recv.at[block],
+            send_sem=send.at[16 + t],
+            recv_sem=recv.at[16 + t],
+            device_id=y_peer,
+            device_id_type=MESH,
+        )
+
+    def store_down(t, block, value):
+        down_grad[block, 0] = value[: part // 2]
+        down_grad[block, 1] = value[part // 2 :]
+        if exchange:
+            y_copy(t, block).start()
+
+    weight_blocks(cot, hidden, store_down)
+    both = terms(far * rows + half, diag * rows + half)
+    scatter.send_diag(1, both[half:])
+    far_terms[pl.ds(half, half), :] = both[:half]
+    scatter.send_near(terms(core * rows, core * rows + half))
+    scatter.send_far(1, far_terms[pl.ds(half, half), :])
+
+    def save(slot, block, to, sem):
+        return pltpu.make_async_copy(weight_grad.at[slot], to.at[block], local.at[sem])
+
+    def store_gate(t, block, value):
+        weight_grad[block, 0] = value[: part // 2]
+        weight_grad[block, 1] = value[part // 2 :]
+        save(block, block, gate_out, 4 + t).start()
+
+    def store_up(t, block, value):
+        save(block, block, gate_out, 4 + t).wait()
+        weight_grad[block, 0] = value[: part // 2]
+        weight_grad[block, 1] = value[part // 2 :]
+        save(block, block, up_out, 8 + t).start()
+
+    weight_blocks(normed, gate_act, store_gate)
+
+    def ff_terms(dev):
+        return mm(hidden[block_rows(dev, rows), :], wd[...])
+
+    scatter_ff.send_diag(0, ff_terms(diag))
+    scatter_ff.send_near(ff_terms(core))
+    scatter_ff.send_far(0, ff_terms(far))
+    weight_blocks(normed, up_act, store_up)
+
+    residual = h1[...]
+    pulled, gain_part = norm_pull(residual, gain[...], scatter.total(own_terms[...]))
+    gain_grad[...] = gain_part
+    grad = cot[block_rows(me, rows), :].astype(f32) + pulled
+    grad_h1[...] = grad
+    grad_attn[...] = grad.astype(bf16)
+    own_terms[...] = ff_terms(me)
+
+    def sum_down(t, carry):
+        block = block_at(t)
+        y_copy(t, block).wait_recv()
+        down_grad[block, y] = (
+            down_grad[block, y].astype(f32) + y_recv[block].astype(f32)
+        ).astype(bf16)
+        pltpu.make_async_copy(
+            down_grad.at[block, y], down_out.at[block], local.at[12 + t]
+        ).start()
+        return carry
+
+    if exchange:
+        lax.fori_loop(0, 4, sum_down, 0)
+    else:
+        save_down = pltpu.make_async_copy(down_grad, down_out, local.at[12])
+        save_down.start()
+
+    output[...] = (h1[...] + scatter_ff.total(own_terms[...])).astype(bf16)
+
+    def finish(t, carry):
+        block = block_at(t)
+        save(block, block, up_out, 8 + t).wait()
+        if exchange:
+            y_copy(t, block).wait_send()
+            pltpu.make_async_copy(
+                down_grad.at[block, y], down_out.at[block], local.at[12 + t]
+            ).wait()
+        return carry
+
+    lax.fori_loop(0, 4, finish, 0)
+    if not exchange:
+        save_down.wait()
+    gather.wait_send()
+    scatter.wait_send()
+    scatter_ff.wait_send()
+
+
+def feed_forward(exchange, normed_own, h1, gain, gate_w, up_w, down_w, cot_full):
+    rows, width = h1.shape
+    length = 4 * rows
+    cols = gate_w.shape[0]
+    part = width // 8
+    shape = jax.ShapeDtypeStruct
+    halves = (4, 2, part, cols)
+    return pl.pallas_call(
+        functools.partial(feed_kernel, exchange),
+        out_shape=(
+            shape((rows, width), bf16),
+            shape((rows, width), f32),
+            shape((rows, width), bf16),
+            shape((1, width), f32),
+            shape((4, part, cols) if exchange else halves, bf16),
+            shape(halves, bf16),
+            shape(halves, bf16),
+        ),
+        in_specs=[in_vmem()] * 3 + [anywhere()] * 4,
+        out_specs=[in_vmem()] * 4 + [anywhere()] * 3,
+        scratch_shapes=[
+            pltpu.VMEM((length, width), bf16),
+            pltpu.VMEM((length, width), bf16),
+            pltpu.VMEM((cols, width), bf16),
+            pltpu.VMEM((cols, width), bf16),
+            pltpu.VMEM((cols, width), bf16),
+            pltpu.VMEM((rows, cols), f32),
+            pltpu.VMEM((rows, cols), f32),
+            pltpu.VMEM((rows, cols), f32),
+            pltpu.VMEM((length, cols), bf16),
+            pltpu.VMEM((length, cols), bf16),
+            pltpu.VMEM((length, cols), bf16),
+            pltpu.VMEM((rows, width), f32),
+            pltpu.VMEM((rows, width), f32),
+            pltpu.VMEM((3, rows, width), bf16),
+            pltpu.VMEM((3, rows, width), bf16),
+            pltpu.VMEM((3, rows, width), bf16),
+            pltpu.VMEM((3, rows, width), bf16),
+            pltpu.VMEM(halves, bf16),
+            pltpu.VMEM(halves, bf16),
+            pltpu.VMEM((4, part, cols), bf16),
+            pltpu.SemaphoreType.DMA((20,)),
+            pltpu.SemaphoreType.DMA((20,)),
+            pltpu.SemaphoreType.DMA((16,)),
+        ],
+        compiler_params=pltpu.CompilerParams(
+            collective_id=1, has_side_effects=True, vmem_limit_bytes=VMEM_BYTES
+        ),
+    )(normed_own, h1, gain, gate_w, up_w, down_w, cot_full)
+
+
+class Halving:
+    def __init__(self, links, dp, mp, own, y_recv, z_recv):
+        self.own, self.y_recv, self.z_recv = own, y_recv, z_recv
+        z, y = dp // 2, lax.rem(dp, 2)
+        near = z + 1 - 2 * lax.rem(z, 2)
+        across = lax.rem(z + 2, 4)
+        self.y_peer = (2 * z + 1 - y, mp)
+        self.near, self.across = (2 * near + y, mp), (2 * across + y, mp)
+        self.links = links
+        self.z_copies = [None] * 3
+
+    def plan_y(self, sources):
+        self.y_copies = [
+            self.links.copy(src, self.y_recv.at[i], self.y_peer) for i, src in enumerate(sources)
+        ]
+
+    def plan_z(self, first=None, third=None):
+        own, to = self.own, self.z_recv
+        self.z_copies = [
+            self.links.copy(own.at[0] if first is None else first, to.at[0], self.near),
+            self.links.copy(own.at[1], to.at[2], self.across),
+            self.links.copy(own.at[2] if third is None else third, to.at[1], self.near),
+        ]
+
+    def add(self, i, other):
+        self.own[i] = (self.own[i].astype(f32) + other.astype(f32)).astype(bf16)
+
+    def take_y(self, i):
+        self.y_copies[i].wait_recv()
+        self.add(i, self.y_recv[i])
+        if i == 0 or i == 2:
+            self.z_copies[i].start()
+
+    def take_near(self):
+        self.z_copies[0].wait_recv()
+        self.add(1, self.z_recv[0])
+        self.z_copies[1].start()
+
+    def total(self):
+        self.z_copies[2].wait_recv()
+        self.z_copies[1].wait_recv()
+        return self.own[3].astype(f32) + self.z_recv[1].astype(f32) + self.z_recv[2].astype(f32)
+
+    def wait_send(self, with_y=True):
+        for copy in (self.y_copies if with_y else []) + self.z_copies:
+            copy.wait_send()
+
+
+def z_order(z):
+    near = z + 1 - 2 * lax.rem(z, 2)
+    return [lax.rem(near + 2, 4), lax.rem(z + 2, 4), near, z]
+
+
+def back_kernel(
+    exchange,
+    grad_attn_own,
+    tokens,
+    gain,
+    grad_h1,
+    qkv,
+    mixed,
+    lse,
+    w_query,
+    w_key,
+    w_value,
+    w_out,
+    bucket,
+    gain_ff_part,
+    table,
+    first,
+    normed_in,
+    down_in,
+    gate_in,
+    up_in,
+    grad_input,
+    stats_out,
+    attn_out,
+    gate_out,
+    up_out,
+    down_out,
+    grad_attn,
+    normed,
+    strip,
+    strip_grad,
+    key_head,
+    value_head,
+    grad_mixed,
+    query_sum,
+    key_sum,
+    value_sum,
+    grad_qkv,
+    own_terms,
+    tx,
+    rx,
+    down_own,
+    down_z,
+    gate_own,
+    gate_y,
+    gate_z,
+    up_own,
+    up_y,
+    up_z,
+    attn_own,
+    attn_send,
+    attn_y,
+    attn_z,
+    stats,
+    stats_recv,
+    send,
+    recv,
+    local,
+):
+    group = Group()
+    me, core, far, diag = group.me, group.core, group.far, group.diag
+    rows, width = grad_h1.shape
+    half = rows // 2
+    length = 4 * rows
+    part = width // 4
+    heads = table.shape[1]
+    span = 2 * length
+    links = Links(send, recv)
+    dp = group.dp
+    peers = [group.at(core), group.at(far)]
+    copies = []
+
+    def load(src, dst):
+        copy = pltpu.make_async_copy(src, dst, local.at[len(copies)])
+        copies.append(copy)
+        return copy
+
+    save_normed = load(normed_in, normed)
+    save_normed.start()
+    if exchange:
+        z, y = dp // 2, lax.rem(dp, 2)
+        order = z_order(z)
+        sums = [
+            Halving(links, dp, me, own, y_recv, z_recv)
+            for own, y_recv, z_recv in (
+                (down_own, None, down_z),
+                (gate_own, gate_y, gate_z),
+                (up_own, up_y, up_z),
+                (attn_own, attn_y, attn_z),
+            )
+        ]
+        down, gate, up, attn = sums
+        peers += [down.y_peer, down.near, down.across]
+        loads = [load(down_in.at[order[i]], down_own.at[i]) for i in (1, 3)]
+        gate_loads = [load(gate_in.at[order[i], y], gate_own.at[i]) for i in range(4)]
+        up_loads = [load(up_in.at[order[i], y], up_own.at[i]) for i in range(4)]
+        for copy in loads + gate_loads + up_loads:
+            copy.start()
+        down.plan_z(down_in.at[order[0]], down_in.at[order[2]])
+        gate.plan_y([gate_in.at[order[i], 1 - y] for i in range(4)])
+        gate.plan_z()
+        up.plan_y([up_in.at[order[i], 1 - y] for i in range(4)])
+        up.plan_z()
+        attn.plan_y([attn_send.at[i] for i in range(4)])
+        attn.plan_z()
+    else:
+        order = [0, 1, 2, 3]
+    grad_attn[block_rows(me, rows), :] = grad_attn_own[...]
+    greet(peers)
+    gather = Gather(links, group, grad_attn, rows, 2)
+    gather.start()
+    if exchange:
+        for copy in gate.y_copies:
+            copy.start()
+        down.z_copies[0].start()
+        down.z_copies[2].start()
+    scatter = Scatter(links, group, tx, rx, rows, 1)
+    stages = []
+    for i, to in enumerate([group.at(core), group.at(far)] + peers[2:]):
+        stages.append(links.copy(stats.at[i], stats_recv.at[i], to))
+
+    build_strips(strip, bucket, table)
+    strip_grad[...] = jnp.zeros_like(strip_grad)
+    query_sum[...] = jnp.zeros_like(query_sum)
+    key_sum[...] = jnp.zeros_like(key_sum)
+    value_sum[...] = jnp.zeros_like(value_sum)
+
+    def mix_back(dev):
+        at = block_rows(dev, rows)
+        grad_mixed[at, :] = contract_cols(grad_attn[at, :], w_out[...]).astype(bf16)
+
+    mix_back(me)
+    gather.near.wait_recv()
+    mix_back(core)
+
+    def attend_back(dev, h):
+        at = block_rows(dev, rows)
+        seen = visible_pairs(dev, rows, length, first[0])
+        query, grad = qkv[0, at, :], grad_mixed[at, :]
+        lanes = head_lanes(query.shape, h)
+        zero = jnp.zeros_like(query)
+        scores = contract_cols(query, key_head[...])
+        scores = jnp.where(seen, add_bias(scores, strip, h, dev, length), masked_score)
+        probs = jnp.exp(scores - lse[at, h : h + 1])
+        inner = contract_cols(grad, value_head[...])
+        center = jnp.sum(probs * inner, axis=-1, keepdims=True)
+        score_grad = (probs * (inner - center)).astype(bf16)
+        query_sum[at, :] += mm(score_grad, key_head[...])
+        key_sum[...] += contract_rows(score_grad, jnp.where(lanes, query, zero))
+        value_sum[...] += contract_rows(probs.astype(bf16), jnp.where(lanes, grad, zero))
+        count = length // 128
+        for i in range(rows // 128):
+            start = (count - 1 - i) * 128 - dev * rows
+            to = pl.ds(pl.multiple_of(start, 128), length)
+            strip_grad[h, :, to] += score_grad[i * 128 : (i + 1) * 128].astype(f32)
+
+    def head_keys(h):
+        key, value = qkv[1], qkv[2]
+        lanes = head_lanes(key.shape, h)
+        key_head[...] = jnp.where(lanes, key, jnp.zeros_like(key))
+        value_head[...] = jnp.where(lanes, value, jnp.zeros_like(value))
+
+    def take_gate(i):
+        gate_loads[i].wait()
+        gate.take_y(i)
+        if i == 0:
+            up.y_copies[0].start()
+            up.y_copies[1].start()
+        if i == 1:
+            up.y_copies[2].start()
+            up.y_copies[3].start()
+
+    def take_up(i):
+        up_loads[i].wait()
+        up.take_y(i)
+
+    def down_near():
+        loads[0].wait()
+        loads[1].wait()
+        down.take_near()
+
+    def down_total():
+        down_out[...] = down.total()
+
+    def gate_total():
+        gate_out[...] = gate.total()
+
+    def up_total():
+        up_out[...] = up.total()
+
+    head_keys(0)
+    if exchange:
+        take_gate(0)
+    gather.forward(0)
+    gather.forward(1)
+    mix_back(far)
+    for copy in gather.passed:
+        copy.wait_recv()
+    mix_back(diag)
+    between = {
+        (0, 1): [lambda: take_gate(1), down_near],
+        (1, 1): [lambda: take_gate(2)],
+        (2, 0): [down_total],
+        (2, 2): [lambda: take_gate(3), gate.take_near],
+    } if exchange else {}
+    for h in range(heads):
+        if h:
+            head_keys(h)
+        for j, dev in enumerate((diag, far, core, me)):
+            attend_back(dev, h)
+            for step in between.get((h, j), []):
+                step()
+
+    grad_qkv[0] = query_sum[...].astype(bf16)
+    grad_qkv[1] = key_sum[...].astype(bf16)
+    grad_qkv[2] = value_sum[...].astype(bf16)
+
+    def terms(dev):
+        at = block_rows(dev, rows)
+        return (
+            mm(grad_qkv[0, at, :], w_query[...])
+            + mm(grad_qkv[1, at, :], w_key[...])
+            + mm(grad_qkv[2, at, :], w_value[...])
+        )
+
+    scatter.send_diag(0, terms(diag))
+    scatter.send_near(terms(core))
+    scatter.send_far(0, terms(far))
+    own_terms[...] = terms(me)
+    save_normed.wait()
+
+    cols = mixed.shape[1]
+    for i in range(4):
+        at = pl.ds(pl.multiple_of(order[i] * part, 128), part)
+        for m in range(4):
+            if m < 3:
+                block = contract_rows(normed[:, at], grad_qkv[m]).astype(bf16)
+            else:
+                block = contract_rows(grad_attn[:, at], mixed[...]).astype(bf16)
+            if exchange:
+                low, high = block[: part // 2], block[part // 2 :]
+                attn_send[i, m] = jnp.where(y == 0, high, low)
+                attn_own[i, m] = jnp.where(y == 0, low, high)
+            else:
+                attn_out[m, at, :] = block
+        if exchange:
+            attn.y_copies[i].start()
+        if exchange and i == 1:
+            take_up(0)
+
+    index = bucket[...]
+    lines = []
+    for h in range(heads):
+        fold = strip_grad[h]
+        count = 128
+        while count > 1:
+            count //= 2
+            fold = fold[:count] + pltpu.roll(fold[count:], span - count, 1)
+        lines.append(pltpu.roll(fold, 127, 1))
+    diagonals = jnp.concatenate(lines + [jnp.zeros((8 - heads, span), f32)], axis=0)
+    buckets = table.shape[0]
+    onehot = (lax.broadcasted_iota(jnp.int32, (buckets, span), 0) == index).astype(f32)
+    table_part = lax.dot_general(
+        diagonals, onehot, (((1,), (1,)), ((), ())), precision=highest, preferred_element_type=f32
+    )
+    if exchange:
+        take_up(1)
+
+    value = tokens[...].astype(f32)
+    pulled, gain_part = norm_pull(value, gain[...], scatter.total(own_terms[...]))
+    grad_input[...] = grad_h1[...] + pulled
+    stats[0] = jnp.zeros_like(stats[0])
+    stats[0, 0:1, :] = gain_part
+    stats[0, 1:2, :] = gain_ff_part[...]
+    last = len(stages)
+    for i, stage in enumerate(stages):
+        stage.start()
+        if exchange and i == 2:
+            take_up(2)
+            up.take_near()
+        stage.wait_recv()
+        total = stats[i] + stats_recv[i]
+        if i + 1 < last:
+            stats[i + 1] = total
+            if i == 1:
+                stats[i + 1, 2 : 2 + heads, 0:buckets] = table_part[0:heads]
+        else:
+            stats_out[...] = total
+            if i == 1:
+                stats_out[2 : 2 + heads, 0:buckets] = table_part[0:heads]
+    if exchange:
+        gate_total()
+        take_up(3)
+        for i in range(3):
+            attn.take_y(i)
+        attn.take_near()
+        attn.take_y(3)
+        up_total()
+        attn_out[...] = attn.total()
+        down.wait_send(with_y=False)
+        gate.wait_send()
+        up.wait_send()
+        attn.wait_send()
+    gather.wait_send()
+    scatter.wait_send()
+    for stage in stages:
+        stage.wait_send()
+
+
+def attention_backward(
+    exchange, grad_attn, tokens, gain, grad_h1, qkv, mixed, lse, w_query, w_key, w_value, w_out, bucket, gain_ff_part,
+    table, first, normed, down_in, gate_in, up_in,
+):
+    rows, width = grad_h1.shape
+    length = 4 * rows
+    cols = w_query.shape[0]
+    ff = down_in.shape[-1]
+    heads = table.shape[1]
+    part = width // 8
+    shape = jax.ShapeDtypeStruct
+    small = (1,) if not exchange else None
+    scratch = [
+        pltpu.VMEM((length, width), bf16),
+        pltpu.VMEM((length, width), bf16),
+        pltpu.VMEM((heads, 128, 2 * length), f32),
+        pltpu.VMEM((heads, 128, 2 * length), f32),
+        pltpu.VMEM((length, cols), bf16),
+        pltpu.VMEM((length, cols), bf16),
+        pltpu.VMEM((length, cols), bf16),
+        pltpu.VMEM((length, cols), f32),
+        pltpu.VMEM((length, cols), f32),
+        pltpu.VMEM((length, cols), f32),
+        pltpu.VMEM((3, length, cols), bf16),
+        pltpu.VMEM((rows, width), f32),
+        pltpu.VMEM((3, rows, width), bf16),
+        pltpu.VMEM((3, rows, width), bf16),
+    ]
+    for count in (4, 3, 4, 4, 3, 4, 4, 3):
+        scratch.append(pltpu.VMEM((count, part, ff) if exchange else (8, 128), bf16))
+    for count in (4, 4, 4, 3):
+        scratch.append(pltpu.VMEM((count, 4, part, cols) if exchange else (8, 128), bf16))
+    stages = 5 if exchange else 2
+    scratch += [
+        pltpu.VMEM((stages, 8, width), f32),
+        pltpu.VMEM((stages, 8, width), f32),
+        pltpu.SemaphoreType.DMA((40,)),
+        pltpu.SemaphoreType.DMA((40,)),
+        pltpu.SemaphoreType.DMA((12,)),
+    ]
+    ff_out = shape((part, ff) if exchange else (8, 128), f32)
+    return pl.pallas_call(
+        functools.partial(back_kernel, exchange),
+        out_shape=(
+            shape((rows, width), f32),
+            shape((8, width), f32),
+            shape((4, part, cols), f32) if exchange else shape((4, width, cols), bf16),
+            ff_out,
+            ff_out,
+            ff_out,
+        ),
+        in_specs=[in_vmem()] * 13 + [in_smem()] * 2 + [anywhere()] * 4,
+        out_specs=[in_vmem()] * 6,
+        scratch_shapes=scratch,
+        compiler_params=pltpu.CompilerParams(
+            collective_id=2, has_side_effects=True, vmem_limit_bytes=VMEM_BYTES
+        ),
+    )(
+        grad_attn, tokens, gain, grad_h1, qkv, mixed, lse, w_query, w_key, w_value, w_out, bucket, gain_ff_part,
+        table, first, normed, down_in, gate_in, up_in,
+    )
 
 
 def shards(
@@ -394,154 +1133,44 @@
     first_length,
     offset_bucket,
 ):
-    inputs = tokens.astype(jnp.float32)
     n_dp = lax.axis_size("dp")
+    exchange = n_dp == 8
+    buckets, heads = bias_table.shape
+    width = tokens.shape[1]
     bucket = jnp.pad(offset_bucket, (0, 1), constant_values=-1)[None, :]
-    qkv, mixed, lse, residual, normed_ff_part, normed, cot_full = attention_forward(
-        n_dp, tokens, gain_attn[None], gain_ff[None], w_query, w_key, w_value, bucket, bias_table,
-        first_length, w_out, cotangent)
-    normed_ff = lax.all_gather(normed_ff_part, "mp", axis=0, tiled=True)
-    length = normed.shape[0]
-    heads = w_query.shape[1] // DH
-    query_all, key_all, value_all = qkv[0], qkv[1], qkv[2]
-    key_heads = key_all.reshape(length, heads, DH)
-    value_heads = value_all.reshape(length, heads, DH)
-    places = jnp.arange(length, dtype=jnp.int32)
-    row_side = (places >= first_length[0]).astype(jnp.int32)
-    onehot = (
-        offset_bucket[:, None] == jnp.arange(bias_table.shape[0], dtype=jnp.int32)[None, :]
-    ).astype(jnp.float32)
-    bias_rows = lax.dot_general(
-        bias_table,
-        onehot,
-        (((0,), (1,)), ((), ())),
-        precision=highest,
-        preferred_element_type=jnp.float32,
+    gain_first, gain_second = gain_attn[None], gain_ff[None]
+    turned = [w_query.T, w_key.T, w_value.T]
+    qkv, mixed, lse, h1, normed_ff, normed, cot_full = attention_forward(
+        n_dp, tokens, gain_first, gain_second, *turned, bucket, bias_table, first_length, w_out, cotangent
     )
-    block = min(512, length)
-    count = length // block
-    starts = jnp.arange(count, dtype=jnp.int32) * block
-    query_blocks = query_all.reshape(count, block, heads, DH)
-
-    def block_scores(query_block, start):
-        bias_block = skew_bias(bias_rows, start, block, length)
-        block_side = lax.dynamic_slice_in_dim(row_side, start, block)
-        visible = block_side[:, None] == row_side[None, :]
-        scores = (
-            jnp.einsum("qhd,khd->hqk", query_block, key_heads, preferred_element_type=jnp.float32)
-            + bias_block
-        )
-        return jnp.where(visible[None], scores, masked_score)
-
-    log_totals = lse[:, :heads].reshape(count, block, heads).transpose(0, 2, 1)
-    gate_val = jnp.dot(normed_ff, w_gate, preferred_element_type=jnp.float32)
-    up_val = jnp.dot(normed_ff, w_up, preferred_element_type=jnp.float32)
-    hidden = gated(gate_val, up_val).astype(jnp.bfloat16)
-    ff_terms = jnp.dot(hidden, w_down, preferred_element_type=jnp.float32)
-    ff_part = lax.psum_scatter(
-        ff_terms.astype(jnp.bfloat16), "mp", scatter_dimension=0, tiled=True
-    ).astype(jnp.float32)
-    output = (residual + ff_part).astype(jnp.bfloat16)
-    grad_down_t = contract_rows(cot_full, hidden)
-    grad_hidden = contract_cols(cot_full, w_down)
-    _, gated_pull = jax.vjp(gated, gate_val, up_val)
-    grad_gate_act, grad_up_act = gated_pull(grad_hidden)
-    grad_gate_act = grad_gate_act.astype(jnp.bfloat16)
-    grad_up_act = grad_up_act.astype(jnp.bfloat16)
-    grad_gate = contract_rows(normed_ff, grad_gate_act)
-    grad_up = contract_rows(normed_ff, grad_up_act)
-    normed_ff_terms = contract_cols(grad_gate_act, w_gate) + contract_cols(grad_up_act, w_up)
-    grad_normed_ff = lax.psum_scatter(normed_ff_terms, "mp", scatter_dimension=0, tiled=True)
-    _, norm_ff_pull = jax.vjp(normalize, residual, gain_ff)
-    residual_grad, gain_ff_grad = norm_ff_pull(grad_normed_ff)
-    residual_grad = cotangent.astype(jnp.float32) + residual_grad
-    attn_grad = lax.all_gather(residual_grad.astype(jnp.bfloat16), "mp", axis=0, tiled=True)
-    grad_out_t = contract_rows(attn_grad, mixed)
-    grad_mixed = (
-        contract_cols(attn_grad, w_out).astype(jnp.bfloat16).reshape(count, block, heads, DH)
+    output, grad_h1, grad_attn, gain_ff_part, down, gate, up = feed_forward(
+        exchange, normed_ff, h1, gain_second, w_gate.T, w_up.T, w_down, cot_full
     )
-    span = length + block - 1
-
-    def backward_block(carry, items):
-        key_acc, value_acc, bias_acc = carry
-        query_block, grad_block, lse_block, start = items
-        scores = block_scores(query_block, start)
-        probs = jnp.exp(scores - lse_block[..., None])
-        probs_low = probs.astype(jnp.bfloat16)
-        value_acc = value_acc + jnp.einsum(
-            "hqk,qhd->khd", probs_low, grad_block, preferred_element_type=jnp.float32
-        )
-        inner = jnp.einsum(
-            "qhd,khd->hqk", grad_block, value_heads, preferred_element_type=jnp.float32
-        )
-        center = jnp.sum(probs * inner, axis=-1, keepdims=True)
-        score_grad = (probs * (inner - center)).astype(jnp.bfloat16)
-        query_grad = jnp.einsum(
-            "hqk,khd->qhd", score_grad, key_heads, preferred_element_type=jnp.float32
-        ).astype(jnp.bfloat16)
-        key_acc = key_acc + jnp.einsum(
-            "hqk,qhd->khd", score_grad, query_block, preferred_element_type=jnp.float32
-        )
-        diagonal_sums = unskew_sum(score_grad.astype(jnp.float32), block, length)
-        begin = length - block - start
-        current = lax.dynamic_slice_in_dim(bias_acc, begin, span, 1)
-        bias_acc = lax.dynamic_update_slice_in_dim(bias_acc, current + diagonal_sums, begin, 1)
-        return ((key_acc, value_acc, bias_acc), query_grad)
-
-    empty_heads = jnp.zeros((length, heads, DH), jnp.float32)
-    empty_bias = jnp.zeros((heads, 2 * length - 1), jnp.float32)
-    carried, query_grads = lax.scan(
-        backward_block,
-        (empty_heads, empty_heads, empty_bias),
-        (query_blocks, grad_mixed, log_totals, starts),
+    grad_input, stats, attn, gate_sum, up_sum, down_sum = attention_backward(
+        exchange, grad_attn, tokens, gain_first, grad_h1, qkv, mixed, lse, *turned, w_out, bucket, gain_ff_part,
+        bias_table, first_length, normed, down, gate, up,
     )
-    key_grads, value_grads, offset_grads = carried
-    grad_q = query_grads.reshape(length, heads * DH)
-    grad_k = key_grads.astype(jnp.bfloat16).reshape(length, heads * DH)
-    grad_v = value_grads.astype(jnp.bfloat16).reshape(length, heads * DH)
-    grad_query = contract_rows(normed, grad_q)
-    grad_key = contract_rows(normed, grad_k)
-    grad_value = contract_rows(normed, grad_v)
-    normed_terms = (
-        contract_cols(grad_q, w_query)
-        + contract_cols(grad_k, w_key)
-        + contract_cols(grad_v, w_value)
-    )
-    grad_normed = lax.psum_scatter(normed_terms, "mp", scatter_dimension=0, tiled=True)
-    _, norm_pull = jax.vjp(normalize, inputs, gain_attn)
-    input_grad, gain_attn_grad = norm_pull(grad_normed)
-    grad_input = residual_grad + input_grad
-    table_grad = lax.dot_general(
-        onehot,
-        offset_grads,
-        (((0,), (1,)), ((), ())),
-        precision=highest,
-        preferred_element_type=jnp.float32,
-    )
-    grad_table = lax.psum(table_grad, "dp")
-    grad_gain_attn, grad_gain_ff = lax.psum((gain_attn_grad, gain_ff_grad), ("dp", "mp"))
-    sum_query, sum_key, sum_value, sum_out, sum_gate, sum_up, sum_down = (
-        lax.psum_scatter(grad_query, "dp", scatter_dimension=0, tiled=True),
-        lax.psum_scatter(grad_key, "dp", scatter_dimension=0, tiled=True),
-        lax.psum_scatter(grad_value, "dp", scatter_dimension=0, tiled=True),
-        lax.psum_scatter(grad_out_t, "dp", scatter_dimension=0, tiled=True),
-        lax.psum_scatter(grad_gate, "dp", scatter_dimension=0, tiled=True),
-        lax.psum_scatter(grad_up, "dp", scatter_dimension=0, tiled=True),
-        lax.psum_scatter(grad_down_t, "dp", scatter_dimension=0, tiled=True),
-    )
+    if not exchange:
+        def scatter(value):
+            value = value.reshape(width, -1).astype(f32)
+            return lax.psum_scatter(value, "dp", scatter_dimension=0, tiled=True)
+
+        stats = lax.psum(stats, "dp")
+        gate_sum, up_sum, down_sum = scatter(gate), scatter(up), scatter(down)
+        attn = [scatter(attn[i]) for i in range(4)]
     return (
         output,
         grad_input,
-        grad_gain_attn,
-        sum_query,
-        sum_key,
-        sum_value,
-        sum_out.T,
-        grad_table,
-        grad_gain_ff,
-        sum_gate,
-        sum_up,
-        sum_down.T,
+        stats[0],
+        attn[0],
+        attn[1],
+        attn[2],
+        attn[3].T,
+        stats[2 : 2 + heads, :buckets].T,
+        stats[1],
+        gate_sum,
+        up_sum,
+        down_sum.T,
     )
 
 

time: 1460 us -> 295 us (0.20); the launches traced: 1440 us -> 291 us
  waiting for transfers between devices: 648 us -> 0 us
  local copies, waits for them, and re-layouts: 459 us -> 15.7 us
  Pallas kernels: 61.3 us -> 274 us
  matrix products: 117 us -> 0 us
  blocking collectives: 58.8 us -> 0 us
  other arithmetic: 38.3 us -> 0 us
  loops' own time: 36.1 us -> 0 us
    reduce_scatter x10 -> x0, waiting for transfers between devices: 608 us -> none  [the longest x1 121 us: shards(): lax.psum_scatter(grad_gate, 'dp', scatter_dimension=0, tiled=True)]
    pallas_call x0 -> x2, Pallas kernels: none -> 213 us  [the longest x1 146 us: attention_backward(): pl.pallas_call(functools.partial(back_kernel, exchange), out_shape=(shape...]
    rev x4 -> x0, local copies, waits for them, and re-layouts: 189 us -> none  [the longest x2 97 us: skew_bias(): return tiled[:, ::-1, :length]]
    while x39 -> x0, local copies, waits for them, and re-layouts: 125 us -> none
    dot_general x29 -> x0, matrix products: 117 us -> none  [the longest x7 43.3 us: contract_rows(): lax.dot_general(left, right, (((0,), (0,)), ((), ())), preferred_element_...]
    reshape x6 -> x0, local copies, waits for them, and re-layouts: 61.4 us -> none  [the longest x2 31.1 us: unskew_sum(): return padded[:, :block * span].reshape(heads, block, span).sum(axis=1)]
    psum x2 -> x0, blocking collectives: 58.8 us -> none  [the longest x1 37.2 us: shards(): lax.psum((gain_attn_grad, gain_ff_grad), ('dp', 'mp'))]
    all_gather x2 -> x0, waiting for transfers between devices: 40.1 us -> none  [the longest x1 27.3 us: shards(): normed_ff = lax.all_gather(normed_ff_part, 'mp', axis=0, tiled=True)]
  transfers between devices with their start and end apart: 12 -> 0, of which waited for: 9 -> 0; matrix products, arithmetic and copies ran while one was open for 39% -> 0% of each run, Pallas kernels for 0% -> 0%
where the time goes in v2:
time: 295 us; the launch traced here: 291 us
  Pallas kernels  274 us (93%)
  local copies, waits for them, and re-layouts  15.7 us (5%)
    pallas_call x1, Pallas kernels, attention_backward(): pl.pallas_call(functools.partial(back_kernel, exchange), out_shape=(shape...  146 us
    pallas_call x1, Pallas kernels, feed_forward(): pl.pallas_call(functools.partial(feed_kernel, exchange), out_shape=(shape...  67 us
    pallas_call x1, Pallas kernels, attention_forward(): pl.pallas_call(functools.partial(attend_kernel, 4 if n_dp == 8 else 1), o...  61.2 us
    unnamed x17, local copies, waits for them, and re-layouts  6.84 us

profile of v2, /device:TPU:0, one launch (start us, length us, event | category | flops | bytes accessed | tf_op | source)
XLA Modules:
  0.0 291.1 jit_solution(1611879599473621677)
XLA Ops:
  1.3 1.3 broadcast_in_dim.9.gain_attn.gain
  2.6 1.3 broadcast_in_dim.10.gain_ff.gain
  3.9 1.3 pad.4
  5.2 1.4 copy.26.table
  6.5 61.2 %shard_map.229 = (bf16[3,1024,192]{2,1,0:T(8,128)(2,1)}, bf16[1024,192]{1,0:T(8,128)(2,1)}, f32[1024,128]{1,0:T(8,128)}, f32[256,1536]{1,0:T(8,128)}, bf16[256,1...) custom-call(bf16[256,1536]{1,0:T(8,128)(2,1)} %tokens.3, ...), custom_call_target="tpu_custom_call" | custom-call | tf_op jit(solution)/shard_map/pallas_call | solution.py:325
  67.7 67.0 %shard_map.230 = (bf16[256,1536]{1,0:T(8,128)(2,1)}, f32[256,1536]{1,0:T(8,128)}, bf16[256,1536]{1,0:T(8,128)(2,1)}, f32[1,1536]{1,0:T(1,128)}, bf16[4,192,992]{...) custom-call(bf16[256,1536]{1,0:T(8,128)(2,1)} %get-tuple-element.32.normed_own, ...), custom_call_target="tpu_custom_call" | custom-call | tf_op jit(solution)/shard_map/pallas_call | solution.py:651
  134.7 0.0 copy-start.1
  134.7 145.6 %shard_map.231 = (f32[256,1536]{1,0:T(8,128)}, f32[8,1536]{1,0:T(8,128)}, f32[4,192,192]{2,1,0:T(8,128)}, f32[192,992]{1,0:T(8,128)}, f32[192,992]{1,0:T(8,128)}, /*index=5*/f32[192,992]{1,0:T(8,128)}) custom-call(bf16[256,1536]{1,0:T(8,128)(2,1)} %get-tuple-element.36.grad_attn_own, bf16[256,1536]{1,0:T(8,128)(2,1)} %tokens.3, ...), custom_call_target="tpu_custom_call" | custom-call | tf_op jit(solution)/shard_map/pallas_call | solution.py:1098
  280.4 0.0 copy-start
  280.4 1.4 slice_bitcast_fusion.4
  281.8 1.5 slice_reduce_fusion
  283.3 0.0 copy-start.4
  283.3 2.1 slice_bitcast_fusion
  285.4 0.8 copy.28
  286.2 0.0 copy-done.1
  286.2 0.0 copy-start.3
  286.2 0.9 copy.35
  287.0 0.0 copy-done
  287.1 0.0 copy-start.2
  287.1 1.1 copy.36
  288.2 0.0 copy-done.4
  288.2 0.9 copy.37
  289.1 0.0 copy-done.3
  289.1 0.9 copy.38
  290.0 0.0 copy-done.2
  290.0 0.9 copy.39
Async XLA Ops:
  134.7 151.4 %copy-start.1 = (bf16[256,1536]{1,0:T(8,128)(2,1)S(1)}, bf16[256,1536]{1,0:T(8,128)(2,1)}, u32[]{:S(2)}) copy-start(bf16[256,1536]{1,0:T(8,128)(2,1)} %get-tuple-element.82) | copy-start | bytes 2359300
  280.4 6.7 %copy-start = (f32[256,1536]{1,0:T(8,128)S(1)}, f32[256,1536]{1,0:T(8,128)}, u32[]{:S(2)}) copy-start(f32[256,1536]{1,0:T(8,128)} %get-tuple-element.83) | copy-start | bytes 4718596
  283.3 4.9 %copy-start.4 = (f32[192,992]{1,0:T(8,128)S(1)}, f32[192,992]{1,0:T(8,128)}, u32[]{:S(2)}) copy-start(f32[192,992]{1,0:T(8,128)} %get-tuple-element.91) | copy-start | bytes 2285572
  286.2 2.9 %copy-start.3 = (f32[192,992]{1,0:T(8,128)S(1)}, f32[192,992]{1,0:T(8,128)}, u32[]{:S(2)}) copy-start(f32[192,992]{1,0:T(8,128)} %get-tuple-element.92) | copy-start | bytes 2285572
  287.1 2.9 %copy-start.2 = (f32[192,992]{1,0:T(8,128)S(1)}, f32[192,992]{1,0:T(8,128)}, u32[]{:S(2)}) copy-start(f32[192,992]{1,0:T(8,128)} %get-tuple-element.51) | copy-start | bytes 2285572

commit v3 on v2

v3 whole, which is shorter than its diff:
```python
import functools

import jax
import jax.numpy as jnp
from jax import lax
from jax.experimental import pallas as pl
from jax.experimental.pallas import tpu as pltpu
from jax.sharding import PartitionSpec as P

MESH = pl.DeviceIdType.MESH
DH = 64
epsilon = 1e-06
masked_score = -1000000000.0
highest = lax.Precision.HIGHEST
bf16 = jnp.bfloat16
f32 = jnp.float32
VMEM_BYTES = 62 * 2**20


def mm(left, right):
    return jnp.dot(left, right, preferred_element_type=f32)


def contract_rows(left, right):
    return lax.dot_general(left, right, (((0,), (0,)), ((), ())), preferred_element_type=f32)


def contract_cols(left, right):
    return lax.dot_general(left, right, (((1,), (1,)), ((), ())), preferred_element_type=f32)


def rms(values):
    return values * lax.rsqrt(jnp.mean(values * values, axis=-1, keepdims=True) + epsilon)


class Links:
    def __init__(self, send, recv):
        self.send, self.recv, self.used = send, recv, 0

    def copy(self, src, dst, to):
        at = self.used
        self.used += 1
        return pltpu.make_async_remote_copy(
            src_ref=src,
            dst_ref=dst,
            send_sem=self.send.at[at],
            recv_sem=self.recv.at[at],
            device_id=to,
            device_id_type=MESH,
        )


class Group:
    def __init__(self):
        self.dp, self.me = lax.axis_index("dp"), lax.axis_index("mp")
        self.core = self.me + 1 - 2 * lax.rem(self.me, 2)
        self.far = lax.rem(self.me + 2, 4)
        self.diag = 3 - self.me

    def at(self, mp):
        return (self.dp, mp)


def greet(peers):
    barrier = pltpu.get_barrier_semaphore()
    for peer in peers:
        pl.semaphore_signal(barrier, inc=1, device_id=peer, device_id_type=MESH)
    pl.semaphore_wait(barrier, len(peers))


def block_rows(dev, rows, start=0, size=None):
    return pl.ds(pl.multiple_of(dev * rows + start, 16), rows if size is None else size)


class Gather:
    def __init__(self, links, group, full, rows, chunks, source=None):
        size = rows // chunks
        own = block_rows(group.me, rows)
        self.near = links.copy(full.at[own] if source is None else source, full.at[own], group.at(group.core))
        self.far, self.passed = [], []
        for i in range(chunks):
            mine = block_rows(group.me, rows, i * size, size)
            theirs = block_rows(group.far, rows, i * size, size)
            src = full.at[mine] if source is None else source.at[pl.ds(i * size, size)]
            self.far.append(links.copy(src, full.at[mine], group.at(group.far)))
            self.passed.append(links.copy(full.at[theirs], full.at[theirs], group.at(group.core)))

    def start(self):
        self.near.start()
        for copy in self.far:
            copy.start()

    def forward(self, i):
        self.far[i].wait_recv()
        self.passed[i].start()

    def wait_send(self):
        self.near.wait_send()
        for copy in self.far + self.passed:
            copy.wait_send()


def pack_small(gain_attn, gain_ff, offset_bucket, table):
    width = offset_bucket.shape[0] + 1

    def row(values, fill=0.0):
        values = values.astype(f32).reshape(-1, values.shape[-1])
        return jnp.pad(values, ((0, 0), (0, width - values.shape[1])), constant_values=fill)

    return jnp.concatenate([row(gain_attn), row(gain_ff), row(offset_bucket, -1.0), row(table.T)])


def build_strips(strip, small, buckets):
    index = small[2:3, :]
    heads, _, width = strip.shape
    for h in range(heads):
        row = jnp.zeros(index.shape, f32)
        for b in range(buckets):
            row = jnp.where(index == float(b), small[3 + h : 4 + h, b : b + 1], row)
        strip[h] = pltpu.roll(
            jnp.broadcast_to(row, (128, width)), width - 127, 1, stride=1, stride_axis=0
        )


def add_bias(scores, strip, h, dev, length):
    parts = []
    count = length // 128
    for i in range(scores.shape[0] // 128):
        first = (count - 1 - i) * 128 - dev * scores.shape[0]
        parts.append(
            scores[i * 128 : (i + 1) * 128]
            + strip[h, :, pl.ds(pl.multiple_of(first, 128), length)]
        )
    return jnp.concatenate(parts, axis=0)


def visible_pairs(dev, rows, length, first):
    query = lax.broadcasted_iota(jnp.int32, (rows, length), 0) + dev * rows >= first
    key = lax.broadcasted_iota(jnp.int32, (rows, length), 1) >= first
    return query == key


def head_lanes(shape, h):
    lane = lax.broadcasted_iota(jnp.int32, shape, len(shape) - 1)
    return (lane >= h * DH) & (lane < (h + 1) * DH)


def norm_pull(values, gain, grad):
    inverse = lax.rsqrt(jnp.mean(values * values, axis=-1, keepdims=True) + epsilon)
    scaled = grad * gain
    along = jnp.mean(values * scaled, axis=-1, keepdims=True)
    gain_grad = jnp.sum(grad * values * inverse, axis=0, keepdims=True)
    return inverse * scaled - values * (along * inverse * inverse * inverse), gain_grad


class Scatter:
    def __init__(self, links, group, tx, rx, rows, parts):
        self.tx, self.rx, self.size = tx, rx, rows // parts
        core, far = group.at(group.core), group.at(group.far)
        self.near = links.copy(tx.at[2], rx.at[2], core)
        self.diag, self.far = [], []
        for i in range(parts):
            at = pl.ds(i * self.size, self.size)
            self.diag.append(links.copy(tx.at[0, at], rx.at[0, at], core))
            self.far.append(links.copy(tx.at[1, at], rx.at[1, at], far))

    def send_diag(self, i, terms):
        self.tx[0, pl.ds(i * self.size, self.size), :] = terms.astype(bf16)
        self.diag[i].start()

    def send_near(self, terms):
        self.tx[2] = terms.astype(bf16)
        self.near.start()

    def send_far(self, i, terms):
        at = pl.ds(i * self.size, self.size)
        self.diag[i].wait_recv()
        self.tx[1, at, :] = (terms + self.rx[0, at, :].astype(f32)).astype(bf16)
        self.far[i].start()

    def total(self, own):
        self.near.wait_recv()
        for copy in self.far:
            copy.wait_recv()
        return own + self.rx[2].astype(f32) + self.rx[1].astype(f32)

    def wait_send(self):
        for copy in [self.near] + self.diag + self.far:
            copy.wait_send()


GELU_SLOPE = 0.7978845608028654
GELU_CUBE = 0.044715


def z_order(z):
    near = z + 1 - 2 * lax.rem(z, 2)
    return [lax.rem(near + 2, 4), lax.rem(z + 2, 4), near, z]


def forward_kernel(
    exchange,
    buckets,
    tokens,
    small,
    first,
    w_query,
    w_key,
    w_value,
    w_out,
    gate_w,
    up_w,
    down_w,
    cot_in,
    qkv,
    mixed,
    lse,
    output,
    grad_h1,
    grad_attn,
    gain_grad,
    normed_out,
    down_out,
    gate_out,
    up_out,
    normed,
    cot,
    wg,
    wu,
    wd,
    strip,
    hidden,
    gate_act,
    up_act,
    mixed_all,
    mixed_sum,
    far_terms,
    own_terms,
    tx,
    rx,
    tx_ff,
    rx_ff,
    down_grad,
    gate_grad,
    up_grad,
    y_recv,
    z_recv,
    send,
    recv,
    local,
):
    group = Group()
    me, core, far, diag = group.me, group.core, group.far, group.diag
    rows, width = tokens.shape
    half = rows // 2
    length = 4 * rows
    heads = strip.shape[0]
    depth = w_out.shape[0]
    ff = wg.shape[0]
    part = width // 4
    gain_attn, gain_ff = small[0:1, 0:width], small[1:2, 0:width]
    links = Links(send, recv)
    peers = [group.at(core), group.at(far), group.at(diag)]
    z_peers = []
    if exchange:
        z, y = group.dp // 2, lax.rem(group.dp, 2)
        order = z_order(z)
        y_peer = (2 * z + 1 - y, me)
        near_peer = (2 * order[2] + y, me)
        z_peers = [(2 * lax.rem(z + t, 4) + y, me) for t in (1, 2, 3)]
        peers += [y_peer] + z_peers
    else:
        order, y = [0, 1, 2, 3], 0

    def block_at(t):
        found = jnp.int32(order[3])
        for i in range(3):
            found = jnp.where(t == i, order[i], found)
        return found

    started = []

    def load(src, dst):
        copy = pltpu.make_async_copy(src, dst, local.at[len(started)])
        started.append(copy)
        return copy

    def depth_rows(i):
        return pl.ds(pl.multiple_of(i * depth, 16), depth)

    own = block_rows(me, rows)
    out_own = load(w_out, wu.at[depth_rows(me)])
    out_own.start()
    proj_loads = [load(w, wg.at[depth_rows(i)]) for i, w in enumerate((w_query, w_key, w_value))]
    for copy in proj_loads:
        copy.start()
    cot_own = load(cot_in, cot.at[own])
    cot_own.start()
    down_load = load(down_w, wd)
    down_load.start()
    greet(peers)

    x = tokens[...].astype(f32)
    normed[own, :] = (rms(x) * gain_attn).astype(bf16)
    gather = Gather(links, group, normed, rows, 2)
    gather.start()
    out_own.wait()
    parts = 4 if exchange else 1
    piece = depth // parts

    def out_rows(dev):
        start = dev * depth + (z * piece if exchange else 0)
        return pl.ds(pl.multiple_of(start, 16), piece)

    out_near = links.copy(wu.at[depth_rows(me)], wu.at[depth_rows(me)], group.at(core))
    out_far = links.copy(wu.at[out_rows(me)], wu.at[out_rows(me)], group.at(far))
    out_near.start()
    out_z = [links.copy(wu.at[out_rows(far)], wu.at[out_rows(far)], peer) for peer in z_peers]
    out_pass = links.copy(wu.at[depth_rows(far)], wu.at[depth_rows(far)], group.at(core))
    cot_gather = Gather(links, group, cot, rows, 4, source=cot_in)
    cot_gather.near.start()
    mixed_near = links.copy(mixed.at[block_rows(core, rows)], mixed_all.at[me], group.at(core))
    mixed_far = links.copy(mixed.at[block_rows(far, rows)], mixed_all.at[me], group.at(far))
    mixed_diag = links.copy(mixed.at[block_rows(diag, rows)], mixed_all.at[me], group.at(diag))

    build_strips(strip, small, buckets)
    for copy in proj_loads:
        copy.wait()

    def project(dev):
        at = block_rows(dev, rows)
        block = normed[at, :]
        for i in range(3):
            qkv[i, at, :] = contract_cols(block, wg[i * depth : (i + 1) * depth, :]).astype(bf16)

    project(me)
    gather.near.wait_recv()
    project(core)
    gather.forward(0)
    gather.forward(1)
    out_far.start()
    cot_gather.far[0].start()
    project(far)
    for copy in gather.passed:
        copy.wait_recv()
    normed_save = load(normed, normed_out)
    normed_save.start()
    project(diag)
    gate_load = load(gate_w, wg)
    gate_load.start()

    def attend(dev):
        at = block_rows(dev, rows)
        seen = visible_pairs(dev, rows, length, first[0])
        mixed_sum[...] = jnp.zeros_like(mixed_sum)
        lse[at, :] = jnp.zeros((rows, 128), f32)

        def one_head(h, carry):
            query = qkv[0, at, :]
            lanes = head_lanes(query.shape, h)
            scores = contract_cols(jnp.where(lanes, query, jnp.zeros_like(query)), qkv[1])
            scores = jnp.where(seen, add_bias(scores, strip, h, dev, length), masked_score)
            top = jnp.max(scores, axis=-1, keepdims=True)
            expo = jnp.exp(scores - top)
            total = jnp.sum(expo, axis=-1, keepdims=True)
            weights = (expo * (1.0 / total)).astype(bf16)
            mixed_sum[...] = jnp.where(lanes, mm(weights, qkv[2]), mixed_sum[...])
            lane = lax.broadcasted_iota(jnp.int32, (rows, 128), 1)
            lse[at, :] = jnp.where(lane == h, top + jnp.log(total), lse[at, :])
            return carry

        lax.fori_loop(0, heads, one_head, 0)
        mixed[at, :] = mixed_sum[...].astype(bf16)

    attend(far)
    gather.wait_send()
    normed_save.wait()
    mixed_far.start()
    cot_gather.far[1].start()
    out_far.wait_recv()
    for copy in out_z:
        copy.start()
    attend(diag)
    mixed_diag.start()
    cot_gather.far[2].start()
    attend(core)
    mixed_near.start()
    for copy in out_z:
        copy.wait_recv()
    out_pass.start()
    cot_gather.forward(0)
    attend(me)
    mixed_all[me] = mixed[own, :]
    out_near.wait_recv()
    attn = mm(mixed_all[me], wu[depth_rows(me), :])
    mixed_near.wait_recv()
    attn = attn + mm(mixed_all[core], wu[depth_rows(core), :])
    mixed_far.wait_recv()
    attn = attn + mm(mixed_all[far], wu[depth_rows(far), :])
    mixed_diag.wait_recv()
    out_pass.wait_recv()
    attn = attn + mm(mixed_all[diag], wu[depth_rows(diag), :])
    residual = x + attn
    grad_h1[...] = residual
    normed[own, :] = (rms(residual) * gain_ff).astype(bf16)
    second = Gather(links, group, normed, rows, 2)
    second.near.start()
    second.far[0].start()
    cot_gather.far[3].start()
    second.far[1].start()
    for copy in [out_near, out_far, out_pass] + out_z:
        copy.wait_send()
    up_load = load(up_w, wu)
    up_load.start()

    scatter = Scatter(links, group, tx, rx, rows, 2)
    scatter_ff = Scatter(links, group, tx_ff, rx_ff, rows, 1)

    def pair(ref, start, after):
        return jnp.concatenate(
            [
                ref[pl.ds(pl.multiple_of(start, 128), half), :],
                ref[pl.ds(pl.multiple_of(after, 128), half), :],
            ],
            axis=0,
        )

    def keep(i, value):
        strip[i, :, 0:ff] = value[:half]
        strip[i, :, length : length + ff] = value[half:]

    def unit(start, after):
        block = pair(normed, start, after)
        keep(0, contract_cols(block, wg[...]))
        keep(1, contract_cols(block, wu[...]))
        keep(2, contract_cols(pair(cot, start, after), wd[...]))
        for offset, lane in ((start, 0), (after, length)):

            def act(i, carry):
                at = pl.ds(pl.multiple_of(i * 16, 16), 16)
                to = pl.ds(pl.multiple_of(offset + i * 16, 16), 16)
                v, u, g = (strip[k, at, lane : lane + ff] for k in range(3))
                square = v * v
                t = jnp.tanh(GELU_SLOPE * v * (1.0 + GELU_CUBE * square))
                lift = 0.5 * (1.0 + t)
                value = v * lift
                slope = lift + 0.5 * v * (1.0 - t * t) * (
                    GELU_SLOPE * (1.0 + 3.0 * GELU_CUBE * square)
                )
                hidden[to, :] = (value * u).astype(bf16)
                gate_act[to, :] = (g * u * slope).astype(bf16)
                up_act[to, :] = (g * value).astype(bf16)
                return carry

            lax.fori_loop(0, half // 16, act, 0)

    def terms(start, after):
        return mm(pair(gate_act, start, after), wg[...]) + mm(
            pair(up_act, start, after), wu[...]
        )

    def weight_blocks(left, right, store):
        def one(t, carry):
            at = pl.ds(pl.multiple_of(block_at(t) * part, 128), part)
            value = contract_rows(left[:, at], right[...]).astype(bf16)
            store(t, value[: part // 2], value[part // 2 :])
            return carry

        lax.fori_loop(0, 4, one, 0)

    cot_own.wait()
    down_load.wait()
    gate_load.wait()
    up_load.wait()
    unit(me * rows, me * rows + half)
    cot_gather.forward(1)
    cot_gather.near.wait_recv()
    second.near.wait_recv()
    unit(core * rows, core * rows + half)
    second.forward(0)
    second.passed[0].wait_recv()
    for i in (0, 1):
        cot_gather.passed[i].wait_recv()
    unit(far * rows, diag * rows)
    both = terms(far * rows, diag * rows)
    scatter.send_diag(0, both[half:])
    far_terms[pl.ds(0, half), :] = both[:half]
    cot_gather.forward(2)
    cot_gather.forward(3)
    scatter.send_far(0, far_terms[pl.ds(0, half), :])
    second.forward(1)
    own_terms[...] = terms(me * rows, me * rows + half)
    for i in (2, 3):
        cot_gather.passed[i].wait_recv()
    second.passed[1].wait_recv()
    unit(far * rows + half, diag * rows + half)

    base = links.used
    links.used += 8

    def y_copy(t):
        return pltpu.make_async_remote_copy(
            src_ref=down_grad.at[t, 1 - y],
            dst_ref=y_recv.at[t],
            send_sem=send.at[base + t],
            recv_sem=recv.at[base + t],
            device_id=y_peer,
            device_id_type=MESH,
        )

    def z_copy(i, side):
        return pltpu.make_async_remote_copy(
            src_ref=gate_grad.at[2 * i, side],
            dst_ref=z_recv.at[i, side],
            send_sem=send.at[base + 4 + 2 * i + side],
            recv_sem=recv.at[base + 4 + 2 * i + side],
            device_id=near_peer,
            device_id_type=MESH,
        )

    spots = len(started)

    def save(src, dst, at):
        return pltpu.make_async_copy(src, dst, local.at[spots + at])

    def store_down(t, low, high):
        down_grad[t, 0] = low
        down_grad[t, 1] = high
        if exchange:
            y_copy(t).start()
        else:
            save(down_grad.at[t], down_out.at[t], t).start()

    def store_gate(t, low, high):
        gate_grad[t, 0] = low
        gate_grad[t, 1] = high
        if exchange:

            @pl.when(lax.rem(t, 2) == 0)
            def _():
                z_copy(t // 2, 0).start()
                z_copy(t // 2, 1).start()
        else:
            save(gate_grad.at[t], gate_out.at[t], 4 + t).start()

    def store_up(t, low, high):
        slot = lax.rem(t, 2)

        @pl.when(t >= 2)
        def _():
            save(up_grad.at[slot], up_out.at[t - 2], 8 + t - 2).wait()

        up_grad[slot, 0] = low
        up_grad[slot, 1] = high
        save(up_grad.at[slot], up_out.at[t], 8 + t).start()

    weight_blocks(cot, hidden, store_down)
    both = terms(far * rows + half, diag * rows + half)
    scatter.send_diag(1, both[half:])
    far_terms[pl.ds(half, half), :] = both[:half]
    scatter.send_near(terms(core * rows, core * rows + half))
    scatter.send_far(1, far_terms[pl.ds(half, half), :])
    weight_blocks(normed, gate_act, store_gate)

    def ff_terms(dev):
        return mm(hidden[block_rows(dev, rows), :], wd[...])

    scatter_ff.send_diag(0, ff_terms(diag))
    scatter_ff.send_near(ff_terms(core))
    scatter_ff.send_far(0, ff_terms(far))
    weight_blocks(normed, up_act, store_up)

    residual = grad_h1[...]
    pulled, gain_part = norm_pull(residual, gain_ff, scatter.total(own_terms[...]))
    gain_grad[...] = gain_part
    grad = cot[own, :].astype(f32) + pulled
    own_terms[...] = residual + ff_terms(me)
    grad_h1[...] = grad
    grad_attn[...] = grad.astype(bf16)

    if exchange:

        def sum_down(t, carry):
            y_copy(t).wait_recv()
            down_grad[t, y] = (
                down_grad[t, y].astype(f32) + y_recv[t].astype(f32)
            ).astype(bf16)
            save(down_grad.at[t, y], down_out.at[t], t).start()
            return carry

        lax.fori_loop(0, 4, sum_down, 0)
        for i in range(2):
            for side in range(2):
                z_copy(i, side).wait_recv()
                kept = gate_grad.at[2 * i + 1, side]
                kept[...] = (kept[...].astype(f32) + z_recv[i, side].astype(f32)).astype(bf16)
                save(kept, gate_out.at[i, side], 4 + 2 * i + side).start()

    output[...] = scatter_ff.total(own_terms[...]).astype(bf16)

    for t in range(4):
        if exchange:
            save(down_grad.at[t, y], down_out.at[t], t).wait()
            save(gate_grad.at[t // 2 * 2 + 1, t % 2], gate_out.at[t // 2, t % 2], 4 + t).wait()
            y_copy(t).wait_send()
            z_copy(t // 2, t % 2).wait_send()
        else:
            save(down_grad.at[t], down_out.at[t], t).wait()
            save(gate_grad.at[t], gate_out.at[t], 4 + t).wait()
        if t >= 2:
            save(up_grad.at[t % 2], up_out.at[t], 8 + t).wait()
    for copy in (mixed_near, mixed_far, mixed_diag):
        copy.wait_send()
    cot_gather.wait_send()
    second.wait_send()
    scatter.wait_send()
    scatter_ff.wait_send()


def in_vmem():
    return pl.BlockSpec(memory_space=pltpu.VMEM)


def anywhere():
    return pl.BlockSpec(memory_space=pl.ANY)


def in_smem():
    return pl.BlockSpec(memory_space=pltpu.SMEM)


def forward(exchange, table_shape, tokens, small, first, w_query, w_key, w_value, w_out, gate_w, up_w, down_w, cot):
    rows, width = tokens.shape
    length = 4 * rows
    cols = w_query.shape[0]
    ff = gate_w.shape[0]
    buckets, heads = table_shape
    part = width // 8
    shape = jax.ShapeDtypeStruct
    halves = (4, 2, part, ff)
    return pl.pallas_call(
        functools.partial(forward_kernel, exchange, buckets),
        out_shape=(
            shape((3, length, cols), bf16),
            shape((length, cols), bf16),
            shape((length, 128), f32),
            shape((rows, width), bf16),
            shape((rows, width), f32),
            shape((rows, width), bf16),
            shape((1, width), f32),
            shape((length, width), bf16),
            shape((4, part, ff) if exchange else halves, bf16),
            shape((2, 2, part, ff) if exchange else halves, bf16),
            shape(halves, bf16),
        ),
        in_specs=[in_vmem()] * 2 + [in_smem()] + [anywhere()] * 8,
        out_specs=[in_vmem()] * 7 + [anywhere()] * 4,
        scratch_shapes=[
            pltpu.VMEM((length, width), bf16),
            pltpu.VMEM((length, width), bf16),
            pltpu.VMEM((ff, width), bf16),
            pltpu.VMEM((ff, width), bf16),
            pltpu.VMEM((ff, width), bf16),
            pltpu.VMEM((heads, 128, 2 * length), f32),
            pltpu.VMEM((length, ff), bf16),
            pltpu.VMEM((length, ff), bf16),
            pltpu.VMEM((length, ff), bf16),
            pltpu.VMEM((4, rows, cols), bf16),
            pltpu.VMEM((rows, cols), f32),
            pltpu.VMEM((rows, width), f32),
            pltpu.VMEM((rows, width), f32),
            pltpu.VMEM((3, rows, width), bf16),
            pltpu.VMEM((3, rows, width), bf16),
            pltpu.VMEM((3, rows, width), bf16),
            pltpu.VMEM((3, rows, width), bf16),
            pltpu.VMEM(halves, bf16),
            pltpu.VMEM(halves, bf16),
            pltpu.VMEM((2, 2, part, ff), bf16),
            pltpu.VMEM((4, part, ff) if exchange else (8, 128), bf16),
            pltpu.VMEM((2, 2, part, ff) if exchange else (8, 128), bf16),
            pltpu.SemaphoreType.DMA((48,)),
            pltpu.SemaphoreType.DMA((48,)),
            pltpu.SemaphoreType.DMA((24,)),
        ],
        compiler_params=pltpu.CompilerParams(
            collective_id=0, has_side_effects=True, vmem_limit_bytes=VMEM_BYTES
        ),
    )(tokens, small, first, w_query, w_key, w_value, w_out, gate_w, up_w, down_w, cot)


class Halving:
    def __init__(self, links, dp, mp, own, y_recv, z_recv):
        self.own, self.y_recv, self.z_recv = own, y_recv, z_recv
        z, y = dp // 2, lax.rem(dp, 2)
        near = z + 1 - 2 * lax.rem(z, 2)
        across = lax.rem(z + 2, 4)
        self.y_peer = (2 * z + 1 - y, mp)
        self.near, self.across = (2 * near + y, mp), (2 * across + y, mp)
        self.links = links
        self.z_copies = [None] * 3

    def plan_y(self, sources):
        self.y_copies = [
            self.links.copy(src, self.y_recv.at[i], self.y_peer) for i, src in enumerate(sources)
        ]

    def plan_z(self, first=None, third=None):
        own, to = self.own, self.z_recv
        self.z_copies = [
            self.links.copy(own.at[0] if first is None else first, to.at[0], self.near),
            self.links.copy(own.at[1], to.at[2], self.across),
            self.links.copy(own.at[2] if third is None else third, to.at[1], self.near),
        ]

    def add(self, i, other):
        self.own[i] = (self.own[i].astype(f32) + other.astype(f32)).astype(bf16)

    def take_y(self, i):
        self.y_copies[i].wait_recv()
        self.add(i, self.y_recv[i])
        if i == 0 or i == 2:
            self.z_copies[i].start()

    def take_near(self):
        self.z_copies[0].wait_recv()
        self.add(1, self.z_recv[0])
        self.z_copies[1].start()

    def total(self):
        self.z_copies[2].wait_recv()
        self.z_copies[1].wait_recv()
        return self.own[3].astype(f32) + self.z_recv[1].astype(f32) + self.z_recv[2].astype(f32)

    def wait_send(self, with_y=True):
        for copy in (self.y_copies if with_y else []) + self.z_copies:
            copy.wait_send()


class LastHalvings:
    def __init__(self, links, halving, own, y_recv, z_recv, sources):
        self.own, self.y_recv, self.z_recv = own, y_recv, z_recv
        self.y_copies = [
            links.copy(src, y_recv.at[i], halving.y_peer) for i, src in enumerate(sources)
        ]
        self.across = links.copy(own.at[0], z_recv.at[0], halving.across)

    def take_y(self, i):
        self.y_copies[i].wait_recv()
        self.own[i] = (self.own[i].astype(f32) + self.y_recv[i].astype(f32)).astype(bf16)
        if i == 0:
            self.across.start()

    def total(self):
        self.across.wait_recv()
        return self.own[1].astype(f32) + self.z_recv[0].astype(f32)

    def wait_send(self):
        for copy in self.y_copies + [self.across]:
            copy.wait_send()


def back_kernel(
    exchange,
    buckets,
    grad_attn_own,
    tokens,
    small,
    grad_h1,
    qkv,
    mixed,
    lse,
    w_query,
    w_key,
    w_value,
    w_out,
    gain_ff_part,
    first,
    normed_in,
    down_in,
    gate_in,
    up_in,
    grad_input,
    stats_out,
    attn_out,
    gate_out,
    up_out,
    down_out,
    grad_attn,
    normed,
    strip,
    strip_grad,
    key_head,
    value_head,
    grad_mixed,
    query_sum,
    key_sum,
    value_sum,
    grad_qkv,
    own_terms,
    tx,
    rx,
    down_own,
    down_z,
    gate_own,
    gate_y,
    gate_z,
    up_own,
    up_y,
    up_z,
    attn_own,
    attn_send,
    attn_y,
    attn_z,
    stats,
    stats_recv,
    send,
    recv,
    local,
):
    group = Group()
    me, core, far, diag = group.me, group.core, group.far, group.diag
    rows, width = grad_h1.shape
    half = rows // 2
    length = 4 * rows
    part = width // 4
    heads = strip.shape[0]
    span = 2 * length
    links = Links(send, recv)
    dp = group.dp
    peers = [group.at(core), group.at(far)]
    copies = []

    def load(src, dst):
        copy = pltpu.make_async_copy(src, dst, local.at[len(copies)])
        copies.append(copy)
        return copy

    save_normed = load(normed_in, normed)
    save_normed.start()
    if exchange:
        z, y = dp // 2, lax.rem(dp, 2)
        order = z_order(z)
        sums = [
            Halving(links, dp, me, own, y_recv, z_recv)
            for own, y_recv, z_recv in (
                (down_own, None, down_z),
                (up_own, up_y, up_z),
                (attn_own, attn_y, attn_z),
            )
        ]
        down, up, attn = sums
        peers += [down.y_peer, down.near, down.across]
        loads = [load(down_in.at[i], down_own.at[i]) for i in (1, 3)]
        gate_loads = [load(gate_in.at[i, y], gate_own.at[i]) for i in range(2)]
        up_loads = [load(up_in.at[i, y], up_own.at[i]) for i in range(4)]
        for copy in loads + gate_loads + up_loads:
            copy.start()
        down.plan_z(down_in.at[0], down_in.at[2])
        gate = LastHalvings(links, down, gate_own, gate_y, gate_z, [gate_in.at[i, 1 - y] for i in range(2)])
        up.plan_y([up_in.at[i, 1 - y] for i in range(4)])
        up.plan_z()
        attn.plan_y([attn_send.at[i] for i in range(4)])
        attn.plan_z()
    else:
        order = [0, 1, 2, 3]
    grad_attn[block_rows(me, rows), :] = grad_attn_own[...]
    greet(peers)
    gather = Gather(links, group, grad_attn, rows, 2)
    gather.start()
    if exchange:
        for copy in gate.y_copies:
            copy.start()
        down.z_copies[0].start()
        down.z_copies[2].start()
    scatter = Scatter(links, group, tx, rx, rows, 1)
    stages = []
    for i, to in enumerate([group.at(core), group.at(far)] + peers[2:]):
        stages.append(links.copy(stats.at[i], stats_recv.at[i], to))

    build_strips(strip, small, buckets)
    strip_grad[...] = jnp.zeros_like(strip_grad)
    query_sum[...] = jnp.zeros_like(query_sum)
    key_sum[...] = jnp.zeros_like(key_sum)
    value_sum[...] = jnp.zeros_like(value_sum)

    def mix_back(dev):
        at = block_rows(dev, rows)
        grad_mixed[at, :] = contract_cols(grad_attn[at, :], w_out[...]).astype(bf16)

    mix_back(me)
    gather.near.wait_recv()
    mix_back(core)

    def attend_back(dev, h):
        at = block_rows(dev, rows)
        seen = visible_pairs(dev, rows, length, first[0])
        query, grad = qkv[0, at, :], grad_mixed[at, :]
        lanes = head_lanes(query.shape, h)
        zero = jnp.zeros_like(query)
        scores = contract_cols(query, key_head[...])
        scores = jnp.where(seen, add_bias(scores, strip, h, dev, length), masked_score)
        probs = jnp.exp(scores - lse[at, h : h + 1])
        inner = contract_cols(grad, value_head[...])
        center = jnp.sum(probs * inner, axis=-1, keepdims=True)
        score_grad = (probs * (inner - center)).astype(bf16)
        query_sum[at, :] += mm(score_grad, key_head[...])
        key_sum[...] += contract_rows(score_grad, jnp.where(lanes, query, zero))
        value_sum[...] += contract_rows(probs.astype(bf16), jnp.where(lanes, grad, zero))
        count = length // 128
        for i in range(rows // 128):
            start = (count - 1 - i) * 128 - dev * rows
            to = pl.ds(pl.multiple_of(start, 128), length)
            strip_grad[h, :, to] += score_grad[i * 128 : (i + 1) * 128].astype(f32)

    def head_keys(h):
        key, value = qkv[1], qkv[2]
        lanes = head_lanes(key.shape, h)
        key_head[...] = jnp.where(lanes, key, jnp.zeros_like(key))
        value_head[...] = jnp.where(lanes, value, jnp.zeros_like(value))

    def take_gate(i):
        gate_loads[i].wait()
        gate.take_y(i)
        if i == 0:
            up.y_copies[0].start()
            up.y_copies[1].start()
        if i == 1:
            up.y_copies[2].start()
            up.y_copies[3].start()

    def take_up(i):
        up_loads[i].wait()
        up.take_y(i)

    def down_near():
        loads[0].wait()
        loads[1].wait()
        down.take_near()

    def down_total():
        down_out[...] = down.total()

    def gate_total():
        gate_out[...] = gate.total()

    def up_total():
        up_out[...] = up.total()

    head_keys(0)
    if exchange:
        take_gate(0)
    gather.forward(0)
    gather.forward(1)
    mix_back(far)
    for copy in gather.passed:
        copy.wait_recv()
    mix_back(diag)
    between = {
        (0, 1): [lambda: take_gate(1), down_near],
        (1, 1): [lambda: take_up(0)],
        (2, 0): [down_total],
        (2, 1): [lambda: take_up(1)],
        (2, 3): [gate_total],
    } if exchange else {}
    for h in range(heads):
        if h:
            head_keys(h)
        for j, dev in enumerate((diag, far, core, me)):
            attend_back(dev, h)
            for step in between.get((h, j), []):
                step()

    grad_qkv[0] = query_sum[...].astype(bf16)
    grad_qkv[1] = key_sum[...].astype(bf16)
    grad_qkv[2] = value_sum[...].astype(bf16)

    def terms(dev):
        at = block_rows(dev, rows)
        return (
            mm(grad_qkv[0, at, :], w_query[...])
            + mm(grad_qkv[1, at, :], w_key[...])
            + mm(grad_qkv[2, at, :], w_value[...])
        )

    scatter.send_diag(0, terms(diag))
    scatter.send_near(terms(core))
    scatter.send_far(0, terms(far))
    own_terms[...] = terms(me)
    save_normed.wait()

    cols = mixed.shape[1]
    for i in range(4):
        at = pl.ds(pl.multiple_of(order[i] * part, 128), part)
        for m in range(4):
            if m < 3:
                block = contract_rows(normed[:, at], grad_qkv[m]).astype(bf16)
            else:
                block = contract_rows(grad_attn[:, at], mixed[...]).astype(bf16)
            if exchange:
                low, high = block[: part // 2], block[part // 2 :]
                lanes = slice(m * cols, (m + 1) * cols)
                attn_send[i, :, lanes] = jnp.where(y == 0, high, low)
                attn_own[i, :, lanes] = jnp.where(y == 0, low, high)
            else:
                attn_out[m, at, :] = block
        if exchange:
            attn.y_copies[i].start()

    index = small[2:3, :]
    lines = []
    for h in range(heads):
        fold = strip_grad[h]
        count = 128
        while count > 1:
            count //= 2
            fold = fold[:count] + pltpu.roll(fold[count:], span - count, 1)
        lines.append(pltpu.roll(fold, 127, 1))
    diagonals = jnp.concatenate(lines + [jnp.zeros((8 - heads, span), f32)], axis=0)
    onehot = (lax.broadcasted_iota(jnp.int32, (buckets, span), 0).astype(f32) == index).astype(f32)
    table_part = lax.dot_general(
        diagonals, onehot, (((1,), (1,)), ((), ())), precision=highest, preferred_element_type=f32
    )
    if exchange:
        take_up(2)
        up.take_near()

    value = tokens[...].astype(f32)
    pulled, gain_part = norm_pull(value, small[0:1, 0:width], scatter.total(own_terms[...]))
    grad_input[...] = grad_h1[...] + pulled
    stats[0] = jnp.zeros_like(stats[0])
    stats[0, 0:1, :] = gain_part
    stats[0, 1:2, :] = gain_ff_part[...]
    stages[0].start()

    def next_stage(i):
        stages[i].wait_recv()
        total = stats[i] + stats_recv[i]
        to = stats.at[i + 1] if i + 1 < len(stages) else stats_out
        to[...] = total
        if i == 1:
            to[2 : 2 + heads, 0:buckets] = table_part[0:heads]
        if i + 1 < len(stages):
            stages[i + 1].start()

    next_stage(0)
    if exchange:
        take_up(3)
    next_stage(1)
    if exchange:
        attn.take_y(0)
        attn.take_y(1)
        attn.take_near()
        attn.take_y(2)
        up_total()
        attn.take_y(3)
        next_stage(2)
        next_stage(3)
        total = attn.total()
        for m in range(3):
            attn_out[m] = total[:, m * cols : (m + 1) * cols]
        attn_out[3] = total[:, 3 * cols :].T
        next_stage(4)
        down.wait_send(with_y=False)
        gate.wait_send()
        up.wait_send()
        attn.wait_send()
    gather.wait_send()
    scatter.wait_send()
    for stage in stages:
        stage.wait_send()


def attention_backward(
    exchange, table_shape, grad_attn, tokens, small, grad_h1, qkv, mixed, lse, w_query, w_key, w_value, w_out,
    gain_ff_part, first, normed, down_in, gate_in, up_in,
):
    rows, width = grad_h1.shape
    length = 4 * rows
    cols = w_query.shape[0]
    ff = down_in.shape[-1]
    buckets, heads = table_shape
    part = width // 8
    shape = jax.ShapeDtypeStruct
    scratch = [
        pltpu.VMEM((length, width), bf16),
        pltpu.VMEM((length, width), bf16),
        pltpu.VMEM((heads, 128, 2 * length), f32),
        pltpu.VMEM((heads, 128, 2 * length), f32),
        pltpu.VMEM((length, cols), bf16),
        pltpu.VMEM((length, cols), bf16),
        pltpu.VMEM((length, cols), bf16),
        pltpu.VMEM((length, cols), f32),
        pltpu.VMEM((length, cols), f32),
        pltpu.VMEM((length, cols), f32),
        pltpu.VMEM((3, length, cols), bf16),
        pltpu.VMEM((rows, width), f32),
        pltpu.VMEM((3, rows, width), bf16),
        pltpu.VMEM((3, rows, width), bf16),
    ]
    for count in (4, 3, 2, 2, 1, 4, 4, 3):
        scratch.append(pltpu.VMEM((count, part, ff) if exchange else (8, 128), bf16))
    for count in (4, 4, 4, 3):
        scratch.append(pltpu.VMEM((count, part, 4 * cols) if exchange else (8, 128), bf16))
    stages = 5 if exchange else 2
    scratch += [
        pltpu.VMEM((stages, 8, width), f32),
        pltpu.VMEM((stages, 8, width), f32),
        pltpu.SemaphoreType.DMA((40,)),
        pltpu.SemaphoreType.DMA((40,)),
        pltpu.SemaphoreType.DMA((12,)),
    ]
    ff_out = shape((part, ff) if exchange else (8, 128), f32)
    return pl.pallas_call(
        functools.partial(back_kernel, exchange, buckets),
        out_shape=(
            shape((rows, width), f32),
            shape((8, width), f32),
            shape((4, part, cols), f32) if exchange else shape((4, width, cols), bf16),
            ff_out,
            ff_out,
            ff_out,
        ),
        in_specs=[in_vmem()] * 12 + [in_smem()] + [anywhere()] * 4,
        out_specs=[in_vmem()] * 6,
        scratch_shapes=scratch,
        compiler_params=pltpu.CompilerParams(
            collective_id=1, has_side_effects=True, vmem_limit_bytes=VMEM_BYTES
        ),
    )(
        grad_attn, tokens, small, grad_h1, qkv, mixed, lse, w_query, w_key, w_value, w_out, gain_ff_part, first,
        normed, down_in, gate_in, up_in,
    )


def finish_kernel(heads, *refs):
    ins, outs, (attn_held, *held, load, save) = refs[:7], refs[7:19], refs[19:]
    stats, attn = ins[0], ins[1]
    sources = list(ins[2:]) + [attn.at[i] for i in range(4)]
    slots = held + [attn_held.at[i] for i in range(4)]
    targets = list(outs[4:9]) + list(outs[:4])
    loads = [pltpu.make_async_copy(a, b, load.at[i]) for i, (a, b) in enumerate(zip(sources, slots))]
    saves = [pltpu.make_async_copy(a, b, save.at[i]) for i, (a, b) in enumerate(zip(slots, targets))]
    for copy in loads:
        copy.start()
    gain_attn, gain_ff, table = outs[9:]
    gain_attn[...] = stats[0]
    gain_ff[...] = stats[1]
    table[...] = stats[2 : 2 + heads, 0 : table.shape[1]]
    for before, after in zip(loads, saves):
        before.wait()
        after.start()
    for copy in saves:
        copy.wait()


def finish(table_shape, stats, attn, *whole):
    buckets, heads = table_shape
    shape = jax.ShapeDtypeStruct
    outs = [shape(attn.shape[1:], f32)] * 4 + [shape(v.shape, v.dtype) for v in whole]
    small = [shape(stats.shape[1:], f32)] * 2 + [shape((heads, buckets), f32)]
    return pl.pallas_call(
        functools.partial(finish_kernel, heads),
        out_shape=outs + small,
        in_specs=[in_vmem()] + [anywhere()] * 6,
        out_specs=[anywhere()] * 9 + [in_vmem()] * 3,
        scratch_shapes=[pltpu.VMEM(v.shape, v.dtype) for v in (attn, *whole)]
        + [pltpu.SemaphoreType.DMA((9,))] * 2,
        compiler_params=pltpu.CompilerParams(vmem_limit_bytes=VMEM_BYTES),
    )(stats, attn, *whole)


def shards(
    tokens,
    gain_attn,
    w_query,
    w_key,
    w_value,
    w_out,
    bias_table,
    gain_ff,
    w_gate,
    w_up,
    w_down,
    cotangent,
    first_length,
    offset_bucket,
):
    n_dp = lax.axis_size("dp")
    exchange = n_dp == 8
    buckets, heads = bias_table.shape
    width = tokens.shape[1]
    small = pack_small(gain_attn, gain_ff, offset_bucket, bias_table)
    turned = [w_query.T, w_key.T, w_value.T]
    qkv, mixed, lse, output, grad_h1, grad_attn, gain_ff_part, normed, down, gate, up = forward(
        exchange, bias_table.shape, tokens, small, first_length, *turned, w_out, w_gate.T, w_up.T, w_down, cotangent
    )
    grad_input, stats, attn, gate_sum, up_sum, down_sum = attention_backward(
        exchange, bias_table.shape, grad_attn, tokens, small, grad_h1, qkv, mixed, lse, *turned, w_out, gain_ff_part,
        first_length, normed, down, gate, up,
    )
    if exchange:
        *attn, output, grad_input, gate_sum, up_sum, down_sum, gain_first, gain_second, table = finish(
            bias_table.shape, stats, attn, output, grad_input, gate_sum, up_sum, down_sum
        )
    else:
        def scatter(value):
            value = value.reshape(width, -1).astype(f32)
            return lax.psum_scatter(value, "dp", scatter_dimension=0, tiled=True)

        stats = lax.psum(stats, "dp")
        gate_sum, up_sum, down_sum = scatter(gate), scatter(up), scatter(down)
        attn = [scatter(attn[i]) for i in range(4)]
        attn[3] = attn[3].T
        gain_first, gain_second, table = stats[0], stats[1], stats[2 : 2 + heads, :buckets]
    return (
        output,
        grad_input,
        gain_first,
        attn[0],
        attn[1],
        attn[2],
        attn[3],
        table.T,
        gain_second,
        gate_sum,
        up_sum,
        down_sum.T,
    )


def solution(mesh):
    placed = (
        P(("dp", "mp"), None),
        P(),
        P(None, "mp"),
        P(None, "mp"),
        P(None, "mp"),
        P("mp", None),
        P(None, "mp"),
        P(),
        P(None, "mp"),
        P(None, "mp"),
        P("mp", None),
        P(("dp", "mp"), None),
        P("dp"),
        P(),
    )
    return jax.shard_map(
        shards,
        mesh=mesh,
        in_specs=placed,
        out_specs=(
            P(("dp", "mp"), None),
            P(("dp", "mp"), None),
            P(),
            P("dp", "mp"),
            P("dp", "mp"),
            P("dp", "mp"),
            P("mp", "dp"),
            P(None, "mp"),
            P(),
            P("dp", "mp"),
            P("dp", "mp"),
            P("mp", "dp"),
        ),
        check_vma=False,
    )
```

time: 295 us -> 256 us (0.87)
  Pallas kernels: 274 us -> 247 us
  local copies, waits for them, and re-layouts: 15.7 us -> 1.4 us
    pallas_call x3, Pallas kernels: 274 us -> 247 us  [the longest x1 128 us: forward(): pl.pallas_call(functools.partial(forward_kernel, exchange, buckets), out_...]
    unnamed x17 -> x0, local copies, waits for them, and re-layouts: 6.84 us -> none
    transpose x2 -> x0, local copies, waits for them, and re-layouts: 3.47 us -> none  [the longest x1 2.1 us: shards(): attn[3]]
where the time goes in v3:
time: 256 us; the launch traced here: 252 us
  Pallas kernels  247 us (96%)
    pallas_call x1, Pallas kernels, forward(): pl.pallas_call(functools.partial(forward_kernel, exchange, buckets), out_...  128 us
    pallas_call x1, Pallas kernels, attention_backward(): pl.pallas_call(functools.partial(back_kernel, exchange, buckets), out_sha...  113 us
    pallas_call x1, Pallas kernels, finish(): pl.pallas_call(functools.partial(finish_kernel, heads), out_shape=outs +...  5.71 us

profile of v3, /device:TPU:0, one launch (start us, length us, event | category | flops | bytes accessed | tf_op | source)
XLA Modules:
  0.0 251.9 jit_solution(14111944171625519852)
XLA Ops:
  1.3 0.7 reshape.33
  2.0 0.7 reshape.34
  2.7 0.7 convert_element_type.3
  3.4 1.3 select_maximum_fusion.small
  4.7 128.3 %shard_map.229 = (bf16[3,1024,192]{2,1,0:T(8,128)(2,1)}, bf16[1024,192]{1,0:T(8,128)(2,1)}, f32[1024,128]{1,0:T(8,128)}, bf16[256,1536]{1,0:T(8,128)(2,1)}, f32[...) custom-call(bf16[256,1536]{1,0:T(8,128)(2,1)} %tokens.3, ...), custom_call_target="tpu_custom_call" | custom-call | tf_op jit(solution)/shard_map/pallas_call | solution.py:641
  133.0 112.7 %shard_map.230 = (f32[256,1536]{1,0:T(8,128)}, f32[8,1536]{1,0:T(8,128)}, f32[4,192,192]{2,1,0:T(8,128)}, f32[192,992]{1,0:T(8,128)}, f32[192,992]{1,0:T(8,128)}, /*index=5*/f32[192,992]{1,0:T(8,128)}) custom-call(bf16[256,1536]{1,0:T(8,128)(2,1)} %get-tuple-element.41.grad_attn_own, bf16[256,1536]{1,0:T(8,128)(2,1)} %tokens.3, ...), custom_call_target="tpu_custom_call" | custom-call | tf_op jit(solution)/shard_map/pallas_call | solution.py:1113
  245.8 5.7 %shard_map.231 = (f32[192,192]{1,0:T(8,128)}, f32[192,192]{1,0:T(8,128)}, f32[192,192]{1,0:T(8,128)}, f32[192,192]{1,0:T(8,128)}, bf16[256,1536]{1,0:T(8,128)(2,...) custom-call(f32[8,1536]{1,0:T(8,128)} %get-tuple-element.51.refs_0_,, ...), custom_call_target="tpu_custom_call" | custom-call | tf_op jit(solution)/shard_map/pallas_call | solution.py:1161

commit v4 on v3

--- a/solution.py
+++ b/solution.py
@@ -196,6 +196,15 @@
 def z_order(z):
     near = z + 1 - 2 * lax.rem(z, 2)
     return [lax.rem(near + 2, 4), lax.rem(z + 2, 4), near, z]
+
+
+def line_order(z):
+    return [
+        jnp.where(z < 2, 3, 0),
+        jnp.where(z < 2, 2, 1),
+        jnp.where(z == 0, 1, jnp.where(z == 1, 0, jnp.where(z == 2, 3, 2))),
+        z,
+    ]
 
 
 def forward_kernel(
@@ -215,9 +224,11 @@
     qkv,
     mixed,
     lse,
-    output,
+    ff_far,
+    own_terms,
     grad_h1,
-    grad_attn,
+    grad_mixed,
+    out_grad,
     gain_grad,
     normed_out,
     down_out,
@@ -235,7 +246,6 @@
     mixed_all,
     mixed_sum,
     far_terms,
-    own_terms,
     tx,
     rx,
     tx_ff,
@@ -248,6 +258,7 @@
     send,
     recv,
     local,
+    free,
 ):
     group = Group()
     me, core, far, diag = group.me, group.core, group.far, group.diag
@@ -264,15 +275,15 @@
     z_peers = []
     if exchange:
         z, y = group.dp // 2, lax.rem(group.dp, 2)
-        order = z_order(z)
+        line, order = line_order(z), z_order(z)
         y_peer = (2 * z + 1 - y, me)
         near_peer = (2 * order[2] + y, me)
         z_peers = [(2 * lax.rem(z + t, 4) + y, me) for t in (1, 2, 3)]
         peers += [y_peer] + z_peers
     else:
-        order, y = [0, 1, 2, 3], 0
-
-    def block_at(t):
+        line, order, y = [0, 1, 2, 3], [0, 1, 2, 3], 0
+
+    def place(order, t):
         found = jnp.int32(order[3])
         for i in range(3):
             found = jnp.where(t == i, order[i], found)
@@ -385,6 +396,7 @@
     cot_gather.far[2].start()
     attend(core)
     mixed_near.start()
+    cot_gather.far[3].start()
     for copy in out_z:
         copy.wait_recv()
     out_pass.start()
@@ -405,16 +417,16 @@
     normed[own, :] = (rms(residual) * gain_ff).astype(bf16)
     second = Gather(links, group, normed, rows, 2)
     second.near.start()
-    second.far[0].start()
-    cot_gather.far[3].start()
-    second.far[1].start()
+    for copy in second.far:
+        copy.start()
     for copy in [out_near, out_far, out_pass] + out_z:
         copy.wait_send()
     up_load = load(up_w, wu)
     up_load.start()
 
     scatter = Scatter(links, group, tx, rx, rows, 2)
-    scatter_ff = Scatter(links, group, tx_ff, rx_ff, rows, 1)
+    ff_diag = links.copy(tx_ff.at[0], rx_ff.at[0], group.at(core))
+    ff_near = links.copy(tx_ff.at[1], rx_ff.at[1], group.at(core))
 
     def pair(ref, start, after):
         return jnp.concatenate(
@@ -459,11 +471,14 @@
             pair(up_act, start, after), wu[...]
         )
 
-    def weight_blocks(left, right, store):
+    def weight_block(order, left, right, store, t):
+        at = pl.ds(pl.multiple_of(place(order, t) * part, 128), part)
+        value = contract_rows(left[:, at], right[...]).astype(bf16)
+        store(t, value[: part // 2], value[part // 2 :])
+
+    def weight_blocks(order, left, right, store):
         def one(t, carry):
-            at = pl.ds(pl.multiple_of(block_at(t) * part, 128), part)
-            value = contract_rows(left[:, at], right[...]).astype(bf16)
-            store(t, value[: part // 2], value[part // 2 :])
+            weight_block(order, left, right, store, t)
             return carry
 
         lax.fori_loop(0, 4, one, 0)
@@ -518,7 +533,7 @@
             device_id_type=MESH,
         )
 
-    spots = len(started)
+    spots = len(started) + 1
 
     def save(src, dst, at):
         return pltpu.make_async_copy(src, dst, local.at[spots + at])
@@ -536,8 +551,7 @@
         gate_grad[t, 1] = high
         if exchange:
 
-            @pl.when(lax.rem(t, 2) == 0)
-            def _():
+            if t % 2 == 0:
                 z_copy(t // 2, 0).start()
                 z_copy(t // 2, 1).start()
         else:
@@ -554,30 +568,65 @@
         up_grad[slot, 1] = high
         save(up_grad.at[slot], up_out.at[t], 8 + t).start()
 
-    weight_blocks(cot, hidden, store_down)
+    def down_block(t):
+        weight_block(line, cot, hidden, store_down, t)
+
+    def gate_block(t):
+        weight_block(order, normed, gate_act, store_gate, t)
+
+    down_block(0)
+    gate_block(0)
     both = terms(far * rows + half, diag * rows + half)
     scatter.send_diag(1, both[half:])
     far_terms[pl.ds(half, half), :] = both[:half]
     scatter.send_near(terms(core * rows, core * rows + half))
     scatter.send_far(1, far_terms[pl.ds(half, half), :])
-    weight_blocks(normed, gate_act, store_gate)
+    for block in (1, 2):
+        down_block(block)
+    gate_block(2)
+    down_block(3)
+    cot_gather.wait_send()
+    for peer in (core, far):
+        pl.semaphore_signal(free, inc=1, device_id=group.at(peer), device_id_type=MESH)
+    gate_block(1)
+    gate_block(3)
 
     def ff_terms(dev):
         return mm(hidden[block_rows(dev, rows), :], wd[...])
 
-    scatter_ff.send_diag(0, ff_terms(diag))
-    scatter_ff.send_near(ff_terms(core))
-    scatter_ff.send_far(0, ff_terms(far))
-    weight_blocks(normed, up_act, store_up)
-
+    tx_ff[0] = ff_terms(diag).astype(bf16)
+    ff_diag.start()
+    tx_ff[1] = ff_terms(core).astype(bf16)
+    ff_near.start()
+    own_part = ff_terms(far)
+    ff_diag.wait_recv()
+    ff_far[...] = (own_part + rx_ff[0].astype(f32)).astype(bf16)
     residual = grad_h1[...]
+    own_part = residual + ff_terms(me)
     pulled, gain_part = norm_pull(residual, gain_ff, scatter.total(own_terms[...]))
     gain_grad[...] = gain_part
     grad = cot[own, :].astype(f32) + pulled
-    own_terms[...] = residual + ff_terms(me)
     grad_h1[...] = grad
-    grad_attn[...] = grad.astype(bf16)
-
+    cot[own, :] = grad.astype(bf16)
+    third = Gather(links, group, cot, rows, 2)
+    pl.semaphore_wait(free, 2)
+    third.start()
+    scatter.wait_send()
+    out_again = load(w_out, tx.at[0, 0:depth])
+    out_again.start()
+    ff_near.wait_recv()
+    own_terms[...] = own_part + rx_ff[1].astype(f32)
+
+    def mix_back(dev):
+        at = block_rows(dev, rows)
+        grad_mixed[at, :] = contract_cols(cot[at, :], tx[0, 0:depth, :]).astype(bf16)
+
+    weight_blocks(line, normed, up_act, store_up)
+    out_again.wait()
+    mix_back(me)
+    third.near.wait_recv()
+    mix_back(core)
+    third.forward(0)
     if exchange:
 
         def sum_down(t, carry):
@@ -588,15 +637,26 @@
             save(down_grad.at[t, y], down_out.at[t], t).start()
             return carry
 
-        lax.fori_loop(0, 4, sum_down, 0)
+        lax.fori_loop(0, 3, sum_down, 0)
+    third.forward(1)
+    mix_back(far)
+    for copy in third.passed:
+        copy.wait_recv()
+    mix_back(diag)
+
+    def store_out(t, low, high):
+        out_grad[t, 0] = low
+        out_grad[t, 1] = high
+
+    weight_blocks(line, cot, mixed, store_out)
+    if exchange:
+        sum_down(3, 0)
         for i in range(2):
             for side in range(2):
                 z_copy(i, side).wait_recv()
                 kept = gate_grad.at[2 * i + 1, side]
                 kept[...] = (kept[...].astype(f32) + z_recv[i, side].astype(f32)).astype(bf16)
                 save(kept, gate_out.at[i, side], 4 + 2 * i + side).start()
-
-    output[...] = scatter_ff.total(own_terms[...]).astype(bf16)
 
     for t in range(4):
         if exchange:
@@ -611,10 +671,10 @@
             save(up_grad.at[t % 2], up_out.at[t], 8 + t).wait()
     for copy in (mixed_near, mixed_far, mixed_diag):
         copy.wait_send()
-    cot_gather.wait_send()
     second.wait_send()
-    scatter.wait_send()
-    scatter_ff.wait_send()
+    third.wait_send()
+    ff_diag.wait_send()
+    ff_near.wait_send()
 
 
 def in_vmem():
@@ -646,7 +706,9 @@
             shape((length, 128), f32),
             shape((rows, width), bf16),
             shape((rows, width), f32),
-            shape((rows, width), bf16),
+            shape((rows, width), f32),
+            shape((length, cols), bf16),
+            shape((4, 2, part, cols), bf16),
             shape((1, width), f32),
             shape((length, width), bf16),
             shape((4, part, ff) if exchange else halves, bf16),
@@ -654,7 +716,7 @@
             shape(halves, bf16),
         ),
         in_specs=[in_vmem()] * 2 + [in_smem()] + [anywhere()] * 8,
-        out_specs=[in_vmem()] * 7 + [anywhere()] * 4,
+        out_specs=[in_vmem()] * 9 + [anywhere()] * 4,
         scratch_shapes=[
             pltpu.VMEM((length, width), bf16),
             pltpu.VMEM((length, width), bf16),
@@ -668,19 +730,19 @@
             pltpu.VMEM((4, rows, cols), bf16),
             pltpu.VMEM((rows, cols), f32),
             pltpu.VMEM((rows, width), f32),
-            pltpu.VMEM((rows, width), f32),
             pltpu.VMEM((3, rows, width), bf16),
             pltpu.VMEM((3, rows, width), bf16),
-            pltpu.VMEM((3, rows, width), bf16),
-            pltpu.VMEM((3, rows, width), bf16),
+            pltpu.VMEM((2, rows, width), bf16),
+            pltpu.VMEM((2, rows, width), bf16),
             pltpu.VMEM(halves, bf16),
             pltpu.VMEM(halves, bf16),
             pltpu.VMEM((2, 2, part, ff), bf16),
             pltpu.VMEM((4, part, ff) if exchange else (8, 128), bf16),
             pltpu.VMEM((2, 2, part, ff) if exchange else (8, 128), bf16),
-            pltpu.SemaphoreType.DMA((48,)),
-            pltpu.SemaphoreType.DMA((48,)),
+            pltpu.SemaphoreType.DMA((56,)),
+            pltpu.SemaphoreType.DMA((56,)),
             pltpu.SemaphoreType.DMA((24,)),
+            pltpu.SemaphoreType.REGULAR,
         ],
         compiler_params=pltpu.CompilerParams(
             collective_id=0, has_side_effects=True, vmem_limit_bytes=VMEM_BYTES
@@ -688,81 +750,136 @@
     )(tokens, small, first, w_query, w_key, w_value, w_out, gate_w, up_w, down_w, cot)
 
 
-class Halving:
-    def __init__(self, links, dp, mp, own, y_recv, z_recv):
-        self.own, self.y_recv, self.z_recv = own, y_recv, z_recv
+class Line:
+    def __init__(self, links, dp, mp, own, y_recv, z_recv, sources=()):
         z, y = dp // 2, lax.rem(dp, 2)
         near = z + 1 - 2 * lax.rem(z, 2)
-        across = lax.rem(z + 2, 4)
-        self.y_peer = (2 * z + 1 - y, mp)
-        self.near, self.across = (2 * near + y, mp), (2 * across + y, mp)
-        self.links = links
-        self.z_copies = [None] * 3
-
-    def plan_y(self, sources):
-        self.y_copies = [
-            self.links.copy(src, self.y_recv.at[i], self.y_peer) for i, src in enumerate(sources)
+        self.own, self.y_recv, self.z_recv = own, y_recv, z_recv
+        self.inner = (z == 1) | (z == 2)
+        self.y_peer, self.near, self.across = (2 * z + 1 - y, mp), (2 * near + y, mp), (2 * lax.rem(z + 2, 4) + y, mp)
+        self.middle = (2 * (3 - z) + y, mp)
+        self.y_copies = [links.copy(src, y_recv.at[i], self.y_peer) for i, src in enumerate(sources)]
+        base = links.used
+        links.used += 5
+        forth = jnp.where(self.inner, self.middle[0], self.near[0])
+        step = jnp.where(self.inner, 3, 0)
+        self.copies = [
+            pltpu.make_async_remote_copy(
+                src_ref=own.at[i],
+                dst_ref=z_recv.at[slot],
+                send_sem=links.send.at[base + i],
+                recv_sem=links.recv.at[base + slot],
+                device_id=(to, mp),
+                device_id_type=MESH,
+            )
+            for i, (slot, to) in enumerate(((step, forth), (step + 1, forth), (2, self.near[0])))
         ]
-
-    def plan_z(self, first=None, third=None):
-        own, to = self.own, self.z_recv
-        self.z_copies = [
-            self.links.copy(own.at[0] if first is None else first, to.at[0], self.near),
-            self.links.copy(own.at[1], to.at[2], self.across),
-            self.links.copy(own.at[2] if third is None else third, to.at[1], self.near),
+        self.arrivals = [
+            pltpu.make_async_remote_copy(
+                src_ref=own.at[0],
+                dst_ref=z_recv.at[slot],
+                send_sem=links.send.at[base],
+                recv_sem=links.recv.at[base + slot],
+                device_id=self.near,
+                device_id_type=MESH,
+            )
+            for slot in range(5)
         ]
 
     def add(self, i, other):
         self.own[i] = (self.own[i].astype(f32) + other.astype(f32)).astype(bf16)
+
+    def begin(self, i):
+        @pl.when(jnp.logical_not(self.inner))
+        def _():
+            self.copies[i].start()
 
     def take_y(self, i):
         self.y_copies[i].wait_recv()
         self.add(i, self.y_recv[i])
-        if i == 0 or i == 2:
-            self.z_copies[i].start()
-
-    def take_near(self):
-        self.z_copies[0].wait_recv()
-        self.add(1, self.z_recv[0])
-        self.z_copies[1].start()
-
-    def total(self):
-        self.z_copies[2].wait_recv()
-        self.z_copies[1].wait_recv()
-        return self.own[3].astype(f32) + self.z_recv[1].astype(f32) + self.z_recv[2].astype(f32)
-
-    def wait_send(self, with_y=True):
-        for copy in (self.y_copies if with_y else []) + self.z_copies:
+        if i < 3:
+            self.begin(i)
+
+    def relay(self, i):
+        slot = (0, 1, 3)[i]
+
+        @pl.when(self.inner)
+        def _():
+            self.arrivals[slot].wait_recv()
+            self.add(i, self.z_recv[slot])
+            self.copies[i].start()
+
+    def total(self, out):
+        self.arrivals[2].wait_recv()
+        out[...] = self.own[3].astype(f32) + self.z_recv[2].astype(f32)
+
+        @pl.when(self.inner)
+        def _():
+            self.arrivals[4].wait_recv()
+            out[...] += self.z_recv[4].astype(f32)
+
+    def wait_send(self):
+        for copy in self.y_copies + self.copies:
             copy.wait_send()
 
 
 class LastHalvings:
-    def __init__(self, links, halving, own, y_recv, z_recv, sources):
-        self.own, self.y_recv, self.z_recv = own, y_recv, z_recv
+    def __init__(self, links, line, own, y_recv, z_recv, sources):
+        self.own, self.y_recv, self.z_recv, self.inner = own, y_recv, z_recv, line.inner
         self.y_copies = [
-            links.copy(src, y_recv.at[i], halving.y_peer) for i, src in enumerate(sources)
+            links.copy(src, y_recv.at[i], line.y_peer) for i, src in enumerate(sources)
         ]
-        self.across = links.copy(own.at[0], z_recv.at[0], halving.across)
+        base = links.used
+        links.used += 3
+
+        def copy(i, src, slot, to):
+            return pltpu.make_async_remote_copy(
+                src_ref=src,
+                dst_ref=z_recv.at[slot],
+                send_sem=links.send.at[base + i],
+                recv_sem=links.recv.at[base + slot],
+                device_id=to,
+                device_id_type=MESH,
+            )
+
+        mp = line.near[1]
+        forth = (jnp.where(self.inner, line.middle[0], line.near[0]), mp)
+        self.first = copy(0, own.at[0], jnp.where(self.inner, 1, 0), forth)
+        self.inwards = copy(1, z_recv.at[0], 2, line.middle)
+        self.outwards = copy(2, z_recv.at[1], 2, line.near)
+        self.arrivals = [copy(0, own.at[0], slot, line.near) for slot in range(3)]
 
     def take_y(self, i):
         self.y_copies[i].wait_recv()
         self.own[i] = (self.own[i].astype(f32) + self.y_recv[i].astype(f32)).astype(bf16)
         if i == 0:
-            self.across.start()
+            self.first.start()
+
+    def hand_on(self):
+        @pl.when(self.inner)
+        def _():
+            self.arrivals[1].wait_recv()
+            self.outwards.start()
+            self.arrivals[0].wait_recv()
+            self.inwards.start()
 
     def total(self):
-        self.across.wait_recv()
-        return self.own[1].astype(f32) + self.z_recv[0].astype(f32)
+        self.arrivals[2].wait_recv()
+        return self.own[1].astype(f32) + self.z_recv[2].astype(f32)
 
     def wait_send(self):
-        for copy in self.y_copies + [self.across]:
+        for copy in self.y_copies + [self.first]:
             copy.wait_send()
+
+        @pl.when(self.inner)
+        def _():
+            self.outwards.wait_send()
+            self.inwards.wait_send()
 
 
 def back_kernel(
     exchange,
     buckets,
-    grad_attn_own,
     tokens,
     small,
     grad_h1,
@@ -772,26 +889,28 @@
     w_query,
     w_key,
     w_value,
-    w_out,
+    grad_mixed,
+    out_grad,
     gain_ff_part,
+    ff_base,
     first,
     normed_in,
+    ff_far,
     down_in,
     gate_in,
     up_in,
+    output,
     grad_input,
     stats_out,
     attn_out,
     gate_out,
     up_out,
     down_out,
-    grad_attn,
     normed,
     strip,
     strip_grad,
     key_head,
     value_head,
-    grad_mixed,
     query_sum,
     key_sum,
     value_sum,
@@ -811,6 +930,8 @@
     attn_send,
     attn_y,
     attn_z,
+    attn_sum,
+    ff_recv,
     stats,
     stats_recv,
     send,
@@ -839,42 +960,32 @@
     save_normed.start()
     if exchange:
         z, y = dp // 2, lax.rem(dp, 2)
-        order = z_order(z)
-        sums = [
-            Halving(links, dp, me, own, y_recv, z_recv)
-            for own, y_recv, z_recv in (
-                (down_own, None, down_z),
-                (up_own, up_y, up_z),
-                (attn_own, attn_y, attn_z),
-            )
-        ]
-        down, up, attn = sums
-        peers += [down.y_peer, down.near, down.across]
-        loads = [load(down_in.at[i], down_own.at[i]) for i in (1, 3)]
+        order = line_order(z)
+        down = Line(links, dp, me, down_own, None, down_z)
+        gate = LastHalvings(links, down, gate_own, gate_y, gate_z, [gate_in.at[i, 1 - y] for i in range(2)])
+        up = Line(links, dp, me, up_own, up_y, up_z, [up_in.at[i, 1 - y] for i in range(4)])
+        attn = Line(links, dp, me, attn_own, attn_y, attn_z, [attn_send.at[i] for i in range(4)])
+        peers += [down.y_peer, down.near, down.across, down.middle]
+        loads = [load(down_in.at[i], down_own.at[i]) for i in range(4)]
         gate_loads = [load(gate_in.at[i, y], gate_own.at[i]) for i in range(2)]
         up_loads = [load(up_in.at[i, y], up_own.at[i]) for i in range(4)]
         for copy in loads + gate_loads + up_loads:
             copy.start()
-        down.plan_z(down_in.at[0], down_in.at[2])
-        gate = LastHalvings(links, down, gate_own, gate_y, gate_z, [gate_in.at[i, 1 - y] for i in range(2)])
-        up.plan_y([up_in.at[i, 1 - y] for i in range(4)])
-        up.plan_z()
-        attn.plan_y([attn_send.at[i] for i in range(4)])
-        attn.plan_z()
     else:
         order = [0, 1, 2, 3]
-    grad_attn[block_rows(me, rows), :] = grad_attn_own[...]
     greet(peers)
-    gather = Gather(links, group, grad_attn, rows, 2)
-    gather.start()
     if exchange:
-        for copy in gate.y_copies:
+        for copy in gate.y_copies + up.y_copies:
             copy.start()
-        down.z_copies[0].start()
-        down.z_copies[2].start()
+        for i in range(4):
+            loads[i].wait()
+            if i < 3:
+                down.begin(i)
     scatter = Scatter(links, group, tx, rx, rows, 1)
+    ff_copy = links.copy(ff_far, ff_recv, group.at(far))
+    ff_copy.start()
     stages = []
-    for i, to in enumerate([group.at(core), group.at(far)] + peers[2:]):
+    for i, to in enumerate(peers[2:5] + peers[:2]):
         stages.append(links.copy(stats.at[i], stats_recv.at[i], to))
 
     build_strips(strip, small, buckets)
@@ -882,14 +993,6 @@
     query_sum[...] = jnp.zeros_like(query_sum)
     key_sum[...] = jnp.zeros_like(key_sum)
     value_sum[...] = jnp.zeros_like(value_sum)
-
-    def mix_back(dev):
-        at = block_rows(dev, rows)
-        grad_mixed[at, :] = contract_cols(grad_attn[at, :], w_out[...]).astype(bf16)
-
-    mix_back(me)
-    gather.near.wait_recv()
-    mix_back(core)
 
     def attend_back(dev, h):
         at = block_rows(dev, rows)
@@ -921,46 +1024,24 @@
     def take_gate(i):
         gate_loads[i].wait()
         gate.take_y(i)
-        if i == 0:
-            up.y_copies[0].start()
-            up.y_copies[1].start()
-        if i == 1:
-            up.y_copies[2].start()
-            up.y_copies[3].start()
 
     def take_up(i):
         up_loads[i].wait()
         up.take_y(i)
 
-    def down_near():
-        loads[0].wait()
-        loads[1].wait()
-        down.take_near()
-
     def down_total():
-        down_out[...] = down.total()
+        down.total(down_out)
 
     def gate_total():
         gate_out[...] = gate.total()
 
-    def up_total():
-        up_out[...] = up.total()
-
     head_keys(0)
-    if exchange:
-        take_gate(0)
-    gather.forward(0)
-    gather.forward(1)
-    mix_back(far)
-    for copy in gather.passed:
-        copy.wait_recv()
-    mix_back(diag)
     between = {
-        (0, 1): [lambda: take_gate(1), down_near],
-        (1, 1): [lambda: take_up(0)],
-        (2, 0): [down_total],
-        (2, 1): [lambda: take_up(1)],
-        (2, 3): [gate_total],
+        (0, 1): [lambda: take_gate(0)],
+        (0, 2): [lambda: down.relay(0)],
+        (1, 2): [lambda: take_gate(1), lambda: down.relay(1)],
+        (1, 3): [lambda: down.relay(2)],
+        (2, 2): [lambda: take_up(0)],
     } if exchange else {}
     for h in range(heads):
         if h:
@@ -982,29 +1063,19 @@
             + mm(grad_qkv[2, at, :], w_value[...])
         )
 
-    scatter.send_diag(0, terms(diag))
-    scatter.send_near(terms(core))
-    scatter.send_far(0, terms(far))
-    own_terms[...] = terms(me)
+    gain_parts = []
+
+    def gain_terms(dev):
+        value = terms(dev)
+        product = value * normed[block_rows(dev, rows), :].astype(f32)
+        gain_parts.append(jnp.sum(product, axis=0, keepdims=True))
+        return value
+
     save_normed.wait()
-
-    cols = mixed.shape[1]
-    for i in range(4):
-        at = pl.ds(pl.multiple_of(order[i] * part, 128), part)
-        for m in range(4):
-            if m < 3:
-                block = contract_rows(normed[:, at], grad_qkv[m]).astype(bf16)
-            else:
-                block = contract_rows(grad_attn[:, at], mixed[...]).astype(bf16)
-            if exchange:
-                low, high = block[: part // 2], block[part // 2 :]
-                lanes = slice(m * cols, (m + 1) * cols)
-                attn_send[i, :, lanes] = jnp.where(y == 0, high, low)
-                attn_own[i, :, lanes] = jnp.where(y == 0, low, high)
-            else:
-                attn_out[m, at, :] = block
-        if exchange:
-            attn.y_copies[i].start()
+    scatter.send_diag(0, gain_terms(diag))
+    scatter.send_near(gain_terms(core))
+    scatter.send_far(0, gain_terms(far))
+    own_terms[...] = gain_terms(me)
 
     index = small[2:3, :]
     lines = []
@@ -1020,59 +1091,94 @@
     table_part = lax.dot_general(
         diagonals, onehot, (((1,), (1,)), ((), ())), precision=highest, preferred_element_type=f32
     )
-    if exchange:
-        take_up(2)
-        up.take_near()
-
-    value = tokens[...].astype(f32)
-    pulled, gain_part = norm_pull(value, small[0:1, 0:width], scatter.total(own_terms[...]))
-    grad_input[...] = grad_h1[...] + pulled
     stats[0] = jnp.zeros_like(stats[0])
-    stats[0, 0:1, :] = gain_part
+    stats[0, 0:1, :] = (gain_parts[0] + gain_parts[1] + gain_parts[2] + gain_parts[3]) / small[0:1, 0:width]
     stats[0, 1:2, :] = gain_ff_part[...]
+    stats[0, 2 : 2 + heads, 0:buckets] = table_part[0:heads]
     stages[0].start()
+    dp_stages = len(stages) - 2
 
     def next_stage(i):
         stages[i].wait_recv()
         total = stats[i] + stats_recv[i]
-        to = stats.at[i + 1] if i + 1 < len(stages) else stats_out
-        to[...] = total
-        if i == 1:
-            to[2 : 2 + heads, 0:buckets] = table_part[0:heads]
+        if i >= dp_stages:
+            row = lax.broadcasted_iota(jnp.int32, total.shape, 0)
+            total = jnp.where(row < 2, total, stats[i])
         if i + 1 < len(stages):
+            stats[i + 1] = total
             stages[i + 1].start()
-
-    next_stage(0)
+        else:
+            stats_out[...] = total
+
+    cols = mixed.shape[1]
+    for i in range(4):
+        at = pl.ds(pl.multiple_of(order[i] * part, 128), part)
+        for m in range(3):
+            block = contract_rows(normed[:, at], grad_qkv[m]).astype(bf16)
+            if exchange:
+                low, high = block[: part // 2], block[part // 2 :]
+                lanes = slice(m * cols, (m + 1) * cols)
+                attn_send[i, :, lanes] = jnp.where(y == 0, high, low)
+                attn_own[i, :, lanes] = jnp.where(y == 0, low, high)
+            else:
+                attn_out[m, at, :] = block
+        if exchange:
+            attn_send[i, :, 3 * cols :] = out_grad[i, 1 - y]
+            attn_own[i, :, 3 * cols :] = out_grad[i, y]
+            attn.y_copies[i].start()
+        else:
+            for side in range(2):
+                attn_out[3, pl.ds(i * part + side * part // 2, part // 2), :] = out_grad[i, side]
+
+    if exchange:
+        take_up(1)
+        down_total()
+        gate.hand_on()
+    ff_copy.wait_recv()
+    output[...] = (ff_base[...] + ff_recv[...].astype(f32)).astype(bf16)
+    if exchange:
+        up.relay(0)
+        take_up(2)
+    pulled, _ = norm_pull(tokens[...].astype(f32), small[0:1, 0:width], scatter.total(own_terms[...]))
+    grad_input[...] = grad_h1[...] + pulled
     if exchange:
         take_up(3)
-    next_stage(1)
-    if exchange:
+        next_stage(0)
+        up.relay(1)
         attn.take_y(0)
+        gate_total()
+        up.relay(2)
+        next_stage(1)
         attn.take_y(1)
-        attn.take_near()
+        attn.relay(0)
+        next_stage(2)
         attn.take_y(2)
-        up_total()
+        up.total(up_out)
+        attn.relay(1)
+        next_stage(3)
+        next_stage(4)
+        attn.relay(2)
         attn.take_y(3)
-        next_stage(2)
-        next_stage(3)
-        total = attn.total()
+        attn.total(attn_sum)
         for m in range(3):
-            attn_out[m] = total[:, m * cols : (m + 1) * cols]
-        attn_out[3] = total[:, 3 * cols :].T
-        next_stage(4)
-        down.wait_send(with_y=False)
+            attn_out[m] = attn_sum[:, m * cols : (m + 1) * cols]
+        attn_out[3] = attn_sum[:, 3 * cols :].T
+        down.wait_send()
         gate.wait_send()
         up.wait_send()
         attn.wait_send()
-    gather.wait_send()
+    else:
+        next_stage(0)
+        next_stage(1)
+    ff_copy.wait_send()
     scatter.wait_send()
     for stage in stages:
         stage.wait_send()
 
 
 def attention_backward(
-    exchange, table_shape, grad_attn, tokens, small, grad_h1, qkv, mixed, lse, w_query, w_key, w_value, w_out,
-    gain_ff_part, first, normed, down_in, gate_in, up_in,
+    exchange, table_shape, tokens, small, grad_h1, qkv, mixed, lse, w_query, w_key, w_value, grad_mixed, out_grad,
+    gain_ff_part, ff_base, first, normed, ff_far, down_in, gate_in, up_in,
 ):
     rows, width = grad_h1.shape
     length = 4 * rows
@@ -1083,10 +1189,8 @@
     shape = jax.ShapeDtypeStruct
     scratch = [
         pltpu.VMEM((length, width), bf16),
-        pltpu.VMEM((length, width), bf16),
         pltpu.VMEM((heads, 128, 2 * length), f32),
         pltpu.VMEM((heads, 128, 2 * length), f32),
-        pltpu.VMEM((length, cols), bf16),
         pltpu.VMEM((length, cols), bf16),
         pltpu.VMEM((length, cols), bf16),
         pltpu.VMEM((length, cols), f32),
@@ -1097,22 +1201,25 @@
         pltpu.VMEM((3, rows, width), bf16),
         pltpu.VMEM((3, rows, width), bf16),
     ]
-    for count in (4, 3, 2, 2, 1, 4, 4, 3):
+    for count in (4, 5, 2, 2, 3, 4, 4, 5):
         scratch.append(pltpu.VMEM((count, part, ff) if exchange else (8, 128), bf16))
-    for count in (4, 4, 4, 3):
+    for count in (4, 4, 4, 5):
         scratch.append(pltpu.VMEM((count, part, 4 * cols) if exchange else (8, 128), bf16))
     stages = 5 if exchange else 2
     scratch += [
+        pltpu.VMEM((part, 4 * cols), f32),
+        pltpu.VMEM((rows, width), bf16),
         pltpu.VMEM((stages, 8, width), f32),
         pltpu.VMEM((stages, 8, width), f32),
-        pltpu.SemaphoreType.DMA((40,)),
-        pltpu.SemaphoreType.DMA((40,)),
-        pltpu.SemaphoreType.DMA((12,)),
+        pltpu.SemaphoreType.DMA((48,)),
+        pltpu.SemaphoreType.DMA((48,)),
+        pltpu.SemaphoreType.DMA((16,)),
     ]
     ff_out = shape((part, ff) if exchange else (8, 128), f32)
     return pl.pallas_call(
         functools.partial(back_kernel, exchange, buckets),
         out_shape=(
+            shape((rows, width), bf16),
             shape((rows, width), f32),
             shape((8, width), f32),
             shape((4, part, cols), f32) if exchange else shape((4, width, cols), bf16),
@@ -1120,15 +1227,15 @@
             ff_out,
             ff_out,
         ),
-        in_specs=[in_vmem()] * 12 + [in_smem()] + [anywhere()] * 4,
-        out_specs=[in_vmem()] * 6,
+        in_specs=[in_vmem()] * 13 + [in_smem()] + [anywhere()] * 5,
+        out_specs=[in_vmem()] * 7,
         scratch_shapes=scratch,
         compiler_params=pltpu.CompilerParams(
             collective_id=1, has_side_effects=True, vmem_limit_bytes=VMEM_BYTES
         ),
     )(
-        grad_attn, tokens, small, grad_h1, qkv, mixed, lse, w_query, w_key, w_value, w_out, gain_ff_part, first,
-        normed, down_in, gate_in, up_in,
+        tokens, small, grad_h1, qkv, mixed, lse, w_query, w_key, w_value, grad_mixed, out_grad, gain_ff_part, ff_base,
+        first, normed, ff_far, down_in, gate_in, up_in,
     )
 
 
@@ -1191,12 +1298,12 @@
     width = tokens.shape[1]
     small = pack_small(gain_attn, gain_ff, offset_bucket, bias_table)
     turned = [w_query.T, w_key.T, w_value.T]
-    qkv, mixed, lse, output, grad_h1, grad_attn, gain_ff_part, normed, down, gate, up = forward(
+    qkv, mixed, lse, ff_far, ff_base, grad_h1, grad_mixed, out_grad, gain_ff_part, normed, down, gate, up = forward(
         exchange, bias_table.shape, tokens, small, first_length, *turned, w_out, w_gate.T, w_up.T, w_down, cotangent
     )
-    grad_input, stats, attn, gate_sum, up_sum, down_sum = attention_backward(
-        exchange, bias_table.shape, grad_attn, tokens, small, grad_h1, qkv, mixed, lse, *turned, w_out, gain_ff_part,
-        first_length, normed, down, gate, up,
+    output, grad_input, stats, attn, gate_sum, up_sum, down_sum = attention_backward(
+        exchange, bias_table.shape, tokens, small, grad_h1, qkv, mixed, lse, *turned, grad_mixed, out_grad, gain_ff_part,
+        ff_base, first_length, normed, ff_far, down, gate, up,
     )
     if exchange:
         *attn, output, grad_input, gate_sum, up_sum, down_sum, gain_first, gain_second, table = finish(

time: 256 us -> 236 us (0.922)
  Pallas kernels: 247 us -> 227 us
    pallas_call x1, Pallas kernels: 113 us -> 102 us  [attention_backward(): pl.pallas_call(functools.partial(back_kernel, exchange, buckets), out_sha...]
    pallas_call x1, Pallas kernels: 128 us -> 120 us  [forward(): pl.pallas_call(functools.partial(forward_kernel, exchange, buckets), out_...]
where the time goes in v4:
time: 236 us; the launch traced here: 233 us
  Pallas kernels  227 us (96%)
    pallas_call x1, Pallas kernels, forward(): pl.pallas_call(functools.partial(forward_kernel, exchange, buckets), out_...  120 us
    pallas_call x1, Pallas kernels, attention_backward(): pl.pallas_call(functools.partial(back_kernel, exchange, buckets), out_sha...  102 us
    pallas_call x1, Pallas kernels, finish(): pl.pallas_call(functools.partial(finish_kernel, heads), out_shape=outs +...  5.71 us

profile of v4, /device:TPU:0, one launch (start us, length us, event | category | flops | bytes accessed | tf_op | source)
XLA Modules:
  0.0 232.6 jit_solution(501269973900462601)
XLA Ops:
  1.3 0.7 reshape.33
  2.0 0.7 reshape.34
  2.7 0.7 convert_element_type.3
  3.4 1.3 select_maximum_fusion.small
  4.7 120.1 %shard_map.229 = (bf16[3,1024,192]{2,1,0:T(8,128)(2,1)}, bf16[1024,192]{1,0:T(8,128)(2,1)}, f32[1024,128]{1,0:T(8,128)}, bf16[256,1536]{1,0:T(8,128)(2,1)}, f32[...) custom-call(bf16[256,1536]{1,0:T(8,128)(2,1)} %tokens.3, ...), custom_call_target="tpu_custom_call" | custom-call | tf_op jit(solution)/shard_map/pallas_call | solution.py:701
  124.9 101.6 %shard_map.230 = (bf16[256,1536]{1,0:T(8,128)(2,1)}, f32[256,1536]{1,0:T(8,128)}, f32[8,1536]{1,0:T(8,128)}, f32[4,192,192]{2,1,0:T(8,128)}, f32[192,992]{1,0:T(...) custom-call(bf16[256,1536]{1,0:T(8,128)(2,1)} %tokens.3, f32[6,2048]{1,0:T(8,128)} %select_maximum_fusion.small, ...), custom_call_target="tpu_custom_call" | custom-call | tf_op jit(solution)/shard_map/pallas_call | solution.py:1219
  226.4 5.7 %shard_map.231 = (f32[192,192]{1,0:T(8,128)}, f32[192,192]{1,0:T(8,128)}, f32[192,192]{1,0:T(8,128)}, f32[192,192]{1,0:T(8,128)}, bf16[256,1536]{1,0:T(8,128)(2,...) custom-call(f32[8,1536]{1,0:T(8,128)} %get-tuple-element.57.refs_0_,, ...), custom_call_target="tpu_custom_call" | custom-call | tf_op jit(solution)/shard_map/pallas_call | solution.py:1268

commit v5 on v4

--- a/solution.py
+++ b/solution.py
@@ -134,10 +134,9 @@
     return jnp.concatenate(parts, axis=0)
 
 
-def visible_pairs(dev, rows, length, first):
-    query = lax.broadcasted_iota(jnp.int32, (rows, length), 0) + dev * rows >= first
-    key = lax.broadcasted_iota(jnp.int32, (rows, length), 1) >= first
-    return query == key
+def visible_keys(dev, rows, length, first):
+    key = lax.broadcasted_iota(jnp.int32, (1, length), 1)
+    return (key >= first) == (dev * rows >= first)
 
 
 def head_lanes(shape, h):
@@ -221,19 +220,25 @@
     up_w,
     down_w,
     cot_in,
+    grad_mixed,
+    out_grad,
+    gain_grad,
+    qkv_out,
+    mixed_out,
+    lse_out,
+    ff_far_out,
+    own_terms_out,
+    grad_h1_out,
+    normed_out,
+    down_out,
+    gate_out,
+    up_out,
     qkv,
     mixed,
     lse,
     ff_far,
     own_terms,
     grad_h1,
-    grad_mixed,
-    out_grad,
-    gain_grad,
-    normed_out,
-    down_out,
-    gate_out,
-    up_out,
     normed,
     cot,
     wg,
@@ -362,7 +367,7 @@
 
     def attend(dev):
         at = block_rows(dev, rows)
-        seen = visible_pairs(dev, rows, length, first[0])
+        seen = visible_keys(dev, rows, length, first[0])
         mixed_sum[...] = jnp.zeros_like(mixed_sum)
         lse[at, :] = jnp.zeros((rows, 128), f32)
 
@@ -504,7 +509,6 @@
     cot_gather.forward(3)
     scatter.send_far(0, far_terms[pl.ds(0, half), :])
     second.forward(1)
-    own_terms[...] = terms(me * rows, me * rows + half)
     for i in (2, 3):
         cot_gather.passed[i].wait_recv()
     second.passed[1].wait_recv()
@@ -538,6 +542,16 @@
     def save(src, dst, at):
         return pltpu.make_async_copy(src, dst, local.at[spots + at])
 
+    results = []
+
+    def keep_result(src, dst):
+        results.append(save(src, dst, 12 + len(results)))
+        results[-1].start()
+
+    keep_result(qkv, qkv_out)
+    keep_result(mixed, mixed_out)
+    keep_result(lse, lse_out)
+
     def store_down(t, low, high):
         down_grad[t, 0] = low
         down_grad[t, 1] = high
@@ -583,13 +597,28 @@
     scatter.send_far(1, far_terms[pl.ds(half, half), :])
     for block in (1, 2):
         down_block(block)
+    own_terms[...] = terms(me * rows, me * rows + half)
     gate_block(2)
     down_block(3)
     cot_gather.wait_send()
     for peer in (core, far):
         pl.semaphore_signal(free, inc=1, device_id=group.at(peer), device_id_type=MESH)
+    residual = grad_h1[...]
+    pulled, gain_part = norm_pull(residual, gain_ff, scatter.total(own_terms[...]))
+    gain_grad[...] = gain_part
+    own_terms[...] = residual
+    grad = cot[own, :].astype(f32) + pulled
+    grad_h1[...] = grad
+    cot[own, :] = grad.astype(bf16)
+    third = Gather(links, group, cot, rows, 2)
+    pl.semaphore_wait(free, 2)
+    third.start()
+    keep_result(grad_h1, grad_h1_out)
     gate_block(1)
     gate_block(3)
+    scatter.wait_send()
+    out_again = pltpu.make_async_copy(w_out, tx.at[0, 0:depth], local.at[spots - 1])
+    out_again.start()
 
     def ff_terms(dev):
         return mm(hidden[block_rows(dev, rows), :], wd[...])
@@ -601,22 +630,11 @@
     own_part = ff_terms(far)
     ff_diag.wait_recv()
     ff_far[...] = (own_part + rx_ff[0].astype(f32)).astype(bf16)
-    residual = grad_h1[...]
-    own_part = residual + ff_terms(me)
-    pulled, gain_part = norm_pull(residual, gain_ff, scatter.total(own_terms[...]))
-    gain_grad[...] = gain_part
-    grad = cot[own, :].astype(f32) + pulled
-    grad_h1[...] = grad
-    cot[own, :] = grad.astype(bf16)
-    third = Gather(links, group, cot, rows, 2)
-    pl.semaphore_wait(free, 2)
-    third.start()
-    scatter.wait_send()
-    out_again = load(w_out, tx.at[0, 0:depth])
-    out_again.start()
+    keep_result(ff_far, ff_far_out)
+    own_part = ff_terms(me)
     ff_near.wait_recv()
-    own_terms[...] = own_part + rx_ff[1].astype(f32)
-
+    own_terms[...] += own_part + rx_ff[1].astype(f32)
+    keep_result(own_terms, own_terms_out)
     def mix_back(dev):
         at = block_rows(dev, rows)
         grad_mixed[at, :] = contract_cols(cot[at, :], tx[0, 0:depth, :]).astype(bf16)
@@ -671,6 +689,8 @@
             save(up_grad.at[t % 2], up_out.at[t], 8 + t).wait()
     for copy in (mixed_near, mixed_far, mixed_diag):
         copy.wait_send()
+    for copy in results:
+        copy.wait()
     second.wait_send()
     third.wait_send()
     ff_diag.wait_send()
@@ -698,26 +718,30 @@
     part = width // 8
     shape = jax.ShapeDtypeStruct
     halves = (4, 2, part, ff)
+    kept = [
+        shape((3, length, cols), bf16),
+        shape((length, cols), bf16),
+        shape((length, 128), f32),
+        shape((rows, width), bf16),
+        shape((rows, width), f32),
+        shape((rows, width), f32),
+    ]
     return pl.pallas_call(
         functools.partial(forward_kernel, exchange, buckets),
         out_shape=(
-            shape((3, length, cols), bf16),
-            shape((length, cols), bf16),
-            shape((length, 128), f32),
-            shape((rows, width), bf16),
-            shape((rows, width), f32),
-            shape((rows, width), f32),
             shape((length, cols), bf16),
             shape((4, 2, part, cols), bf16),
             shape((1, width), f32),
+            *kept,
             shape((length, width), bf16),
             shape((4, part, ff) if exchange else halves, bf16),
             shape((2, 2, part, ff) if exchange else halves, bf16),
             shape(halves, bf16),
         ),
         in_specs=[in_vmem()] * 2 + [in_smem()] + [anywhere()] * 8,
-        out_specs=[in_vmem()] * 9 + [anywhere()] * 4,
-        scratch_shapes=[
+        out_specs=[in_vmem()] * 3 + [anywhere()] * 10,
+        scratch_shapes=[pltpu.VMEM(v.shape, v.dtype) for v in kept]
+        + [
             pltpu.VMEM((length, width), bf16),
             pltpu.VMEM((length, width), bf16),
             pltpu.VMEM((ff, width), bf16),
@@ -741,7 +765,7 @@
             pltpu.VMEM((2, 2, part, ff) if exchange else (8, 128), bf16),
             pltpu.SemaphoreType.DMA((56,)),
             pltpu.SemaphoreType.DMA((56,)),
-            pltpu.SemaphoreType.DMA((24,)),
+            pltpu.SemaphoreType.DMA((32,)),
             pltpu.SemaphoreType.REGULAR,
         ],
         compiler_params=pltpu.CompilerParams(
@@ -880,32 +904,40 @@
 def back_kernel(
     exchange,
     buckets,
-    tokens,
     small,
-    grad_h1,
     qkv,
-    mixed,
     lse,
-    w_query,
-    w_key,
-    w_value,
     grad_mixed,
     out_grad,
     gain_ff_part,
-    ff_base,
     first,
+    tokens_in,
+    grad_h1_in,
+    w_query_in,
+    w_key_in,
+    w_value_in,
+    ff_base_in,
     normed_in,
     ff_far,
     down_in,
     gate_in,
     up_in,
+    stats_out,
+    attn_out,
     output,
     grad_input,
-    stats_out,
-    attn_out,
     gate_out,
     up_out,
     down_out,
+    tokens,
+    grad_h1,
+    ff_base,
+    w_query,
+    w_key,
+    w_value,
+    gate_sum,
+    up_sum,
+    down_sum,
     normed,
     strip,
     strip_grad,
@@ -957,7 +989,17 @@
         return copy
 
     save_normed = load(normed_in, normed)
-    save_normed.start()
+    late = [
+        load(src, dst)
+        for src, dst in (
+            (tokens_in, tokens),
+            (grad_h1_in, grad_h1),
+            (ff_base_in, ff_base),
+            (w_query_in, w_query),
+            (w_key_in, w_key),
+            (w_value_in, w_value),
+        )
+    ]
     if exchange:
         z, y = dp // 2, lax.rem(dp, 2)
         order = line_order(z)
@@ -969,7 +1011,7 @@
         loads = [load(down_in.at[i], down_own.at[i]) for i in range(4)]
         gate_loads = [load(gate_in.at[i, y], gate_own.at[i]) for i in range(2)]
         up_loads = [load(up_in.at[i, y], up_own.at[i]) for i in range(4)]
-        for copy in loads + gate_loads + up_loads:
+        for copy in loads:
             copy.start()
     else:
         order = [0, 1, 2, 3]
@@ -981,6 +1023,10 @@
             loads[i].wait()
             if i < 3:
                 down.begin(i)
+        for copy in gate_loads + up_loads:
+            copy.start()
+    for copy in [save_normed] + late:
+        copy.start()
     scatter = Scatter(links, group, tx, rx, rows, 1)
     ff_copy = links.copy(ff_far, ff_recv, group.at(far))
     ff_copy.start()
@@ -996,7 +1042,7 @@
 
     def attend_back(dev, h):
         at = block_rows(dev, rows)
-        seen = visible_pairs(dev, rows, length, first[0])
+        seen = visible_keys(dev, rows, length, first[0])
         query, grad = qkv[0, at, :], grad_mixed[at, :]
         lanes = head_lanes(query.shape, h)
         zero = jnp.zeros_like(query)
@@ -1030,10 +1076,12 @@
         up.take_y(i)
 
     def down_total():
-        down.total(down_out)
+        down.total(down_sum)
+        save(down_sum, down_out)
 
     def gate_total():
-        gate_out[...] = gate.total()
+        gate_sum[...] = gate.total()
+        save(gate_sum, gate_out)
 
     head_keys(0)
     between = {
@@ -1071,7 +1119,14 @@
         gain_parts.append(jnp.sum(product, axis=0, keepdims=True))
         return value
 
-    save_normed.wait()
+    for copy in [save_normed] + late:
+        copy.wait()
+    saves = []
+
+    def save(src, dst):
+        saves.append(load(src, dst))
+        saves[-1].start()
+
     scatter.send_diag(0, gain_terms(diag))
     scatter.send_near(gain_terms(core))
     scatter.send_far(0, gain_terms(far))
@@ -1110,7 +1165,7 @@
         else:
             stats_out[...] = total
 
-    cols = mixed.shape[1]
+    cols = w_query.shape[0]
     for i in range(4):
         at = pl.ds(pl.multiple_of(order[i] * part, 128), part)
         for m in range(3):
@@ -1135,25 +1190,31 @@
         down_total()
         gate.hand_on()
     ff_copy.wait_recv()
-    output[...] = (ff_base[...] + ff_recv[...].astype(f32)).astype(bf16)
+    ff_recv[...] = (ff_base[...] + ff_recv[...].astype(f32)).astype(bf16)
+    save(ff_recv, output)
+
+    def input_total():
+        pulled, _ = norm_pull(tokens[...].astype(f32), small[0:1, 0:width], scatter.total(own_terms[...]))
+        grad_h1[...] += pulled
+        save(grad_h1, grad_input)
+
     if exchange:
         up.relay(0)
         take_up(2)
-    pulled, _ = norm_pull(tokens[...].astype(f32), small[0:1, 0:width], scatter.total(own_terms[...]))
-    grad_input[...] = grad_h1[...] + pulled
-    if exchange:
         take_up(3)
         next_stage(0)
         up.relay(1)
         attn.take_y(0)
         gate_total()
+        input_total()
         up.relay(2)
         next_stage(1)
         attn.take_y(1)
         attn.relay(0)
         next_stage(2)
         attn.take_y(2)
-        up.total(up_out)
+        up.total(up_sum)
+        save(up_sum, up_out)
         attn.relay(1)
         next_stage(3)
         next_stage(4)
@@ -1168,8 +1229,11 @@
         up.wait_send()
         attn.wait_send()
     else:
+        input_total()
         next_stage(0)
         next_stage(1)
+    for copy in saves:
+        copy.wait()
     ff_copy.wait_send()
     scatter.wait_send()
     for stage in stages:
@@ -1177,7 +1241,7 @@
 
 
 def attention_backward(
-    exchange, table_shape, tokens, small, grad_h1, qkv, mixed, lse, w_query, w_key, w_value, grad_mixed, out_grad,
+    exchange, table_shape, tokens, small, grad_h1, qkv, lse, w_query, w_key, w_value, grad_mixed, out_grad,
     gain_ff_part, ff_base, first, normed, ff_far, down_in, gate_in, up_in,
 ):
     rows, width = grad_h1.shape
@@ -1187,7 +1251,17 @@
     buckets, heads = table_shape
     part = width // 8
     shape = jax.ShapeDtypeStruct
+    ff_scratch = pltpu.VMEM((part, ff) if exchange else (8, 128), f32)
     scratch = [
+        pltpu.VMEM((rows, width), bf16),
+        pltpu.VMEM((rows, width), f32),
+        pltpu.VMEM((rows, width), f32),
+        pltpu.VMEM((cols, width), bf16),
+        pltpu.VMEM((cols, width), bf16),
+        pltpu.VMEM((cols, width), bf16),
+        ff_scratch,
+        ff_scratch,
+        ff_scratch,
         pltpu.VMEM((length, width), bf16),
         pltpu.VMEM((heads, 128, 2 * length), f32),
         pltpu.VMEM((heads, 128, 2 * length), f32),
@@ -1213,29 +1287,29 @@
         pltpu.VMEM((stages, 8, width), f32),
         pltpu.SemaphoreType.DMA((48,)),
         pltpu.SemaphoreType.DMA((48,)),
-        pltpu.SemaphoreType.DMA((16,)),
+        pltpu.SemaphoreType.DMA((24,)),
     ]
     ff_out = shape((part, ff) if exchange else (8, 128), f32)
     return pl.pallas_call(
         functools.partial(back_kernel, exchange, buckets),
         out_shape=(
+            shape((8, width), f32),
+            shape((4, part, cols), f32) if exchange else shape((4, width, cols), bf16),
             shape((rows, width), bf16),
             shape((rows, width), f32),
-            shape((8, width), f32),
-            shape((4, part, cols), f32) if exchange else shape((4, width, cols), bf16),
             ff_out,
             ff_out,
             ff_out,
         ),
-        in_specs=[in_vmem()] * 13 + [in_smem()] + [anywhere()] * 5,
-        out_specs=[in_vmem()] * 7,
+        in_specs=[in_vmem()] * 6 + [in_smem()] + [anywhere()] * 11,
+        out_specs=[in_vmem()] * 2 + [anywhere()] * 5,
         scratch_shapes=scratch,
         compiler_params=pltpu.CompilerParams(
             collective_id=1, has_side_effects=True, vmem_limit_bytes=VMEM_BYTES
         ),
     )(
-        tokens, small, grad_h1, qkv, mixed, lse, w_query, w_key, w_value, grad_mixed, out_grad, gain_ff_part, ff_base,
-        first, normed, ff_far, down_in, gate_in, up_in,
+        small, qkv, lse, grad_mixed, out_grad, gain_ff_part, first, tokens, grad_h1, w_query, w_key, w_value,
+        ff_base, normed, ff_far, down_in, gate_in, up_in,
     )
 
 
@@ -1298,11 +1372,11 @@
     width = tokens.shape[1]
     small = pack_small(gain_attn, gain_ff, offset_bucket, bias_table)
     turned = [w_query.T, w_key.T, w_value.T]
-    qkv, mixed, lse, ff_far, ff_base, grad_h1, grad_mixed, out_grad, gain_ff_part, normed, down, gate, up = forward(
+    grad_mixed, out_grad, gain_ff_part, qkv, mixed, lse, ff_far, ff_base, grad_h1, normed, down, gate, up = forward(
         exchange, bias_table.shape, tokens, small, first_length, *turned, w_out, w_gate.T, w_up.T, w_down, cotangent
     )
-    output, grad_input, stats, attn, gate_sum, up_sum, down_sum = attention_backward(
-        exchange, bias_table.shape, tokens, small, grad_h1, qkv, mixed, lse, *turned, grad_mixed, out_grad, gain_ff_part,
+    stats, attn, output, grad_input, gate_sum, up_sum, down_sum = attention_backward(
+        exchange, bias_table.shape, tokens, small, grad_h1, qkv, lse, *turned, grad_mixed, out_grad, gain_ff_part,
         ff_base, first_length, normed, ff_far, down, gate, up,
     )
     if exchange:

time: 236 us -> 229 us (0.970)
  Pallas kernels: 227 us -> 220 us
    pallas_call x1, Pallas kernels: 102 us -> 97.8 us  [attention_backward(): pl.pallas_call(functools.partial(back_kernel, exchange, buckets), out_sha...]
    pallas_call x1, Pallas kernels: 120 us -> 117 us  [forward(): pl.pallas_call(functools.partial(forward_kernel, exchange, buckets), out_...]
where the time goes in v5:
time: 229 us; the launch traced here: 226 us
  Pallas kernels  220 us (96%)
    pallas_call x1, Pallas kernels, forward(): pl.pallas_call(functools.partial(forward_kernel, exchange, buckets), out_...  117 us
    pallas_call x1, Pallas kernels, attention_backward(): pl.pallas_call(functools.partial(back_kernel, exchange, buckets), out_sha...  97.8 us
    pallas_call x1, Pallas kernels, finish(): pl.pallas_call(functools.partial(finish_kernel, heads), out_shape=outs +...  5.71 us

profile of v5, /device:TPU:0, one launch (start us, length us, event | category | flops | bytes accessed | tf_op | source)
XLA Modules:
  0.0 225.6 jit_solution(16471688907725430118)
XLA Ops:
  1.3 0.7 reshape.33
  2.0 0.7 reshape.34
  2.7 0.7 convert_element_type.3
  3.4 1.3 select_maximum_fusion.small
  4.7 116.9 %shard_map.229 = (bf16[1024,192]{1,0:T(8,128)(2,1)}, bf16[4,2,192,192]{3,2,1,0:T(8,128)(2,1)}, f32[1,1536]{1,0:T(1,128)}, bf16[3,1024,192]{2,1,0:T(8,128)(2,1)},...) custom-call(bf16[256,1536]{1,0:T(8,128)(2,1)} %tokens_in.1, ...), custom_call_target="tpu_custom_call" | custom-call | tf_op jit(solution)/shard_map/pallas_call | solution.py:729
  121.6 97.8 %shard_map.230 = (f32[8,1536]{1,0:T(8,128)}, f32[4,192,192]{2,1,0:T(8,128)}, bf16[256,1536]{1,0:T(8,128)(2,1)}, f32[256,1536]{1,0:T(8,128)}, f32[192,992]{1,0:T(...) custom-call(f32[6,2048]{1,0:T(8,128)} %select_maximum_fusion.small, bf16[3,1024,192]{2,1,0:T(8,128)(2,1)} %get-tuple-element.43.qkv, ...), custom_call_target="tpu_custom_call" | custom-call | tf_op jit(solution)/shard_map/pallas_call | solution.py:1293
  219.4 5.7 %shard_map.231 = (f32[192,192]{1,0:T(8,128)}, f32[192,192]{1,0:T(8,128)}, f32[192,192]{1,0:T(8,128)}, f32[192,192]{1,0:T(8,128)}, bf16[256,1536]{1,0:T(8,128)(2,...) custom-call(f32[8,1536]{1,0:T(8,128)} %get-tuple-element.55.refs_0_,, ...), custom_call_target="tpu_custom_call" | custom-call | tf_op jit(solution)/shard_map/pallas_call | solution.py:1342

commit v6 on v5

--- a/solution.py
+++ b/solution.py
@@ -100,14 +100,14 @@
             copy.wait_send()
 
 
-def pack_small(gain_attn, gain_ff, offset_bucket, table):
-    width = offset_bucket.shape[0] + 1
-
-    def row(values, fill=0.0):
-        values = values.astype(f32).reshape(-1, values.shape[-1])
-        return jnp.pad(values, ((0, 0), (0, width - values.shape[1])), constant_values=fill)
-
-    return jnp.concatenate([row(gain_attn), row(gain_ff), row(offset_bucket, -1.0), row(table.T)])
+def pack_small(small, gain_attn, gain_ff, offset_bucket, table):
+    width, offsets = gain_attn.shape[0], offset_bucket.shape[0]
+    heads, buckets = table.shape
+    small[...] = jnp.full(small.shape, -1.0, f32)
+    small[0:1, 0:width] = gain_attn[...].reshape(1, width)
+    small[1:2, 0:width] = gain_ff[...].reshape(1, width)
+    small[2:3, 0:offsets] = offset_bucket[...].astype(f32).reshape(1, offsets)
+    small[3 : 3 + heads, 0:buckets] = table[...]
 
 
 def build_strips(strip, small, buckets):
@@ -210,7 +210,10 @@
     exchange,
     buckets,
     tokens,
-    small,
+    gain_attn_in,
+    gain_ff_in,
+    offset_bucket,
+    table,
     first,
     w_query,
     w_key,
@@ -223,6 +226,7 @@
     grad_mixed,
     out_grad,
     gain_grad,
+    small,
     qkv_out,
     mixed_out,
     lse_out,
@@ -274,6 +278,7 @@
     depth = w_out.shape[0]
     ff = wg.shape[0]
     part = width // 4
+    pack_small(small, gain_attn_in, gain_ff_in, offset_bucket, table)
     gain_attn, gain_ff = small[0:1, 0:width], small[1:2, 0:width]
     links = Links(send, recv)
     peers = [group.at(core), group.at(far), group.at(diag)]
@@ -645,17 +650,26 @@
     third.near.wait_recv()
     mix_back(core)
     third.forward(0)
+
+    def sum_down(t):
+        y_copy(t).wait_recv()
+        down_grad[t, y] = (
+            down_grad[t, y].astype(f32) + y_recv[t].astype(f32)
+        ).astype(bf16)
+        save(down_grad.at[t, y], down_out.at[t], t).start()
+
+    def sum_gate(i):
+        for side in range(2):
+            z_copy(i, side).wait_recv()
+            kept = gate_grad.at[2 * i + 1, side]
+            kept[...] = (kept[...].astype(f32) + z_recv[i, side].astype(f32)).astype(bf16)
+            save(kept, gate_out.at[i, side], 4 + 2 * i + side).start()
+
     if exchange:
-
-        def sum_down(t, carry):
-            y_copy(t).wait_recv()
-            down_grad[t, y] = (
-                down_grad[t, y].astype(f32) + y_recv[t].astype(f32)
-            ).astype(bf16)
-            save(down_grad.at[t, y], down_out.at[t], t).start()
-            return carry
-
-        lax.fori_loop(0, 3, sum_down, 0)
+        sum_down(0)
+        sum_down(1)
+        sum_gate(0)
+        sum_down(2)
     third.forward(1)
     mix_back(far)
     for copy in third.passed:
@@ -668,13 +682,8 @@
 
     weight_blocks(line, cot, mixed, store_out)
     if exchange:
-        sum_down(3, 0)
-        for i in range(2):
-            for side in range(2):
-                z_copy(i, side).wait_recv()
-                kept = gate_grad.at[2 * i + 1, side]
-                kept[...] = (kept[...].astype(f32) + z_recv[i, side].astype(f32)).astype(bf16)
-                save(kept, gate_out.at[i, side], 4 + 2 * i + side).start()
+        sum_down(3)
+        sum_gate(1)
 
     for t in range(4):
         if exchange:
@@ -709,12 +718,12 @@
     return pl.BlockSpec(memory_space=pltpu.SMEM)
 
 
-def forward(exchange, table_shape, tokens, small, first, w_query, w_key, w_value, w_out, gate_w, up_w, down_w, cot):
+def forward(exchange, tokens, gain_attn, gain_ff, offset_bucket, table, first, w_query, w_key, w_value, w_out, gate_w, up_w, down_w, cot):
     rows, width = tokens.shape
     length = 4 * rows
     cols = w_query.shape[0]
     ff = gate_w.shape[0]
-    buckets, heads = table_shape
+    heads, buckets = table.shape
     part = width // 8
     shape = jax.ShapeDtypeStruct
     halves = (4, 2, part, ff)
@@ -732,14 +741,15 @@
             shape((length, cols), bf16),
             shape((4, 2, part, cols), bf16),
             shape((1, width), f32),
+            shape((8, 2 * length), f32),
             *kept,
             shape((length, width), bf16),
             shape((4, part, ff) if exchange else halves, bf16),
             shape((2, 2, part, ff) if exchange else halves, bf16),
             shape(halves, bf16),
         ),
-        in_specs=[in_vmem()] * 2 + [in_smem()] + [anywhere()] * 8,
-        out_specs=[in_vmem()] * 3 + [anywhere()] * 10,
+        in_specs=[in_vmem()] * 5 + [in_smem()] + [anywhere()] * 8,
+        out_specs=[in_vmem()] * 4 + [anywhere()] * 10,
         scratch_shapes=[pltpu.VMEM(v.shape, v.dtype) for v in kept]
         + [
             pltpu.VMEM((length, width), bf16),
@@ -771,7 +781,7 @@
         compiler_params=pltpu.CompilerParams(
             collective_id=0, has_side_effects=True, vmem_limit_bytes=VMEM_BYTES
         ),
-    )(tokens, small, first, w_query, w_key, w_value, w_out, gate_w, up_w, down_w, cot)
+    )(tokens, gain_attn, gain_ff, offset_bucket, table, first, w_query, w_key, w_value, w_out, gate_w, up_w, down_w, cot)
 
 
 class Line:
@@ -1211,15 +1221,15 @@
         next_stage(1)
         attn.take_y(1)
         attn.relay(0)
-        next_stage(2)
-        attn.take_y(2)
         up.total(up_sum)
         save(up_sum, up_out)
+        attn.take_y(2)
         attn.relay(1)
+        attn.relay(2)
+        next_stage(2)
+        attn.take_y(3)
         next_stage(3)
         next_stage(4)
-        attn.relay(2)
-        attn.take_y(3)
         attn.total(attn_sum)
         for m in range(3):
             attn_out[m] = attn_sum[:, m * cols : (m + 1) * cols]
@@ -1370,10 +1380,9 @@
     exchange = n_dp == 8
     buckets, heads = bias_table.shape
     width = tokens.shape[1]
-    small = pack_small(gain_attn, gain_ff, offset_bucket, bias_table)
     turned = [w_query.T, w_key.T, w_value.T]
-    grad_mixed, out_grad, gain_ff_part, qkv, mixed, lse, ff_far, ff_base, grad_h1, normed, down, gate, up = forward(
-        exchange, bias_table.shape, tokens, small, first_length, *turned, w_out, w_gate.T, w_up.T, w_down, cotangent
+    grad_mixed, out_grad, gain_ff_part, small, qkv, mixed, lse, ff_far, ff_base, grad_h1, normed, down, gate, up = forward(
+        exchange, tokens, gain_attn, gain_ff, offset_bucket, bias_table.T, first_length, *turned, w_out, w_gate.T, w_up.T, w_down, cotangent
     )
     stats, attn, output, grad_input, gate_sum, up_sum, down_sum = attention_backward(
         exchange, bias_table.shape, tokens, small, grad_h1, qkv, lse, *turned, grad_mixed, out_grad, gain_ff_part,

time: 229 us -> 225 us (0.983)
  no operation moved by 1% of the time
where the time goes in v6:
time: 225 us; the launch traced here: 222 us
  Pallas kernels  220 us (98%)
    pallas_call x1, Pallas kernels, forward(): pl.pallas_call(functools.partial(forward_kernel, exchange, buckets), out_...  117 us
    pallas_call x1, Pallas kernels, attention_backward(): pl.pallas_call(functools.partial(back_kernel, exchange, buckets), out_sha...  97.7 us
    pallas_call x1, Pallas kernels, finish(): pl.pallas_call(functools.partial(finish_kernel, heads), out_shape=outs +...  5.71 us

profile of v6, /device:TPU:0, one launch (start us, length us, event | category | flops | bytes accessed | tf_op | source)
XLA Modules:
  0.0 221.9 jit_solution(15355793240765605845)
XLA Ops:
  1.3 116.8 %shard_map.229 = (bf16[1024,192]{1,0:T(8,128)(2,1)}, bf16[4,2,192,192]{3,2,1,0:T(8,128)(2,1)}, f32[1,1536]{1,0:T(1,128)}, f32[8,2048]{1,0:T(8,128)}, bf16[3,1024...) custom-call(bf16[256,1536]{1,0:T(8,128)(2,1)} %tokens_in.1, ...), custom_call_target="tpu_custom_call" | custom-call | tf_op jit(solution)/shard_map/pallas_call | solution.py:738
  118.1 97.7 %shard_map.230 = (f32[8,1536]{1,0:T(8,128)}, f32[4,192,192]{2,1,0:T(8,128)}, bf16[256,1536]{1,0:T(8,128)(2,1)}, f32[256,1536]{1,0:T(8,128)}, f32[192,992]{1,0:T(...) custom-call(f32[8,2048]{1,0:T(8,128)} %get-tuple-element.44.small, bf16[3,1024,192]{2,1,0:T(8,128)(2,1)} %get-tuple-element.45.qkv, ...), custom_call_target="tpu_custom_call" | custom-call | tf_op jit(solution)/shard_map/pallas_call | solution.py:1303
  215.8 5.7 %shard_map.231 = (f32[192,192]{1,0:T(8,128)}, f32[192,192]{1,0:T(8,128)}, f32[192,192]{1,0:T(8,128)}, f32[192,192]{1,0:T(8,128)}, bf16[256,1536]{1,0:T(8,128)(2,...) custom-call(f32[8,1536]{1,0:T(8,128)} %get-tuple-element.57.refs_0_,, ...), custom_call_target="tpu_custom_call" | custom-call | tf_op jit(solution)/shard_map/pallas_call | solution.py:1352

commit v7 on v6

--- a/solution.py
+++ b/solution.py
@@ -65,7 +65,10 @@
     barrier = pltpu.get_barrier_semaphore()
     for peer in peers:
         pl.semaphore_signal(barrier, inc=1, device_id=peer, device_id_type=MESH)
-    pl.semaphore_wait(barrier, len(peers))
+
+
+def meet(peers):
+    pl.semaphore_wait(pltpu.get_barrier_semaphore(), len(peers))
 
 
 def block_rows(dev, rows, start=0, size=None):
@@ -278,8 +281,6 @@
     depth = w_out.shape[0]
     ff = wg.shape[0]
     part = width // 4
-    pack_small(small, gain_attn_in, gain_ff_in, offset_bucket, table)
-    gain_attn, gain_ff = small[0:1, 0:width], small[1:2, 0:width]
     links = Links(send, recv)
     peers = [group.at(core), group.at(far), group.at(diag)]
     z_peers = []
@@ -292,6 +293,7 @@
         peers += [y_peer] + z_peers
     else:
         line, order, y = [0, 1, 2, 3], [0, 1, 2, 3], 0
+    greet(peers)
 
     def place(order, t):
         found = jnp.int32(order[3])
@@ -319,10 +321,11 @@
     cot_own.start()
     down_load = load(down_w, wd)
     down_load.start()
-    greet(peers)
-
+    pack_small(small, gain_attn_in, gain_ff_in, offset_bucket, table)
+    gain_attn, gain_ff = small[0:1, 0:width], small[1:2, 0:width]
     x = tokens[...].astype(f32)
     normed[own, :] = (rms(x) * gain_attn).astype(bf16)
+    meet(peers)
     gather = Gather(links, group, normed, rows, 2)
     gather.start()
     out_own.wait()
@@ -1026,6 +1029,7 @@
     else:
         order = [0, 1, 2, 3]
     greet(peers)
+    meet(peers)
     if exchange:
         for copy in gate.y_copies + up.y_copies:
             copy.start()

time: 225 us -> 225 us (level)
  no operation moved by 1% of the time
where the time goes in v7:
time: 225 us; the launch traced here: 222 us
  Pallas kernels  220 us (98%)
    pallas_call x1, Pallas kernels, forward(): pl.pallas_call(functools.partial(forward_kernel, exchange, buckets), out_...  116 us
    pallas_call x1, Pallas kernels, attention_backward(): pl.pallas_call(functools.partial(back_kernel, exchange, buckets), out_sha...  97.7 us
    pallas_call x1, Pallas kernels, finish(): pl.pallas_call(functools.partial(finish_kernel, heads), out_shape=outs +...  5.71 us

profile of v7, /device:TPU:0, one launch (start us, length us, event | category | flops | bytes accessed | tf_op | source)
XLA Modules:
  0.0 221.6 jit_solution(4415030290536034938)
XLA Ops:
  1.3 116.4 %shard_map.229 = (bf16[1024,192]{1,0:T(8,128)(2,1)}, bf16[4,2,192,192]{3,2,1,0:T(8,128)(2,1)}, f32[1,1536]{1,0:T(1,128)}, f32[8,2048]{1,0:T(8,128)}, bf16[3,1024...) custom-call(bf16[256,1536]{1,0:T(8,128)(2,1)} %tokens_in.1, ...), custom_call_target="tpu_custom_call" | custom-call | tf_op jit(solution)/shard_map/pallas_call | solution.py:741
  117.7 97.7 %shard_map.230 = (f32[8,1536]{1,0:T(8,128)}, f32[4,192,192]{2,1,0:T(8,128)}, bf16[256,1536]{1,0:T(8,128)(2,1)}, f32[256,1536]{1,0:T(8,128)}, f32[192,992]{1,0:T(...) custom-call(f32[8,2048]{1,0:T(8,128)} %get-tuple-element.44.small, bf16[3,1024,192]{2,1,0:T(8,128)(2,1)} %get-tuple-element.45.qkv, ...), custom_call_target="tpu_custom_call" | custom-call | tf_op jit(solution)/shard_map/pallas_call | solution.py:1307
  215.4 5.7 %shard_map.231 = (f32[192,192]{1,0:T(8,128)}, f32[192,192]{1,0:T(8,128)}, f32[192,192]{1,0:T(8,128)}, f32[192,192]{1,0:T(8,128)}, bf16[256,1536]{1,0:T(8,128)(2,...) custom-call(f32[8,1536]{1,0:T(8,128)} %get-tuple-element.57.refs_0_,, ...), custom_call_target="tpu_custom_call" | custom-call | tf_op jit(solution)/shard_map/pallas_call | solution.py:1356
